TPU v7x, 256 devices: a whole 4x4x8 slice. The times are simulated.
256 devices in a mesh: pipe: 8 (over y, x_lo), expert: 16 (over x_hi, z), dp: 2 (over core).
Axes of the slice: x: 4 (x_hi: 2, x_lo: 2; x = x_hi * 2 + x_lo), y: 4, z: 8, core: 2. Of those that a mesh axis runs over, the one named last changes fastest.
Arguments:
- inputs: bfloat16 [8, 2, 4096, 2048], P('pipe', None, ('expert', 'dp')), may hold values from -6 to 6
- upstream: bfloat16 [8, 2, 4096, 2048], P('pipe', None, ('expert', 'dp')), may hold values from -6 to 6
- routes: int32 [8, 2, 4096, 8], P('pipe', None, ('expert', 'dp')), may hold values from 0 to 127, all different within a row; in each aligned block of 128 rows (0 to 127, 128 to 255, ..., all dimensions but the last counted through in order) at most 24 rows name the same one
- gate_weights: bfloat16 [8, 2, 4096, 8], P('pipe', None, ('expert', 'dp')), may hold values from 0.5 to 2
- proj_in: bfloat16 [8, 16, 2048, 768], P('pipe', 'expert'), may hold values from -0.125 to 0.125
- proj_out: bfloat16 [8, 16, 768, 2048], P('pipe', 'expert'), may hold values from -0.21875 to 0.21875
Outputs:
- prev_grad: bfloat16 [8, 2, 4096, 2048], P('pipe', None, ('expert', 'dp'))
- proj_out_grad: bfloat16 [8, 16, 768, 2048], P('pipe', 'expert')
Inputs may be any that keep to these rules, and one draw needn't show every extreme that they name: `routes`: in each aligned block of 128 rows (one device's tokens of one section and micro-batch) no expert is named by more than 24 rows; the experts of one row differ.
All inputs are finite; a program needn't handle non-finite values.
Results may differ from a plain program's by a relative error of at most 0.0062.
Values may be sent and summed in bfloat16 or wider, within the bound.
No kernel may reach another device: no remote copies, remote signals or barrier semaphores. Data moves between devices by JAX's collectives and lax.ppermute only.
A program may use at most 128 MiB of HBM per device.

v0:
```python
import jax
import jax.numpy as jnp
from jax import lax
from jax.sharding import PartitionSpec as P

EXPERTS = 128
CAP = 24


def from_behind(value, axis, steps):
    count = lax.axis_size(axis)
    pairs = [(source, (source + steps) % count) for source in range(count)]
    return lax.ppermute(value, axis, pairs)


def expert_rows(rows_in, rows_grad, rows_gate, weight_in, weight_out):
    scaled = (rows_gate.astype(jnp.float32)[:, None] * rows_grad.astype(jnp.float32)).astype(
        jnp.bfloat16
    )
    pre_act = jnp.dot(rows_in, weight_in, preferred_element_type=jnp.float32)
    sigmoid = jax.nn.sigmoid(pre_act)
    hidden = (pre_act * sigmoid).astype(jnp.bfloat16)
    hidden_grad = jnp.dot(scaled, weight_out.T, preferred_element_type=jnp.float32)
    pre_grad = (hidden_grad * sigmoid * (1.0 + pre_act * (1.0 - sigmoid))).astype(jnp.bfloat16)
    returned = jnp.dot(pre_grad, weight_in.T, preferred_element_type=jnp.float32).astype(
        jnp.bfloat16
    )
    partial_value = jnp.dot(hidden.T, scaled, preferred_element_type=jnp.float32)
    return (returned, partial_value)


def build_slots(route_ids, gate_rows, groups, local_count):
    targets = jnp.arange(groups, dtype=jnp.int32) * local_count
    matches = route_ids[:, :, None] == targets
    routed = jnp.any(matches, axis=1)
    weight = jnp.sum(jnp.where(matches, gate_rows.astype(jnp.float32)[:, :, None], 0.0), axis=1)
    slot_rank = jnp.cumsum(routed.astype(jnp.int32), axis=0) - 1
    slot_ids = jnp.arange(CAP, dtype=jnp.int32)
    placing = (routed.T[:, None, :] & (slot_rank.T[:, None, :] == slot_ids[None, :, None])).astype(
        jnp.bfloat16
    )
    return (placing, weight.astype(jnp.bfloat16))


def gather_rows(placing, weight, rows_in, rows_grad):
    send_in = jnp.einsum(
        "nct,td->ncd", placing, rows_in, preferred_element_type=jnp.float32
    ).astype(jnp.bfloat16)
    send_grad = jnp.einsum(
        "nct,td->ncd", placing, rows_grad, preferred_element_type=jnp.float32
    ).astype(jnp.bfloat16)
    send_gate = jnp.einsum(
        "nct,tn->nc", placing, weight, preferred_element_type=jnp.float32
    ).astype(jnp.bfloat16)
    return (send_in, send_grad, send_gate)


def shards(inputs, upstream, routes, gate_weights, proj_in, proj_out):
    groups = lax.axis_size("expert")
    local_count = EXPERTS // groups
    micro_count = inputs.shape[1]
    width = inputs.shape[3]
    weight_in = proj_in[0, 0]
    weight_out = proj_out[0, 0]
    tables = [
        build_slots(routes[0, micro_idx], gate_weights[0, micro_idx], groups, local_count)
        for micro_idx in range(micro_count)
    ]
    sends = [
        gather_rows(
            tables[micro_idx][0], tables[micro_idx][1], inputs[0, micro_idx], upstream[0, micro_idx]
        )
        for micro_idx in range(micro_count)
    ]
    partial_value = jnp.zeros((weight_in.shape[1], width), jnp.float32)
    outputs = []
    for micro_idx in range(micro_count):
        received = (
            lax.all_to_all(sends[micro_idx][0], "expert", split_axis=0, concat_axis=0, tiled=True),
            lax.all_to_all(sends[micro_idx][1], "expert", split_axis=0, concat_axis=0, tiled=True),
            lax.all_to_all(sends[micro_idx][2], "expert", split_axis=0, concat_axis=0, tiled=True),
        )
        returned, term = expert_rows(
            received[0].reshape(-1, width),
            received[1].reshape(-1, width),
            received[2].reshape(-1),
            weight_in,
            weight_out,
        )
        partial_value = partial_value + term
        arrived = lax.all_to_all(
            returned.reshape(groups, -1, width), "expert", split_axis=0, concat_axis=0, tiled=True
        )
        combined = jnp.einsum(
            "nct,ncd->td", tables[micro_idx][0], arrived, preferred_element_type=jnp.float32
        ).astype(jnp.bfloat16)
        outputs.append(from_behind(combined, "pipe", -1))
    prev_grad = jnp.stack(outputs)[None]
    proj_grad = lax.psum(partial_value, "dp").astype(jnp.bfloat16)[None, None]
    return (prev_grad, proj_grad)


def solution(mesh):
    placed = (
        P("pipe", None, ("expert", "dp"), None),
        P("pipe", None, ("expert", "dp"), None),
        P("pipe", None, ("expert", "dp"), None),
        P("pipe", None, ("expert", "dp"), None),
        P("pipe", "expert", None, None),
        P("pipe", "expert", None, None),
    )
    return jax.shard_map(
        shards,
        mesh=mesh,
        in_specs=placed,
        out_specs=(P("pipe", None, ("expert", "dp"), None), P("pipe", "expert", None, None)),
        check_vma=False,
    )
```

profile of v0, /device:TPU:1, one launch (start us, length us, event | category | flops | bytes accessed | tf_op | source)
XLA Modules:
  0.0 323.4 jit_solution(4648551050357955410)
XLA Ops:
  0.6 0.0 copy-start
  0.7 0.9 slice_bitcast_fusion
  1.5 0.1 compare_reduce_fusion.1
  1.6 0.7 bitcast_convert_fusion
  2.3 0.1 copy.37
  2.4 0.2 reduce_window_sum.18
  2.6 0.1 copy.38
  2.7 0.1 fusion.85
  2.8 0.2 fusion.67
  2.9 0.6 copy.39
  3.6 11.6 %all-to-all-start.4 = ((bf16[16,1,24]{2,1,0:T(2,128)(2,1)}), bf16[16,1,24]{2,1,0:T(2,128)(2,1)S(1)}, u32[]{:S(2)}, u32[]{:S(2)}) async-start(bf16[16,1,24]{2,1,0:T(2,128)(2,1)} %copy.39), calls=%async_computation.4 | async-start | bytes 16384 | tf_op jit(solution)/shard_map/all_to_all | solution.py:81
  15.1 0.1 copy.34
  15.2 0.2 reduce_window_sum.17
  15.4 0.1 copy.35
  15.5 0.2 fusion.61
  15.7 0.6 copy.36
  16.3 7.6 %all-to-all-done.4 = bf16[16,1,24]{2,1,0:T(2,128)(2,1)S(1)} async-done(((bf16[16,1,24]{2,1,0:T(2,128)(2,1)}), bf16[16,1,24]{2,1,0:T(2,128)(2,1)S(1)}, u32[]{:S(2)}, u32[]{:S(2)}) %all-to-all-start.4) | async-done | bytes 800 | tf_op jit(solution)/shard_map/all_to_all | solution.py:81
  23.9 3.5 %all-to-all-start = ((bf16[16,1,24]{2,1,0:T(2,128)(2,1)}), bf16[16,1,24]{2,1,0:T(2,128)(2,1)S(1)}, u32[]{:S(2)}, u32[]{:S(2)}) async-start(bf16[16,1,24]{2,1,0:T(2,128)(2,1)} %copy.36), calls=%async_computation | async-start | bytes 16384 | tf_op jit(solution)/shard_map/all_to_all | solution.py:81
  27.4 2.8 convolution_convert_fusion.2
  30.1 5.9 %all-to-all-done = bf16[16,1,24]{2,1,0:T(2,128)(2,1)S(1)} async-done(((bf16[16,1,24]{2,1,0:T(2,128)(2,1)}), bf16[16,1,24]{2,1,0:T(2,128)(2,1)S(1)}, u32[]{:S(2)}, u32[]{:S(2)}) %all-to-all-start) | async-done | bytes 800 | tf_op jit(solution)/shard_map/all_to_all | solution.py:81
  36.0 4.4 %all-to-all-start.2 = ((bf16[16,24,2048]{2,1,0:T(8,128)(2,1)}), bf16[16,24,2048]{2,1,0:T(8,128)(2,1)}, u32[]{:S(2)}, u32[]{:S(2)}) async-start(bf16[16,24,2048]{2,1,0:T(8,128)(2,1)} %convolution_convert_fusion.2), calls=%async_computation.2 | async-start | bytes 3145728 | tf_op jit(solution)/shard_map/all_to_all | solution.py:79
  40.5 2.7 convolution_convert_fusion.3
  43.2 32.7 %all-to-all-done.2 = bf16[16,24,2048]{2,1,0:T(8,128)(2,1)} async-done(((bf16[16,24,2048]{2,1,0:T(8,128)(2,1)}), bf16[16,24,2048]{2,1,0:T(8,128)(2,1)}, u32[]{:S(2)}, u32[]{:S(2)}) %all-to-all-start.2) | async-done | bytes 1572896 | tf_op jit(solution)/shard_map/all_to_all | solution.py:79
  75.9 7.2 %all-to-all-start.1 = ((bf16[16,24,2048]{2,1,0:T(8,128)(2,1)}), bf16[16,24,2048]{2,1,0:T(8,128)(2,1)}, u32[]{:S(2)}, u32[]{:S(2)}) async-start(bf16[16,24,2048]{2,1,0:T(8,128)(2,1)} %convolution_convert_fusion.3), calls=%async_computation.1 | async-start | bytes 3145728 | tf_op jit(solution)/shard_map/all_to_all | solution.py:80
  83.0 2.8 convolution_convert_fusion
  85.8 34.3 %all-to-all-done.1 = bf16[16,24,2048]{2,1,0:T(8,128)(2,1)} async-done(((bf16[16,24,2048]{2,1,0:T(8,128)(2,1)}), bf16[16,24,2048]{2,1,0:T(8,128)(2,1)}, u32[]{:S(2)}, u32[]{:S(2)}) %all-to-all-start.1) | async-done | bytes 1572896 | tf_op jit(solution)/shard_map/all_to_all | solution.py:80
  120.1 5.7 %all-to-all-start.6 = ((bf16[16,24,2048]{2,1,0:T(8,128)(2,1)}), bf16[16,24,2048]{2,1,0:T(8,128)(2,1)}, u32[]{:S(2)}, u32[]{:S(2)}) async-start(bf16[16,24,2048]{2,1,0:T(8,128)(2,1)} %convolution_convert_fusion), calls=%async_computation.6 | async-start | bytes 3145728 | tf_op jit(solution)/shard_map/all_to_all | solution.py:79
  125.8 2.7 convolution_convert_fusion.1
  128.5 34.5 %all-to-all-done.6 = bf16[16,24,2048]{2,1,0:T(8,128)(2,1)} async-done(((bf16[16,24,2048]{2,1,0:T(8,128)(2,1)}), bf16[16,24,2048]{2,1,0:T(8,128)(2,1)}, u32[]{:S(2)}, u32[]{:S(2)}) %all-to-all-start.6) | async-done | bytes 1572896 | tf_op jit(solution)/shard_map/all_to_all | solution.py:79
  163.0 5.5 %all-to-all-start.5 = ((bf16[16,24,2048]{2,1,0:T(8,128)(2,1)}), bf16[16,24,2048]{2,1,0:T(8,128)(2,1)}, u32[]{:S(2)}, u32[]{:S(2)}) async-start(bf16[16,24,2048]{2,1,0:T(8,128)(2,1)} %convolution_convert_fusion.1), calls=%async_computation.5 | async-start | bytes 3145728 | tf_op jit(solution)/shard_map/all_to_all | solution.py:80
  168.5 0.0 copy-done
  168.5 3.8 %fusion.8 = f32[384,768]{1,0:T(8,128)} fusion(bf16[384,2048]{1,0:T(8,128)(2,1)} %bitcast.15, bf16[1,1,2048,768]{3,2,1,0:T(8,128)(2,1)S(1)} %copy-done), kind=kOutput, calls=%fused_computation.11 | convolution fusion | flops 1207959552 | bytes 5898240 | tf_op jit(solution)/shard_map/dot_general | solution.py:20
  172.3 2.9 multiply_convert_fusion.1
  175.2 7.0 %fusion.14 = bf16[384,2048]{1,0:T(8,128)(2,1)} fusion(bf16[1,1,2048,768]{3,2,1,0:T(8,128)(2,1)S(1)} %copy-done, bf16[384,2048]{1,0:T(8,128)(2,1)} %bitcast.126, bf16[1,1,768,2048]{3,2,1,0:T(8,128)(2,1)} %param.11, f32[384,768]{1,0:T(8,128)} %fusion.8), kind=kOutput, calls=%fused_computation.20 | convolution fusion | flops 2419359744 | bytes 10616832 | tf_op jit(solution)/shard_map/dot_general | solution.py:25
  182.2 23.5 %all-to-all-done.5 = bf16[16,24,2048]{2,1,0:T(8,128)(2,1)} async-done(((bf16[16,24,2048]{2,1,0:T(8,128)(2,1)}), bf16[16,24,2048]{2,1,0:T(8,128)(2,1)}, u32[]{:S(2)}, u32[]{:S(2)}) %all-to-all-start.5) | async-done | bytes 1572896 | tf_op jit(solution)/shard_map/all_to_all | solution.py:80
  205.7 5.5 %all-to-all-start.3 = ((bf16[16,24,2048]{2,1,0:T(8,128)(2,1)}), bf16[16,24,2048]{2,1,0:T(8,128)(2,1)}, u32[]{:S(2)}, u32[]{:S(2)}) async-start(bf16[16,24,2048]{2,1,0:T(8,128)(2,1)} %bitcast.125), calls=%async_computation.3 | async-start | bytes 3145728 | tf_op jit(solution)/shard_map/all_to_all | solution.py:91
  211.2 3.9 %fusion.4 = f32[384,768]{1,0:T(8,128)} fusion(bf16[384,2048]{1,0:T(8,128)(2,1)} %bitcast.34, bf16[1,1,2048,768]{3,2,1,0:T(8,128)(2,1)S(1)} %copy-done), kind=kOutput, calls=%fused_computation.7 | convolution fusion | flops 1207959552 | bytes 5898240 | tf_op jit(solution)/shard_map/dot_general | solution.py:20
  215.1 2.9 multiply_convert_fusion
  218.0 7.0 %fusion.17 = bf16[384,2048]{1,0:T(8,128)(2,1)} fusion(bf16[1,1,2048,768]{3,2,1,0:T(8,128)(2,1)S(1)} %copy-done, bf16[384,2048]{1,0:T(8,128)(2,1)} %bitcast.127, bf16[1,1,768,2048]{3,2,1,0:T(8,128)(2,1)} %param.11, f32[384,768]{1,0:T(8,128)} %fusion.4), kind=kOutput, calls=%fused_computation.21 | convolution fusion | flops 2419359744 | bytes 10616832 | tf_op jit(solution)/shard_map/dot_general | solution.py:25
  225.0 23.4 %all-to-all-done.3 = bf16[16,24,2048]{2,1,0:T(8,128)(2,1)} async-done(((bf16[16,24,2048]{2,1,0:T(8,128)(2,1)}), bf16[16,24,2048]{2,1,0:T(8,128)(2,1)}, u32[]{:S(2)}, u32[]{:S(2)}) %all-to-all-start.3) | async-done | bytes 1572896 | tf_op jit(solution)/shard_map/all_to_all | solution.py:91
  248.4 5.5 %all-to-all-start.7 = ((bf16[16,24,2048]{2,1,0:T(8,128)(2,1)}), bf16[16,24,2048]{2,1,0:T(8,128)(2,1)}, u32[]{:S(2)}, u32[]{:S(2)}) async-start(bf16[16,24,2048]{2,1,0:T(8,128)(2,1)} %bitcast.124), calls=%async_computation.7 | async-start | bytes 3145728 | tf_op jit(solution)/shard_map/all_to_all | solution.py:91
  254.0 0.1 reshape.96
  254.1 0.1 reshape.94
  254.2 0.0 copy-start.2
  254.2 1.8 fusion.1
  256.0 0.0 copy-done.2
  256.0 1.9 fusion.44
  257.9 0.0 copy-start.1
  257.9 1.8 fusion
  259.8 0.0 copy-done.1
  259.8 4.5 %convolution_add_fusion = f32[768,2048]{1,0:T(8,128)} fusion(f32[768,2048]{1,0:T(8,128)S(1)} %fusion.44, bf16[384,2048]{1,0:T(8,128)(2,1)S(1)} %fusion, f32[384,768]{1,0:T(8,128)S(1)} %copy-done.1), kind=kOutput, calls=%fused_computation | convolution fusion | flops 1211006976 | bytes 15335424 | tf_op jit(solution)/shard_map/dot_general | solution.py:28
  264.3 2.7 fusion.20
  267.0 2.8 collective-permute-start
  269.8 21.4 %all-to-all-done.7 = bf16[16,24,2048]{2,1,0:T(8,128)(2,1)} async-done(((bf16[16,24,2048]{2,1,0:T(8,128)(2,1)}), bf16[16,24,2048]{2,1,0:T(8,128)(2,1)}, u32[]{:S(2)}, u32[]{:S(2)}) %all-to-all-start.7) | async-done | bytes 1572896 | tf_op jit(solution)/shard_map/all_to_all | solution.py:91
  291.1 2.7 fusion.21
  293.8 2.8 collective-permute-start.1
  296.6 24.5 %all-reduce.1 = bf16[768,2048]{1,0:T(8,128)(2,1)} all-reduce(f32[768,2048]{1,0:T(8,128)} %convolution_add_fusion), channel_id=1, replica_groups=mesh['pipe'=8,'expert'=16,'dp'=2] {'dp'}, use_global_device_ids=true, to_apply=%region_6.7 | all-reduce | flops 1572864 | bytes 9437184 | tf_op jit(solution)/shard_map/psum | solution.py:99
  321.1 0.0 collective-permute-done
  321.1 0.0 collective-permute-done.1
  321.1 2.3 maximum_bitcast_fusion
  (11 shorter events, 0.1 us)
Async XLA Ops:
  0.6 167.9 %copy-start = (bf16[1,1,2048,768]{3,2,1,0:T(8,128)(2,1)S(1)}, bf16[1,1,2048,768]{3,2,1,0:T(8,128)(2,1)}, u32[]{:S(2)}) copy-start(bf16[1,1,2048,768]{3,2,1,0:T(8,128)(2,1)} %param.10) | copy-start | bytes 9437188
  3.6 20.3 %all-to-all-start.4 = ((bf16[16,1,24]{2,1,0:T(2,128)(2,1)}), bf16[16,1,24]{2,1,0:T(2,128)(2,1)S(1)}, u32[]{:S(2)}, u32[]{:S(2)}) async-start(bf16[16,1,24]{2,1,0:T(2,128)(2,1)} %copy.39), calls=%async_computation.4 | async-start | bytes 16384 | tf_op jit(solution)/shard_map/all_to_all | solution.py:81
  23.9 12.2 %all-to-all-start = ((bf16[16,1,24]{2,1,0:T(2,128)(2,1)}), bf16[16,1,24]{2,1,0:T(2,128)(2,1)S(1)}, u32[]{:S(2)}, u32[]{:S(2)}) async-start(bf16[16,1,24]{2,1,0:T(2,128)(2,1)} %copy.36), calls=%async_computation | async-start | bytes 16384 | tf_op jit(solution)/shard_map/all_to_all | solution.py:81
  36.0 39.8 %all-to-all-start.2 = ((bf16[16,24,2048]{2,1,0:T(8,128)(2,1)}), bf16[16,24,2048]{2,1,0:T(8,128)(2,1)}, u32[]{:S(2)}, u32[]{:S(2)}) async-start(bf16[16,24,2048]{2,1,0:T(8,128)(2,1)} %convolution_convert_fusion.2), calls=%async_computation.2 | async-start | bytes 3145728 | tf_op jit(solution)/shard_map/all_to_all | solution.py:79
  75.9 44.2 %all-to-all-start.1 = ((bf16[16,24,2048]{2,1,0:T(8,128)(2,1)}), bf16[16,24,2048]{2,1,0:T(8,128)(2,1)}, u32[]{:S(2)}, u32[]{:S(2)}) async-start(bf16[16,24,2048]{2,1,0:T(8,128)(2,1)} %convolution_convert_fusion.3), calls=%async_computation.1 | async-start | bytes 3145728 | tf_op jit(solution)/shard_map/all_to_all | solution.py:80
  120.1 42.9 %all-to-all-start.6 = ((bf16[16,24,2048]{2,1,0:T(8,128)(2,1)}), bf16[16,24,2048]{2,1,0:T(8,128)(2,1)}, u32[]{:S(2)}, u32[]{:S(2)}) async-start(bf16[16,24,2048]{2,1,0:T(8,128)(2,1)} %convolution_convert_fusion), calls=%async_computation.6 | async-start | bytes 3145728 | tf_op jit(solution)/shard_map/all_to_all | solution.py:79
  163.0 42.7 %all-to-all-start.5 = ((bf16[16,24,2048]{2,1,0:T(8,128)(2,1)}), bf16[16,24,2048]{2,1,0:T(8,128)(2,1)}, u32[]{:S(2)}, u32[]{:S(2)}) async-start(bf16[16,24,2048]{2,1,0:T(8,128)(2,1)} %convolution_convert_fusion.1), calls=%async_computation.5 | async-start | bytes 3145728 | tf_op jit(solution)/shard_map/all_to_all | solution.py:80
  205.7 42.7 %all-to-all-start.3 = ((bf16[16,24,2048]{2,1,0:T(8,128)(2,1)}), bf16[16,24,2048]{2,1,0:T(8,128)(2,1)}, u32[]{:S(2)}, u32[]{:S(2)}) async-start(bf16[16,24,2048]{2,1,0:T(8,128)(2,1)} %bitcast.125), calls=%async_computation.3 | async-start | bytes 3145728 | tf_op jit(solution)/shard_map/all_to_all | solution.py:91
  248.4 42.7 %all-to-all-start.7 = ((bf16[16,24,2048]{2,1,0:T(8,128)(2,1)}), bf16[16,24,2048]{2,1,0:T(8,128)(2,1)}, u32[]{:S(2)}, u32[]{:S(2)}) async-start(bf16[16,24,2048]{2,1,0:T(8,128)(2,1)} %bitcast.124), calls=%async_computation.7 | async-start | bytes 3145728 | tf_op jit(solution)/shard_map/all_to_all | solution.py:91
  254.2 1.8 copy-start.2
  257.9 1.8 copy-start.1
  267.0 54.1 %collective-permute-start = (bf16[128,2048]{1,0:T(8,128)(2,1)}, bf16[128,2048]{1,0:T(8,128)(2,1)}, u32[]{:S(2)}, u32[]{:S(2)}) collective-permute-start(bf16[128,2048]{1,0:T(8,128)(2,1)} %fusion.20), channel_id=1, source_target_pairs={{0,224},{32,0},{64,32},{96,64},{128,96},{160,128},{192,160},{224,1... | collective-permute-start | bytes 1572872 | tf_op jit(solution)/shard_map/ppermute | solution.py:13
  293.8 27.3 %collective-permute-start.1 = (bf16[128,2048]{1,0:T(8,128)(2,1)}, bf16[128,2048]{1,0:T(8,128)(2,1)}, u32[]{:S(2)}, u32[]{:S(2)}) collective-permute-start(bf16[128,2048]{1,0:T(8,128)(2,1)} %fusion.21), channel_id=1, source_target_pairs={{0,224},{32,0},{64,32},{96,64},{128,96},{160,128},{192,160},{224,1... | collective-permute-start | bytes 1572872 | tf_op jit(solution)/shard_map/ppermute | solution.py:13
where the time goes:
time: 324 us; the launch traced here: 323 us
  waiting for transfers between devices  183 us (56%)
  starting transfers between devices  54.4 us (17%)
  matrix products  44.8 us (14%)
  blocking collectives  24.5 us (8%)
  other arithmetic  13 us (4%)
    all_to_all x2, waiting for transfers between devices, shards(): lax.all_to_all(sends[micro_idx][0], 'expert', split_axis=0, concat_axis=0...  67.1 us
    all_to_all x2, waiting for transfers between devices, shards(): lax.all_to_all(sends[micro_idx][1], 'expert', split_axis=0, concat_axis=0...  57.8 us
    all_to_all x2, waiting for transfers between devices, shards(): lax.all_to_all(returned.reshape(groups, -1, width), 'expert', split_axis=...  44.8 us
    psum x1, blocking collectives, shards(): proj_grad = lax.psum(partial_value, 'dp').astype(jnp.bfloat16)[None, None]  24.5 us
    all_to_all x2, starting transfers between devices, shards(): lax.all_to_all(sends[micro_idx][2], 'expert', split_axis=0, concat_axis=0...  15.1 us
    dot_general x2, matrix products, expert_rows(): jnp.dot(pre_grad, weight_in.T, preferred_element_type=jnp.float32)  14 us
    all_to_all x2, waiting for transfers between devices, shards(): lax.all_to_all(sends[micro_idx][2], 'expert', split_axis=0, concat_axis=0...  13.5 us
    all_to_all x2, starting transfers between devices, shards(): lax.all_to_all(sends[micro_idx][1], 'expert', split_axis=0, concat_axis=0...  12.7 us
  transfers between devices with their start and end apart: 10, of which 8 were waited for; matrix products, arithmetic and copies ran while one was open for 17% of the time, Pallas kernels for 0%

commit v1 on v0

v1 whole, which is shorter than its diff:
```python
import jax
import jax.numpy as jnp
from jax import lax
from jax.sharding import PartitionSpec as P

EXPERTS = 128
CAP = 24


def from_behind(value, axis, steps):
    count = lax.axis_size(axis)
    pairs = [(source, (source + steps) % count) for source in range(count)]
    return lax.ppermute(value, axis, pairs)


def build_slots(route_ids, gate_rows, groups, local_count):
    targets = jnp.arange(groups, dtype=jnp.int32) * local_count
    matches = route_ids[:, :, None] == targets
    routed = jnp.any(matches, axis=1)
    weight = jnp.sum(jnp.where(matches, gate_rows.astype(jnp.float32)[:, :, None], 0.0), axis=1)
    slot_rank = jnp.cumsum(routed.astype(jnp.int32), axis=0) - 1
    slot_ids = jnp.arange(CAP, dtype=jnp.int32)
    chosen = routed.T[:, None, :] & (slot_rank.T[:, None, :] == slot_ids[None, :, None])
    placing = chosen.astype(jnp.bfloat16)
    gated = jnp.where(chosen, weight.T[:, None, :], 0.0).astype(jnp.bfloat16)
    return (placing, gated)


def take_rows(placing, rows):
    return jnp.einsum("nct,td->ncd", placing, rows, preferred_element_type=jnp.float32).astype(
        jnp.bfloat16
    )


def expert_rows(rows_in, scaled, weight_in, weight_out):
    pre_act = jnp.dot(rows_in, weight_in, preferred_element_type=jnp.float32)
    sigmoid = jax.nn.sigmoid(pre_act)
    hidden = (pre_act * sigmoid).astype(jnp.bfloat16)
    hidden_grad = jnp.dot(scaled, weight_out.T, preferred_element_type=jnp.float32)
    pre_grad = (hidden_grad * sigmoid * (1.0 + pre_act * (1.0 - sigmoid))).astype(jnp.bfloat16)
    returned = jnp.dot(pre_grad, weight_in.T, preferred_element_type=jnp.float32).astype(
        jnp.bfloat16
    )
    return (returned, hidden)


def swap(value):
    return lax.all_to_all(value, "expert", split_axis=0, concat_axis=0, tiled=True)


def shards(inputs, upstream, routes, gate_weights, proj_in, proj_out):
    groups = lax.axis_size("expert")
    local_count = EXPERTS // groups
    micro_count = inputs.shape[1]
    width = inputs.shape[3]
    weight_in = proj_in[0, 0]
    weight_out = proj_out[0, 0]
    placings = []
    sends = []
    for micro in range(micro_count):
        placing, gated = build_slots(routes[0, micro], gate_weights[0, micro], groups, local_count)
        placings.append(placing)
        sends.append(
            jnp.concatenate(
                [take_rows(placing, inputs[0, micro]), take_rows(gated, upstream[0, micro])], axis=2
            )
        )
    received = [swap(send) for send in sends]
    returns = []
    hiddens = []
    scaleds = []
    for micro in range(micro_count):
        rows = received[micro].reshape(-1, 2 * width)
        scaled = rows[:, width:]
        returned, hidden = expert_rows(rows[:, :width], scaled, weight_in, weight_out)
        returns.append(swap(returned.reshape(groups, -1, width)))
        hiddens.append(hidden)
        scaleds.append(scaled)
    partial_value = sum(
        jnp.dot(hidden.T, scaled, preferred_element_type=jnp.float32)
        for hidden, scaled in zip(hiddens, scaleds)
    )
    other = from_behind(partial_value, "dp", 1)
    proj_grad = (partial_value + other).astype(jnp.bfloat16)[None, None]
    outputs = []
    for micro in range(micro_count):
        combined = jnp.einsum(
            "nct,ncd->td", placings[micro], returns[micro], preferred_element_type=jnp.float32
        ).astype(jnp.bfloat16)
        outputs.append(from_behind(combined, "pipe", -1))
    return (jnp.stack(outputs)[None], proj_grad)


def solution(mesh):
    placed = (
        P("pipe", None, ("expert", "dp"), None),
        P("pipe", None, ("expert", "dp"), None),
        P("pipe", None, ("expert", "dp"), None),
        P("pipe", None, ("expert", "dp"), None),
        P("pipe", "expert", None, None),
        P("pipe", "expert", None, None),
    )
    return jax.shard_map(
        shards,
        mesh=mesh,
        in_specs=placed,
        out_specs=(P("pipe", None, ("expert", "dp"), None), P("pipe", "expert", None, None)),
        check_vma=False,
    )
```

time: 324 us -> 290 us (0.90)
  the two profiles are of different devices: /device:TPU:1 before, /device:TPU:14 now
where the time goes in v1:
time: 290 us; the launch traced here: 286 us
  waiting for transfers between devices  181 us (62%)
  starting transfers between devices  44.8 us (15%)
  matrix products  42.7 us (15%)
  other arithmetic  14.7 us (5%)
    all_to_all x4, waiting for transfers between devices, swap(): lax.all_to_all(value, 'expert', split_axis=0, concat_axis=0, tiled=True)  169 us
    all_to_all x4, starting transfers between devices, swap(): lax.all_to_all(value, 'expert', split_axis=0, concat_axis=0, tiled=True)  43.1 us
    dot_general x2, matrix products, shards(): jnp.dot(hidden.T, scaled, preferred_element_type=jnp.float32)  14.2 us
    dot_general x2, matrix products, expert_rows(): jnp.dot(pre_grad, weight_in.T, preferred_element_type=jnp.float32)  13.9 us
    ppermute x3, waiting for transfers between devices, from_behind(): return lax.ppermute(value, axis, pairs)  12.1 us
    broadcast_in_dim x1, other arithmetic, shards(): proj_grad = (partial_value + other).astype(jnp.bfloat16)[None, None]  7.3 us
  transfers between devices with their start and end apart: 7, of which 5 were waited for; matrix products, arithmetic and copies ran while one was open for 16% of the time, Pallas kernels for 0%

profile of v1, /device:TPU:14, one launch (start us, length us, event | category | flops | bytes accessed | tf_op | source)
XLA Modules:
  0.0 286.5 jit_solution(7287819173940374340)
XLA Ops:
  0.6 0.0 copy-start
  0.7 0.9 slice_bitcast_fusion
  1.5 0.1 compare_reduce_fusion.1
  1.6 0.7 bitcast_convert_fusion
  2.3 0.1 copy.16
  2.4 0.2 reduce_window_sum.17
  2.6 0.1 copy.17
  2.7 0.0 copy-start.2
  2.7 0.1 fusion.92
  2.8 1.7 convolution_convert_fusion.3
  4.4 0.0 copy-done.2
  4.5 0.6 convolution_convert_fusion.2
  5.0 2.0 pad_maximum_fusion
  7.1 11.4 %all-to-all-start = ((bf16[16,24,4096]{2,1,0:T(8,128)(2,1)}), bf16[16,24,4096]{2,1,0:T(8,128)(2,1)}, u32[]{:S(2)}, u32[]{:S(2)}) async-start(bf16[16,24,4096]{2,1,0:T(8,128)(2,1)} %pad_maximum_fusion), calls=%async_computation | async-start | bytes 6291456 | tf_op jit(solution)/shard_map/all_to_all | solution.py:48
  18.5 0.1 copy.18
  18.6 0.2 reduce_window_sum.18
  18.8 0.1 copy.19
  18.8 0.0 copy-start.3
  18.8 1.7 convolution_convert_fusion.1
  20.6 0.0 copy-done.3
  20.6 0.6 convolution_convert_fusion
  21.1 2.0 pad_maximum_fusion.1
  23.2 64.7 %all-to-all-done = bf16[16,24,4096]{2,1,0:T(8,128)(2,1)} async-done(((bf16[16,24,4096]{2,1,0:T(8,128)(2,1)}), bf16[16,24,4096]{2,1,0:T(8,128)(2,1)}, u32[]{:S(2)}, u32[]{:S(2)}) %all-to-all-start) | async-done | bytes 3145760 | tf_op jit(solution)/shard_map/all_to_all | solution.py:48
  87.8 12.4 %all-to-all-start.2 = ((bf16[16,24,4096]{2,1,0:T(8,128)(2,1)}), bf16[16,24,4096]{2,1,0:T(8,128)(2,1)}, u32[]{:S(2)}, u32[]{:S(2)}) async-start(bf16[16,24,4096]{2,1,0:T(8,128)(2,1)} %pad_maximum_fusion.1), calls=%async_computation.2 | async-start | bytes 6291456 | tf_op jit(solution)/shard_map/all_to_all | solution.py:48
  100.2 0.0 copy-done
  100.2 2.8 fusion.7
  103.0 0.0 copy-start.4
  103.0 1.0 copy-done.4
  104.0 5.9 %fusion.37 = f32[768,2048]{1,0:T(8,128)} fusion(bf16[384,4096]{1,0:T(8,128)(2,1)} %bitcast.9, f32[384,768]{1,0:T(8,128)S(1)} %fusion.7), kind=kOutput, calls=%fused_computation.35 | convolution fusion | flops 1209434112 | bytes 9043968 | tf_op jit(solution)/shard_map/dot_general | solution.py:80
  110.0 6.9 %fusion.13 = bf16[384,2048]{1,0:T(8,128)(2,1)} fusion(bf16[1,1,2048,768]{3,2,1,0:T(8,128)(2,1)S(1)} %copy-done, bf16[1,1,768,2048]{3,2,1,0:T(8,128)(2,1)} %param.11, bf16[384,4096]{1,0:T(8,128)(2,1)} %bitcast.9, f32[384,768]{1,0:T(8,128)} %copy-done.4), kind=kOutput, calls=%fused_computation.17 | convolution fusion | flops 2419359744 | bytes 10616832 | tf_op jit(solution)/shard_map/dot_general | solution.py:41
  116.9 52.7 %all-to-all-done.2 = bf16[16,24,4096]{2,1,0:T(8,128)(2,1)} async-done(((bf16[16,24,4096]{2,1,0:T(8,128)(2,1)}), bf16[16,24,4096]{2,1,0:T(8,128)(2,1)}, u32[]{:S(2)}, u32[]{:S(2)}) %all-to-all-start.2) | async-done | bytes 3145760 | tf_op jit(solution)/shard_map/all_to_all | solution.py:48
  169.6 12.2 %all-to-all-start.1 = ((bf16[16,24,2048]{2,1,0:T(8,128)(2,1)}), bf16[16,24,2048]{2,1,0:T(8,128)(2,1)}, u32[]{:S(2)}, u32[]{:S(2)}) async-start(bf16[16,24,2048]{2,1,0:T(8,128)(2,1)} %bitcast.92), calls=%async_computation.1 | async-start | bytes 3145728 | tf_op jit(solution)/shard_map/all_to_all | solution.py:48
  181.8 2.8 fusion.3
  184.6 0.0 copy-start.1
  184.6 8.2 %convolution_add_fusion = f32[768,2048]{1,0:T(8,128)} fusion(f32[768,2048]{1,0:T(8,128)} %fusion.37, bf16[384,4096]{1,0:T(8,128)(2,1)} %bitcast.24, f32[384,768]{1,0:T(8,128)S(1)} %fusion.3), kind=kOutput, calls=%fused_computation.1 | convolution fusion | flops 1211006976 | bytes 15335424 | tf_op jit(solution)/shard_map/dot_general | solution.py:80
  192.8 0.0 copy-done.1
  192.8 0.0 collective-permute-start.2
  192.8 6.9 %fusion.16 = bf16[384,2048]{1,0:T(8,128)(2,1)} fusion(bf16[1,1,2048,768]{3,2,1,0:T(8,128)(2,1)S(1)} %copy-done, bf16[1,1,768,2048]{3,2,1,0:T(8,128)(2,1)} %param.11, bf16[384,4096]{1,0:T(8,128)(2,1)} %bitcast.24, f32[384,768]{1,0:T(8,128)} %copy-done.1), kind=kOutput, calls=%fused_computation.18 | convolution fusion | flops 2419359744 | bytes 10616832 | tf_op jit(solution)/shard_map/dot_general | solution.py:41
  199.8 18.6 %all-to-all-done.1 = bf16[16,24,2048]{2,1,0:T(8,128)(2,1)} async-done(((bf16[16,24,2048]{2,1,0:T(8,128)(2,1)}), bf16[16,24,2048]{2,1,0:T(8,128)(2,1)}, u32[]{:S(2)}, u32[]{:S(2)}) %all-to-all-start.1) | async-done | bytes 1572896 | tf_op jit(solution)/shard_map/all_to_all | solution.py:48
  218.4 7.0 %all-to-all-start.3 = ((bf16[16,24,2048]{2,1,0:T(8,128)(2,1)}), bf16[16,24,2048]{2,1,0:T(8,128)(2,1)}, u32[]{:S(2)}, u32[]{:S(2)}) async-start(bf16[16,24,2048]{2,1,0:T(8,128)(2,1)} %bitcast.93), calls=%async_computation.3 | async-start | bytes 3145728 | tf_op jit(solution)/shard_map/all_to_all | solution.py:48
  225.4 2.7 fusion.19
  228.1 0.8 collective-permute-start
  228.9 33.2 %all-to-all-done.3 = bf16[16,24,2048]{2,1,0:T(8,128)(2,1)} async-done(((bf16[16,24,2048]{2,1,0:T(8,128)(2,1)}), bf16[16,24,2048]{2,1,0:T(8,128)(2,1)}, u32[]{:S(2)}, u32[]{:S(2)}) %all-to-all-start.3) | async-done | bytes 1572896 | tf_op jit(solution)/shard_map/all_to_all | solution.py:48
  262.2 1.9 fusion.20
  264.1 0.9 collective-permute-start.1
  265.0 0.0 collective-permute-done
  265.0 12.1 %collective-permute-done.1 = bf16[128,2048]{1,0:T(8,128)(2,1)S(1)} collective-permute-done((bf16[128,2048]{1,0:T(8,128)(2,1)S(1)}, bf16[128,2048]{1,0:T(8,128)(2,1)S(1)}, u32[]{:S(2)}, u32[]{:S(2)}) %collective-permute-start.1) | collective-permute-done | bytes 524320 | tf_op jit(solution)/shard_map/ppermute | solution.py:13
  277.0 2.1 maximum_bitcast_fusion
  279.2 0.0 collective-permute-done.2
  279.2 7.3 %fusion = bf16[1,1,768,2048]{3,2,1,0:T(8,128)(2,1)} fusion(f32[768,2048]{1,0:T(8,128)} %convolution_add_fusion, f32[768,2048]{1,0:T(8,128)} %collective-permute-done.2), kind=kLoop, calls=%fused_computation.2 | loop fusion | flops 3145728 | bytes 15728640 | tf_op jit(solution)/shard_map/broadcast_in_dim | solution.py:84
  (5 shorter events, 0.0 us)
Async XLA Ops:
  0.6 99.6 %copy-start = (bf16[1,1,2048,768]{3,2,1,0:T(8,128)(2,1)S(1)}, bf16[1,1,2048,768]{3,2,1,0:T(8,128)(2,1)}, u32[]{:S(2)}) copy-start(bf16[1,1,2048,768]{3,2,1,0:T(8,128)(2,1)} %param.10) | copy-start | bytes 9437188
  2.7 1.8 copy-start.2
  7.1 80.7 %all-to-all-start = ((bf16[16,24,4096]{2,1,0:T(8,128)(2,1)}), bf16[16,24,4096]{2,1,0:T(8,128)(2,1)}, u32[]{:S(2)}, u32[]{:S(2)}) async-start(bf16[16,24,4096]{2,1,0:T(8,128)(2,1)} %pad_maximum_fusion), calls=%async_computation | async-start | bytes 6291456 | tf_op jit(solution)/shard_map/all_to_all | solution.py:48
  18.8 1.7 copy-start.3
  87.8 81.8 %all-to-all-start.2 = ((bf16[16,24,4096]{2,1,0:T(8,128)(2,1)}), bf16[16,24,4096]{2,1,0:T(8,128)(2,1)}, u32[]{:S(2)}, u32[]{:S(2)}) async-start(bf16[16,24,4096]{2,1,0:T(8,128)(2,1)} %pad_maximum_fusion.1), calls=%async_computation.2 | async-start | bytes 6291456 | tf_op jit(solution)/shard_map/all_to_all | solution.py:48
  103.0 1.0 copy-start.4
  169.6 48.8 %all-to-all-start.1 = ((bf16[16,24,2048]{2,1,0:T(8,128)(2,1)}), bf16[16,24,2048]{2,1,0:T(8,128)(2,1)}, u32[]{:S(2)}, u32[]{:S(2)}) async-start(bf16[16,24,2048]{2,1,0:T(8,128)(2,1)} %bitcast.92), calls=%async_computation.1 | async-start | bytes 3145728 | tf_op jit(solution)/shard_map/all_to_all | solution.py:48
  184.6 8.2 %copy-start.1 = (f32[384,768]{1,0:T(8,128)}, f32[384,768]{1,0:T(8,128)S(1)}, u32[]{:S(2)}) copy-start(f32[384,768]{1,0:T(8,128)S(1)} %fusion.3) | copy-start | bytes 3538948
  192.8 86.3 %collective-permute-start.2 = (f32[768,2048]{1,0:T(8,128)}, f32[768,2048]{1,0:T(8,128)}, u32[]{:S(2)}, u32[]{:S(2)}) collective-permute-start(f32[768,2048]{1,0:T(8,128)} %convolution_add_fusion), channel_id=1, source_target_pairs={{0,1},{1,0},{2,3},{3,2},{4,5},{5,4},{6,7},{7,6},{8,9},{9,8},{10,11... | collective-permute-start | bytes 18874376 | tf_op jit(solution)/shard_map/ppermute | solution.py:13
  218.4 43.8 %all-to-all-start.3 = ((bf16[16,24,2048]{2,1,0:T(8,128)(2,1)}), bf16[16,24,2048]{2,1,0:T(8,128)(2,1)}, u32[]{:S(2)}, u32[]{:S(2)}) async-start(bf16[16,24,2048]{2,1,0:T(8,128)(2,1)} %bitcast.93), calls=%async_computation.3 | async-start | bytes 3145728 | tf_op jit(solution)/shard_map/all_to_all | solution.py:48
  228.1 36.9 %collective-permute-start = (bf16[128,2048]{1,0:T(8,128)(2,1)}, bf16[128,2048]{1,0:T(8,128)(2,1)}, u32[]{:S(2)}, u32[]{:S(2)}) collective-permute-start(bf16[128,2048]{1,0:T(8,128)(2,1)} %fusion.19), channel_id=1, source_target_pairs={{0,224},{32,0},{64,32},{96,64},{128,96},{160,128},{192,160},{224,1... | collective-permute-start | bytes 1572872 | tf_op jit(solution)/shard_map/ppermute | solution.py:13
  264.1 13.0 %collective-permute-start.1 = (bf16[128,2048]{1,0:T(8,128)(2,1)S(1)}, bf16[128,2048]{1,0:T(8,128)(2,1)S(1)}, u32[]{:S(2)}, u32[]{:S(2)}) collective-permute-start(bf16[128,2048]{1,0:T(8,128)(2,1)S(1)} %fusion.20), channel_id=1, source_target_pairs={{0,224},{32,0},{64,32},{96,64},{128,96},{160,128},{192,160},{224,1... | collective-permute-start | bytes 1572872 | tf_op jit(solution)/shard_map/ppermute | solution.py:13

commit v2 on v1

v2 whole, which is shorter than its diff:
```python
import functools

import jax
import jax.numpy as jnp
from jax import lax
from jax.experimental import pallas as pl
from jax.experimental.pallas import tpu as pltpu
from jax.sharding import PartitionSpec as P

EXPERTS = 128
CAP = 24
COLUMNS = 2
AWAY = (0, 4, 1, 7, 2, 6, 3, 5)
EARLY = 4
MEANWHILE = (2, 3, 4, 5)
LAST = (0, 2, 3, 4, 5, 1, 6, 7)
BF16 = jnp.bfloat16
MIB = 1024 * 1024


def from_behind(value, axis, steps):
    count = lax.axis_size(axis)
    pairs = [(source, (source + steps) % count) for source in range(count)]
    return lax.ppermute(value, axis, pairs)


def swap_columns(value):
    return from_behind(value, "expert", lax.axis_size("expert") // COLUMNS)


def along_ring_behind(value, steps):
    sections, groups = lax.axis_size("pipe"), lax.axis_size("expert")
    ring = groups // COLUMNS
    pairs = [
        (s * groups + e, (s - 1) % sections * groups + e // ring * ring + (e + steps) % ring)
        for s in range(sections)
        for e in range(groups)
    ]
    return lax.ppermute(value, ("pipe", "expert"), pairs)


def along_ring(value, steps):
    groups = lax.axis_size("expert")
    ring = groups // COLUMNS
    pairs = [(e, e // ring * ring + (e + steps) % ring) for e in range(groups)]
    return lax.ppermute(value, "expert", pairs)


def together(held, blocks, positions):
    held, arrived = lax.optimization_barrier((held, [blocks[i] for i in positions]))
    return held, {**blocks, **dict(zip(positions, arrived))}


def build_slots(route_ids, gate_rows, experts):
    matches = route_ids[:, :, None] == experts
    routed = jnp.any(matches, axis=1)
    weight = jnp.sum(jnp.where(matches, gate_rows.astype(jnp.float32)[:, :, None], 0.0), axis=1)
    slot_rank = jnp.cumsum(routed.astype(jnp.int32), axis=0) - 1
    slot_ids = jnp.arange(CAP, dtype=jnp.int32)
    chosen = routed.T[:, None, :] & (slot_rank.T[:, None, :] == slot_ids[None, :, None])
    placing = chosen.astype(BF16)
    gated = jnp.where(chosen, weight.T[:, None, :], 0.0).astype(BF16)
    return jnp.stack([placing, gated]).reshape(2, experts.shape[0] * CAP, -1)


def take_rows(slots, inputs, upstream, micro, side_by_side):
    _, rows, tokens = slots.shape
    width = inputs.shape[3]
    blocks = rows // CAP
    piece = 512
    tile = width if side_by_side else width // 2
    tiles = width // tile

    def kernel(slots_ref, inputs_ref, upstream_ref, out_ref):
        def take(rows_ref):
            for start in range(0, tile, piece):
                taken = jnp.dot(
                    slots_ref[0],
                    rows_ref[0, 0, :, start : start + piece],
                    preferred_element_type=jnp.float32,
                )
                for n in range(blocks):
                    block = taken[n * CAP : (n + 1) * CAP].astype(BF16)
                    if side_by_side:
                        out_ref[:, n * width + start : n * width + start + piece] = block
                    else:
                        out_ref[n, :, start : start + piece] = block

        @pl.when(pl.program_id(0) < tiles)
        def _():
            take(inputs_ref)

        @pl.when(pl.program_id(0) >= tiles)
        def _():
            take(upstream_ref)

    if side_by_side:
        out_spec = pl.BlockSpec((CAP, blocks * width), lambda i: (0, i))
        out_shape = (CAP, 2 * blocks * width)
    else:
        out_spec = pl.BlockSpec((blocks, CAP, tile), lambda i: (0, 0, i))
        out_shape = (blocks, CAP, 2 * width)
    return pl.pallas_call(
        kernel,
        grid=(2 * tiles,),
        in_specs=[
            pl.BlockSpec((1, rows, tokens), lambda i: (i // tiles, 0, 0)),
            pl.BlockSpec((1, 1, tokens, tile), lambda i: (0, micro, 0, jnp.minimum(i, tiles - 1))),
            pl.BlockSpec((1, 1, tokens, tile), lambda i: (0, micro, 0, jnp.maximum(i - tiles, 0))),
        ],
        out_specs=out_spec,
        out_shape=pltpu.HBM(out_shape, BF16),
        cost_estimate=pl.CostEstimate(
            flops=4 * rows * tokens * width,
            bytes_accessed=4 * width * (rows + tokens),
            transcendentals=0,
        ),
        compiler_params=pltpu.CompilerParams(vmem_limit_bytes=24 * MIB),
    )(slots, inputs, upstream)


def pack(arrays, moves, out_widths, after=()):
    count, outs = len(arrays) + len(after), len(out_widths)

    def kernel(*refs):
        sources, targets = refs[:count], refs[count : count + outs]
        buffers, in_sems, out_sems = refs[count + outs : -2], refs[-2], refs[-1]
        reads = [
            pltpu.make_async_copy(
                sources[a].at[:, pl.ds(start, size)],
                buffers[o].at[:, pl.ds(to, size)],
                in_sems.at[n],
            )
            for n, (a, start, o, to, size) in enumerate(moves)
        ]
        writes = [
            pltpu.make_async_copy(buffers[o], targets[o], out_sems.at[o]) for o in range(outs)
        ]
        for read in reads:
            read.start()
        for o in range(outs):
            for read, move in zip(reads, moves):
                if move[2] == o:
                    read.wait()
            writes[o].start()
        for write in writes:
            write.wait()

    total = sum(out_widths) * CAP * 2
    shapes = [(CAP, size) for size in out_widths]
    return pl.pallas_call(
        kernel,
        in_specs=[pl.BlockSpec(memory_space=pl.ANY)] * count,
        out_specs=[pl.BlockSpec(memory_space=pl.ANY)] * outs,
        out_shape=[jax.ShapeDtypeStruct(shape, BF16) for shape in shapes],
        scratch_shapes=[pltpu.VMEM(shape, BF16) for shape in shapes]
        + [pltpu.SemaphoreType.DMA((len(moves),)), pltpu.SemaphoreType.DMA((outs,))],
        cost_estimate=pl.CostEstimate(flops=0, bytes_accessed=2 * total, transcendentals=0),
        compiler_params=pltpu.CompilerParams(vmem_limit_bytes=16 * MIB),
    )(*arrays, *after)


def pair_up(own, crossed, ring, after=()):
    size = own.shape[1] // ring
    moves = []
    for d in range(ring):
        moves.append((0, d * size, d, 0, size))
        moves.append((1, d * size, d, size, size))
    return pack([own, crossed], moves, [2 * size] * ring, after)


def expert_rows(blocks, me, weight_in, weight_out, after=()):
    width, hid = weight_in.shape
    one = not isinstance(blocks, list)
    arrays = [blocks] if one else blocks
    count = len(arrays)
    number = blocks.shape[0] if one else COLUMNS * count
    rows = number * CAP
    tile = 256
    piece = 512
    ring = number // COLUMNS

    def kernel(*refs):
        in_ref, out_ref, me_ref = refs[count : count + 3]
        backs = refs[count + 3 + len(after) :][:COLUMNS]
        mine, place = me_ref[0] // ring, me_ref[0] % ring
        hidden_ref, scaled_ref, stacked_ref, pre_grad_ref = refs[-4:]

        def block(n, column):
            columns = slice(column, column + piece)
            if one:
                source = (mine + n) % COLUMNS * ring + (place + ring - AWAY[n // COLUMNS]) % ring
                return refs[0][source, :, columns]
            shift = n % COLUMNS * 2 * width
            return refs[n // COLUMNS][:, column + shift : column + shift + piece]

        for n in range(0, number, 2):
            for target_ref, first in ((stacked_ref, 0), (scaled_ref, width)):
                for start in range(0, width, piece):
                    pair = [block(n + k, first + start).astype(jnp.float32) for k in range(2)]
                    target_ref[n * CAP : (n + 2) * CAP, start : start + piece] = jnp.concatenate(
                        pair, axis=0
                    ).astype(BF16)
        for start in range(0, hid, tile):
            pre_act = jnp.dot(
                stacked_ref[...],
                in_ref[:, start : start + tile],
                preferred_element_type=jnp.float32,
            )
            hidden_grad = lax.dot_general(
                scaled_ref[...],
                out_ref[start : start + tile, :],
                (((1,), (1,)), ((), ())),
                preferred_element_type=jnp.float32,
            )
            sigmoid = jax.nn.sigmoid(pre_act)
            hidden_ref[:, start : start + tile] = (pre_act * sigmoid).astype(BF16)
            pre_grad_ref[:, start : start + tile] = (
                hidden_grad * sigmoid * (1.0 + pre_act * (1.0 - sigmoid))
            ).astype(BF16)
        for start in range(0, width, tile):
            returned = lax.dot_general(
                pre_grad_ref[...],
                in_ref[start : start + tile, :],
                (((1,), (1,)), ((), ())),
                preferred_element_type=jnp.float32,
            )
            for n in range(number):
                rows_back = returned[n * CAP : (n + 1) * CAP].astype(BF16)
                to = n // COLUMNS * width + start
                backs[n % COLUMNS][:, to : to + tile] = rows_back

    shapes = [(CAP, ring * width)] * COLUMNS
    shapes = shapes + [(rows, hid), (rows, width)]
    return pl.pallas_call(
        kernel,
        in_specs=[pl.BlockSpec(memory_space=pltpu.VMEM)] * (count + 2)
        + [pl.BlockSpec(memory_space=pltpu.SMEM)]
        + [pl.BlockSpec(memory_space=pl.ANY)] * len(after),
        out_specs=[pl.BlockSpec(memory_space=pltpu.VMEM)] * len(shapes),
        out_shape=[jax.ShapeDtypeStruct(shape, BF16) for shape in shapes],
        scratch_shapes=[pltpu.VMEM((rows, width), BF16), pltpu.VMEM((rows, hid), BF16)],
        cost_estimate=pl.CostEstimate(
            flops=6 * rows * width * hid,
            bytes_accessed=2 * (rows * width * 4 + 2 * width * hid),
            transcendentals=rows * hid,
        ),
        compiler_params=pltpu.CompilerParams(vmem_limit_bytes=40 * MIB),
    )(*arrays, weight_in, weight_out, me.reshape(1), *after)


def combine(placing, arrived, after=()):
    rows, tokens = placing.shape
    count = len(arrived)
    width = arrived[0].shape[1] // COLUMNS
    piece = 512

    def kernel(placing_ref, *refs):
        out_ref = refs[-1]
        for start in range(0, width, piece):
            stacked = jnp.concatenate(
                [
                    refs[d][:, c * width + start : c * width + start + piece].astype(jnp.float32)
                    for c in range(COLUMNS)
                    for d in range(count)
                ],
                axis=0,
            )
            out_ref[:, start : start + piece] = lax.dot_general(
                placing_ref[...],
                stacked.astype(BF16),
                (((0,), (0,)), ((), ())),
                preferred_element_type=jnp.float32,
            ).astype(BF16)

    return pl.pallas_call(
        kernel,
        in_specs=[pl.BlockSpec(memory_space=pltpu.VMEM)] * (count + 1)
        + [pl.BlockSpec(memory_space=pl.ANY)] * len(after),
        out_specs=pl.BlockSpec(memory_space=pltpu.VMEM),
        out_shape=jax.ShapeDtypeStruct((tokens, width), BF16),
        cost_estimate=pl.CostEstimate(
            flops=2 * rows * tokens * width,
            bytes_accessed=2 * (rows + tokens) * width,
            transcendentals=0,
        ),
        compiler_params=pltpu.CompilerParams(vmem_limit_bytes=24 * MIB),
    )(placing, *arrived, *after)


def weight_grad(hiddens, scaleds, after):
    rows, hid = hiddens[0].shape
    width = scaleds[0].shape[1]
    count = len(hiddens)
    tile = 512

    def kernel(*refs):
        out_ref = refs[-1]
        for start in range(0, hid, 256):
            total = None
            for hidden_ref, scaled_ref in zip(refs[:count], refs[count : 2 * count]):
                term = lax.dot_general(
                    hidden_ref[:, start : start + 256],
                    scaled_ref[...],
                    (((0,), (0,)), ((), ())),
                    preferred_element_type=jnp.float32,
                )
                total = term if total is None else total + term
            out_ref[start : start + 256, :] = total

    return pl.pallas_call(
        kernel,
        grid=(width // tile,),
        in_specs=[pl.BlockSpec((rows, hid), lambda i: (0, 0))] * count
        + [pl.BlockSpec((rows, tile), lambda i: (0, i))] * count
        + [pl.BlockSpec(memory_space=pl.ANY)] * len(after),
        out_specs=pl.BlockSpec((hid, tile), lambda i: (0, i)),
        out_shape=jax.ShapeDtypeStruct((hid, width), jnp.float32),
        cost_estimate=pl.CostEstimate(
            flops=2 * count * rows * hid * width,
            bytes_accessed=4 * hid * width + 2 * count * rows * (hid + width),
            transcendentals=0,
        ),
        compiler_params=pltpu.CompilerParams(vmem_limit_bytes=24 * MIB),
    )(*hiddens, *scaleds, *after)


def swap_groups(value):
    return lax.all_to_all(value, "expert", split_axis=0, concat_axis=0, tiled=True)


def shards(inputs, upstream, routes, gate_weights, proj_in, proj_out):
    groups = lax.axis_size("expert")
    ring = groups // COLUMNS
    local_count = EXPERTS // groups
    width = inputs.shape[3]
    weight_in = proj_in[0, 0]
    weight_out = proj_out[0, 0]
    me = lax.axis_index("expert")
    order = jnp.arange(groups, dtype=jnp.int32)
    place = (jnp.array(AWAY * COLUMNS, jnp.int32) + me) % ring
    near = (order // ring + me // ring) % COLUMNS * ring + place

    slots_0 = build_slots(routes[0, 0], gate_weights[0, 0], order * local_count)
    first = swap_groups(take_rows(slots_0, inputs, upstream, 0, False))

    slots_1 = build_slots(routes[0, 1], gate_weights[0, 1], near * local_count)
    behind = from_behind(slots_1[0], "pipe", -1)
    own_rows, away_rows = slots_1[:, : ring * CAP], slots_1[:, ring * CAP :]

    def send_pack(start, stop):
        count = stop - start
        rows = slice(start * CAP, stop * CAP)
        away = swap_columns(take_rows(away_rows[:, rows], inputs, upstream, 1, True))
        own = take_rows(own_rows[:, rows], inputs, upstream, 1, True)
        moves = []
        for n in range(count):
            for c in range(COLUMNS):
                for part in range(2):
                    column = (part * count + n) * width
                    moves.append((c, column, n, (c * 2 + part) * width, width))
        return pack([own, away], moves, [4 * width] * count)

    blocks = send_pack(0, EARLY)
    second = {i: along_ring(blocks[i], AWAY[i]) for i in range(1, EARLY)}
    own_0, away_0, hidden_0, scaled_0 = expert_rows(first, me, weight_in, weight_out)
    (own_0, away_0, behind), second = together((own_0, away_0, behind), second, range(1, EARLY))
    blocks += send_pack(EARLY, ring)
    second[0] = blocks[0]
    second.update({i: along_ring(blocks[i], AWAY[i]) for i in range(EARLY, ring)})
    back = pair_up(own_0, swap_columns(away_0), ring)
    rest = [i for i in range(1, ring) if i not in MEANWHILE]

    own_1, away_1, hidden_1, scaled_1 = expert_rows(
        [second[i] for i in range(ring)], me, weight_in, weight_out, back[:1]
    )
    back_0 = {i: along_ring(back[i], -AWAY[i]) for i in MEANWHILE}
    partial_value = weight_grad([hidden_0, hidden_1], [scaled_0, scaled_1], [])
    held = (own_1, away_1, partial_value, [back[i] for i in rest])
    (own_1, away_1, partial_value, held), back_0 = together(held, back_0, MEANWHILE)
    back_0.update({i: along_ring(held[n], -AWAY[i]) for n, i in enumerate(rest)})
    back_0[0] = back[0]
    proj_grad = (partial_value + from_behind(partial_value, "dp", 1)).astype(BF16)
    after = [proj_grad] + [back_0[i] for i in rest]
    back = pair_up(own_1, swap_columns(away_1), ring, after)
    back_1 = [along_ring_behind(back[i], -AWAY[i]) for i in LAST]
    back_1 = [back_1[LAST.index(i)] for i in range(ring)]

    placing = jnp.take(slots_0[0].reshape(groups, CAP, -1), near, axis=0).reshape(groups * CAP, -1)
    grad_0 = from_behind(combine(placing, [back_0[i] for i in range(ring)]), "pipe", -1)
    grad_1 = combine(behind, back_1, [grad_0])
    return (jnp.stack([grad_0, grad_1])[None], proj_grad[None, None])


def solution(mesh):
    placed = (
        P("pipe", None, ("expert", "dp"), None),
        P("pipe", None, ("expert", "dp"), None),
        P("pipe", None, ("expert", "dp"), None),
        P("pipe", None, ("expert", "dp"), None),
        P("pipe", "expert", None, None),
        P("pipe", "expert", None, None),
    )
    return jax.shard_map(
        shards,
        mesh=mesh,
        in_specs=placed,
        out_specs=(P("pipe", None, ("expert", "dp"), None), P("pipe", "expert", None, None)),
        check_vma=False,
    )
```

time: 290 us -> 278 us (0.959); the launches traced: 286 us -> 278 us
  matrix products: 42.7 us -> 0 us
  waiting for transfers between devices: 181 us -> 143 us
  Pallas kernels: 0 us -> 35.4 us
  starting transfers between devices: 44.8 us -> 77.6 us
  local copies, waits for them, and re-layouts: 2.2 us -> 10.6 us
  other arithmetic: 14.7 us -> 9.94 us
    all_to_all x4 -> x1, waiting for transfers between devices: 169 us -> 29.8 us  [swap_groups(): lax.all_to_all(value, 'expert', split_axis=0, concat_axis=0, tiled=True)]
    ppermute x0 -> x22, waiting for transfers between devices: none -> 78 us  [the longest x14 39.9 us: along_ring(): return lax.ppermute(value, 'expert', pairs)]
    ppermute x0 -> x22, starting transfers between devices: none -> 57.8 us  [the longest x14 42.2 us: along_ring(): return lax.ppermute(value, 'expert', pairs)]
    dot_general x12 -> x0, matrix products: 42.7 us -> none  [the longest x2 14.2 us: shards(): jnp.dot(hidden.T, scaled, preferred_element_type=jnp.float32)]
    pallas_call x0 -> x14, Pallas kernels: none -> 35.4 us  [the longest x2 11.1 us: expert_rows(): pl.pallas_call(kernel, in_specs=[pl.BlockSpec(memory_space=pltpu.VMEM)] *...]
    all_to_all x4 -> x1, starting transfers between devices: 43.1 us -> 11.4 us  [swap_groups(): lax.all_to_all(value, 'expert', split_axis=0, concat_axis=0, tiled=True)]
    ppermute x3 -> x7, waiting for transfers between devices: 12.1 us -> 35.2 us  [from_behind(): return lax.ppermute(value, axis, pairs)]
    broadcast_in_dim x2 -> x1, other arithmetic: 9.41 us -> 1.06 us  [shards(): return (jnp.stack([grad_0, grad_1])[None], proj_grad[None, None])]
  transfers between devices with their start and end apart: 7 -> 30, of which waited for: 5 -> 13; matrix products, arithmetic and copies ran while one was open for 16% -> 2% of each run, Pallas kernels for 0% -> 12%
where the time goes in v2:
time: 278 us
  waiting for transfers between devices  143 us (51%)
  starting transfers between devices  77.6 us (28%)
  Pallas kernels  35.4 us (13%)
  local copies, waits for them, and re-layouts  10.6 us (4%)
  other arithmetic  9.94 us (4%)
    ppermute x14, starting transfers between devices, along_ring(): return lax.ppermute(value, 'expert', pairs)  42.2 us
    ppermute x14, waiting for transfers between devices, along_ring(): return lax.ppermute(value, 'expert', pairs)  39.9 us
    ppermute x8, waiting for transfers between devices, along_ring_behind(): return lax.ppermute(value, ('pipe', 'expert'), pairs)  38.1 us
    ppermute x7, waiting for transfers between devices, from_behind(): return lax.ppermute(value, axis, pairs)  35.2 us
    all_to_all x1, waiting for transfers between devices, swap_groups(): lax.all_to_all(value, 'expert', split_axis=0, concat_axis=0, tiled=True)  29.8 us
    ppermute x8, starting transfers between devices, along_ring_behind(): return lax.ppermute(value, ('pipe', 'expert'), pairs)  15.6 us
    all_to_all x1, starting transfers between devices, swap_groups(): lax.all_to_all(value, 'expert', split_axis=0, concat_axis=0, tiled=True)  11.4 us
    pallas_call x2, Pallas kernels, expert_rows(): pl.pallas_call(kernel, in_specs=[pl.BlockSpec(memory_space=pltpu.VMEM)] *...  11.1 us
  transfers between devices with their start and end apart: 30, of which 13 were waited for; matrix products, arithmetic and copies ran while one was open for 2% of the time, Pallas kernels for 12%

profile of v2, /device:TPU:14, one launch (start us, length us, event | category | flops | bytes accessed | tf_op | source)
XLA Modules:
  0.0 277.5 jit_solution(5008991483193106326)
XLA Ops:
  0.7 0.8 compare_and_fusion
  1.5 0.5 compare_select_fusion.2
  2.1 0.7 slice_bitcast_fusion
  2.9 0.7 bitcast_convert_fusion
  4.1 0.2 reduce_window_sum.18
  5.0 3.0 %shard_map.86 = bf16[16,24,4096]{2,1,0:T(8,128)(2,1)} custom-call(bf16[2,384,128]{2,1,0:T(8,128)(2,1)S(1)} %pad_maximum_fusion.slots_ref, bf16[1,2,128,2048]{3,2,1,0:T(8,128)(2,1)S(1)} %copy-done, bf16[1,2,128,2048]{3,2,1,0:T(8,128)(2,1)S(1)} %copy-done.1), custom_call_target="tpu_custom_call" | custom-call | flops 402653184 | bytes 4194304 | tf_op jit(solution)/shard_map/pallas_call | solution.py:103
  7.9 11.4 %all-to-all-start = ((bf16[16,24,4096]{2,1,0:T(8,128)(2,1)}), bf16[16,24,4096]{2,1,0:T(8,128)(2,1)}, u32[]{:S(2)}, u32[]{:S(2)}) async-start(bf16[16,24,4096]{2,1,0:T(8,128)(2,1)} %shard_map.86), calls=%async_computation | async-start | bytes 6291456 | tf_op jit(solution)/shard_map/all_to_all | solution.py:329
  19.4 1.3 shard_map.89
  20.9 1.3 shard_map.88.refs_0_
  22.2 32.0 %collective-permute-done.1.refs_1_ = bf16[24,16384]{1,0:T(8,128)(2,1)S(1)} collective-permute-done((bf16[24,16384]{1,0:T(8,128)(2,1)}, bf16[24,16384]{1,0:T(8,128)(2,1)S(1)}, u32[]{:S(2)}, u32[]{:S(2)}) %collective-permute-start.1) | collective-permute-done | bytes 786464 | tf_op jit(solution)/shard_map/ppermute | solution.py:24
  54.1 1.1 copy-done.3
  55.3 2.1 shard_map.90
  57.4 5.3 %collective-permute-start.2 = (bf16[24,8192]{1,0:T(8,128)(2,1)}, bf16[24,8192]{1,0:T(8,128)(2,1)}, u32[]{:S(2)}, u32[]{:S(2)}) collective-permute-start(bf16[24,8192]{1,0:T(8,128)(2,1)} %get-tuple-element.52), channel_id=1, source_target_pairs={{0,8},{2,10},{4,12},{6,14},{8,0},{10,2},{12,4},{14,6},{16,24},{18,... | collective-permute-start | bytes 1179656 | tf_op jit(solution)/shard_map/ppermute | solution.py:46
  62.6 0.6 collective-permute-start.3
  63.2 2.7 collective-permute-start.4
  65.9 1.3 shard_map.93
  67.2 3.0 %collective-permute-start.6 = (bf16[24,16384]{1,0:T(8,128)(2,1)}, bf16[24,16384]{1,0:T(8,128)(2,1)S(1)}, u32[]{:S(2)}, u32[]{:S(2)}) collective-permute-start(bf16[24,16384]{1,0:T(8,128)(2,1)} %shard_map.93), channel_id=1, source_target_pairs={{0,16},{2,18},{4,20},{6,22},{8,24},{10,26},{12,28},{14,30},{16,0},... | collective-permute-start | bytes 2359304 | tf_op jit(solution)/shard_map/ppermute | solution.py:24
  70.3 0.9 collective-permute-start
  71.2 29.8 %all-to-all-done.refs_0_ = bf16[16,24,4096]{2,1,0:T(8,128)(2,1)} async-done(((bf16[16,24,4096]{2,1,0:T(8,128)(2,1)}), bf16[16,24,4096]{2,1,0:T(8,128)(2,1)}, u32[]{:S(2)}, u32[]{:S(2)}) %all-to-all-start) | async-done | bytes 3145760 | tf_op jit(solution)/shard_map/all_to_all | solution.py:329
  101.0 1.9 copy-done.5
  102.9 1.9 copy-done.7
  104.8 6.0 %shard_map.87 = (bf16[24,16384]{1,0:T(8,128)(2,1)S(1)}, bf16[24,16384]{1,0:T(8,128)(2,1)S(1)}, bf16[384,768]{1,0:T(8,128)(2,1)S(1)}, bf16[384,2048]{1,0:T(8,128)(2,1)S(1)}) custom-call(bf16[16,24,4096]{2,1,0:T(8,128)(2,1)} %all-to-all-done.refs_0_, bf16[2048,768]{1,0:T(8,128)(2,1)S(1)} %bitcast.80, bf16[768,2048]{1,0:T(8,128)(2,1)S(1)} %bitcast.82, ...), custom_call_target="tpu_custom_call" | custom-call | flops 3623878656 | bytes 12582912 | tf_op jit(solution)/shard_map/pallas_call | solution.py:235
  110.7 4.6 %collective-permute-done.3.refs_2_ = bf16[24,8192]{1,0:T(8,128)(2,1)} collective-permute-done((bf16[24,8192]{1,0:T(8,128)(2,1)}, bf16[24,8192]{1,0:T(8,128)(2,1)}, u32[]{:S(2)}, u32[]{:S(2)}) %collective-permute-start.3) | collective-permute-done | bytes 393248 | tf_op jit(solution)/shard_map/ppermute | solution.py:46
  115.3 0.5 collective-permute-start.5
  115.8 1.3 shard_map.92.refs_0_
  117.1 1.1 copy-done.4
  118.3 1.6 shard_map.94
  119.9 3.5 %collective-permute-start.7 = (bf16[24,8192]{1,0:T(8,128)(2,1)S(1)}, bf16[24,8192]{1,0:T(8,128)(2,1)S(1)}, u32[]{:S(2)}, u32[]{:S(2)}) collective-permute-start(bf16[24,8192]{1,0:T(8,128)(2,1)S(1)} %get-tuple-element.62), channel_id=1, source_target_pairs={{0,4},{2,6},{4,8},{6,10},{8,12},{10,14},{12,0},{14,2},{16,20},{18,... | collective-permute-start | bytes 1179656 | tf_op jit(solution)/shard_map/ppermute | solution.py:46
  123.4 2.8 %collective-permute-start.8 = (bf16[24,8192]{1,0:T(8,128)(2,1)S(1)}, bf16[24,8192]{1,0:T(8,128)(2,1)S(1)}, u32[]{:S(2)}, u32[]{:S(2)}) collective-permute-start(bf16[24,8192]{1,0:T(8,128)(2,1)S(1)} %get-tuple-element.63), channel_id=1, source_target_pairs={{0,12},{2,14},{4,0},{6,2},{8,4},{10,6},{12,8},{14,10},{16,28},{18,... | collective-permute-start | bytes 1179656 | tf_op jit(solution)/shard_map/ppermute | solution.py:46
  126.2 3.7 %collective-permute-start.9 = (bf16[24,8192]{1,0:T(8,128)(2,1)S(1)}, bf16[24,8192]{1,0:T(8,128)(2,1)S(1)}, u32[]{:S(2)}, u32[]{:S(2)}) collective-permute-start(bf16[24,8192]{1,0:T(8,128)(2,1)S(1)} %get-tuple-element.64), channel_id=1, source_target_pairs={{0,6},{2,8},{4,10},{6,12},{8,14},{10,0},{12,2},{14,4},{16,22},{18,... | collective-permute-start | bytes 1179656 | tf_op jit(solution)/shard_map/ppermute | solution.py:46
  129.9 2.3 collective-permute-start.10
  132.2 3.2 %collective-permute-done.5.refs_1_ = bf16[24,16384]{1,0:T(8,128)(2,1)S(1)} collective-permute-done((bf16[24,16384]{1,0:T(8,128)(2,1)S(1)}, bf16[24,16384]{1,0:T(8,128)(2,1)S(1)}, u32[]{:S(2)}, u32[]{:S(2)}) %collective-permute-start.5) | collective-permute-done | bytes 786464 | tf_op jit(solution)/shard_map/ppermute | solution.py:24
  135.3 2.9 %shard_map.91 = (bf16[24,4096]{1,0:T(8,128)(2,1)S(1)}, bf16[24,4096]{1,0:T(8,128)(2,1)S(1)}, bf16[24,4096]{1,0:T(8,128)(2,1)S(1)}, bf16[24,4096]{1,0:T(8,128)(2,...) custom-call(bf16[24,16384]{1,0:T(8,128)(2,1)S(1)} %get-tuple-element, ...), custom_call_target="tpu_custom_call" | custom-call | bytes 3145728 | tf_op jit(solution)/shard_map/pallas_call | solution.py:151
  138.3 0.7 copy-done.11
  139.0 2.6 collective-permute-start.11
  141.5 8.1 %collective-permute-done.7.refs_4_ = bf16[24,8192]{1,0:T(8,128)(2,1)S(1)} collective-permute-done((bf16[24,8192]{1,0:T(8,128)(2,1)S(1)}, bf16[24,8192]{1,0:T(8,128)(2,1)S(1)}, u32[]{:S(2)}, u32[]{:S(2)}) %collective-permute-start.7) | collective-permute-done | bytes 393248 | tf_op jit(solution)/shard_map/ppermute | solution.py:46
  149.6 7.3 %collective-permute-start.13 = (bf16[24,4096]{1,0:T(8,128)(2,1)S(1)}, bf16[24,4096]{1,0:T(8,128)(2,1)S(1)}, u32[]{:S(2)}, u32[]{:S(2)}) collective-permute-start(bf16[24,4096]{1,0:T(8,128)(2,1)S(1)} %get-tuple-element.77), channel_id=1, source_target_pairs={{0,12},{2,14},{4,0},{6,2},{8,4},{10,6},{12,8},{14,10},{16,28},{18,... | collective-permute-start | bytes 589832 | tf_op jit(solution)/shard_map/ppermute | solution.py:46
  156.9 9.3 %collective-permute-done.9.refs_6_ = bf16[24,8192]{1,0:T(8,128)(2,1)S(1)} collective-permute-done((bf16[24,8192]{1,0:T(8,128)(2,1)S(1)}, bf16[24,8192]{1,0:T(8,128)(2,1)S(1)}, u32[]{:S(2)}, u32[]{:S(2)}) %collective-permute-start.9) | collective-permute-done | bytes 393248 | tf_op jit(solution)/shard_map/ppermute | solution.py:46
  166.2 3.3 %collective-permute-start.14 = (bf16[24,4096]{1,0:T(8,128)(2,1)S(1)}, bf16[24,4096]{1,0:T(8,128)(2,1)S(1)}, u32[]{:S(2)}, u32[]{:S(2)}) collective-permute-start(bf16[24,4096]{1,0:T(8,128)(2,1)S(1)} %get-tuple-element.78), channel_id=1, source_target_pairs={{0,4},{2,6},{4,8},{6,10},{8,12},{10,14},{12,0},{14,2},{16,20},{18,... | collective-permute-start | bytes 589832 | tf_op jit(solution)/shard_map/ppermute | solution.py:46
  169.5 0.6 collective-permute-done.10.refs_7_
  170.2 1.9 copy-done.8
  172.0 5.2 %shard_map.95 = (bf16[24,16384]{1,0:T(8,128)(2,1)S(1)}, bf16[24,16384]{1,0:T(8,128)(2,1)S(1)}, bf16[384,768]{1,0:T(8,128)(2,1)S(1)}, bf16[384,2048]{1,0:T(8,128)(2,1)S(1)}) custom-call(bf16[24,8192]{1,0:T(8,128)(2,1)S(1)} %get-tuple-element.58.refs_0_, bf16[24,8192]{1,0:T(8,128)(2,1)} %collective-permute-done.2.refs_1_, ...), custom_call_target="tpu_custom_call" | custom-call | flops 3623878656 | bytes 12582912 | tf_op jit(solution)/shard_map/pallas_call | solution.py:235
  177.2 5.6 %shard_map.96 = f32[768,2048]{1,0:T(8,128)} custom-call(bf16[384,768]{1,0:T(8,128)(2,1)S(1)} %get-tuple-element.68.refs_0_, bf16[384,768]{1,0:T(8,128)(2,1)S(1)} %get-tuple-element.69.refs_1_, bf16[384,2048]{1,0:T(8,128)(2,1)S(1)} %get-tuple-element.70.refs_2_, bf16[384,2048]{1,0:T(8,128)(2,1)S(1)} %get-tuple-element.71.refs_3_), custom_call_target="tpu_custom_call" | custom-call | flops 2415919104 | bytes 10616832 | tf_op jit(solution)/shard_map/pallas_call | solution.py:311
  183.2 0.6 gather_fusion
  183.8 3.0 %collective-permute-start.15 = (bf16[24,4096]{1,0:T(8,128)(2,1)S(1)}, bf16[24,4096]{1,0:T(8,128)(2,1)S(1)}, u32[]{:S(2)}, u32[]{:S(2)}) collective-permute-start(bf16[24,4096]{1,0:T(8,128)(2,1)S(1)} %copy-done.12), channel_id=1, source_target_pairs={{0,8},{2,10},{4,12},{6,14},{8,0},{10,2},{12,4},{14,6},{16,24},{18,... | collective-permute-start | bytes 589832 | tf_op jit(solution)/shard_map/ppermute | solution.py:46
  186.8 5.3 %collective-permute-start.16 = (bf16[24,4096]{1,0:T(8,128)(2,1)S(1)}, bf16[24,4096]{1,0:T(8,128)(2,1)S(1)}, u32[]{:S(2)}, u32[]{:S(2)}) collective-permute-start(bf16[24,4096]{1,0:T(8,128)(2,1)S(1)} %copy-done.10), channel_id=1, source_target_pairs={{0,10},{2,12},{4,14},{6,0},{8,2},{10,4},{12,6},{14,8},{16,26},{18,... | collective-permute-start | bytes 589832 | tf_op jit(solution)/shard_map/ppermute | solution.py:46
  192.2 2.8 %collective-permute-start.19 = (bf16[24,16384]{1,0:T(8,128)(2,1)S(1)}, bf16[24,16384]{1,0:T(8,128)(2,1)S(1)}, u32[]{:S(2)}, u32[]{:S(2)}) collective-permute-start(bf16[24,16384]{1,0:T(8,128)(2,1)S(1)} %get-tuple-element.88), channel_id=1, source_target_pairs={{0,16},{2,18},{4,20},{6,22},{8,24},{10,26},{12,28},{14,30},{16,0},... | collective-permute-start | bytes 2359304 | tf_op jit(solution)/shard_map/ppermute | solution.py:24
  195.0 0.2 collective-permute-done.15.refs_1_.refs_3_
  195.2 12.8 %collective-permute-done.16.refs_6_.refs_4_ = bf16[24,4096]{1,0:T(8,128)(2,1)S(1)} collective-permute-done((bf16[24,4096]{1,0:T(8,128)(2,1)S(1)}, bf16[24,4096]{1,0:T(8,128)(2,1)S(1)}, u32[]{:S(2)}, u32[]{:S(2)}) %collective-permute-start.16) | collective-permute-done | bytes 196640 | tf_op jit(solution)/shard_map/ppermute | solution.py:46
  208.0 4.2 %collective-permute-done.17.refs_7_.refs_5_ = bf16[24,4096]{1,0:T(8,128)(2,1)S(1)} collective-permute-done((bf16[24,4096]{1,0:T(8,128)(2,1)S(1)}, bf16[24,4096]{1,0:T(8,128)(2,1)S(1)}, u32[]{:S(2)}, u32[]{:S(2)}) %collective-permute-start.17) | collective-permute-done | bytes 196640 | tf_op jit(solution)/shard_map/ppermute | solution.py:46
  212.3 0.5 shard_map.97
  212.8 0.9 collective-permute-start.18
  213.7 5.6 %add_convert_fusion.refs_2_ = bf16[768,2048]{1,0:T(8,128)(2,1)S(1)} fusion(f32[768,2048]{1,0:T(8,128)} %shard_map.96, f32[768,2048]{1,0:T(8,128)} %collective-permute-done.20), kind=kLoop, calls=%fused_computation.1 | loop fusion | flops 3145728 | bytes 15728640 | tf_op jit(solution)/shard_map/convert_element_type | solution.py:383
  219.3 2.9 %shard_map.98 = (bf16[24,4096]{1,0:T(8,128)(2,1)S(1)}, bf16[24,4096]{1,0:T(8,128)(2,1)S(1)}, bf16[24,4096]{1,0:T(8,128)(2,1)S(1)}, bf16[24,4096]{1,0:T(8,128)(2,...) custom-call(bf16[24,16384]{1,0:T(8,128)(2,1)S(1)} %get-tuple-element, ...), custom_call_target="tpu_custom_call" | custom-call | bytes 3145728 | tf_op jit(solution)/shard_map/pallas_call | solution.py:151
  222.3 1.2 collective-permute-start.21
  223.5 4.9 %collective-permute-start.22 = (bf16[24,4096]{1,0:T(8,128)(2,1)S(1)}, bf16[24,4096]{1,0:T(8,128)(2,1)S(1)}, u32[]{:S(2)}, u32[]{:S(2)}) collective-permute-start(bf16[24,4096]{1,0:T(8,128)(2,1)S(1)} %get-tuple-element.91), channel_id=1, source_target_pairs={{0,232},{2,234},{4,236},{6,238},{8,224},{10,226},{12,228},{14,230}... | collective-permute-start | bytes 589832 | tf_op jit(solution)/shard_map/ppermute | solution.py:39
  228.4 5.2 %collective-permute-start.23 = (bf16[24,4096]{1,0:T(8,128)(2,1)S(1)}, bf16[24,4096]{1,0:T(8,128)(2,1)S(1)}, u32[]{:S(2)}, u32[]{:S(2)}) collective-permute-start(bf16[24,4096]{1,0:T(8,128)(2,1)S(1)} %get-tuple-element.92), channel_id=1, source_target_pairs={{0,238},{2,224},{4,226},{6,228},{8,230},{10,232},{12,234},{14,236}... | collective-permute-start | bytes 589832 | tf_op jit(solution)/shard_map/ppermute | solution.py:39
  233.8 3.2 %collective-permute-start.25 = (bf16[24,4096]{1,0:T(8,128)(2,1)S(1)}, bf16[24,4096]{1,0:T(8,128)(2,1)S(1)}, u32[]{:S(2)}, u32[]{:S(2)}) collective-permute-start(bf16[24,4096]{1,0:T(8,128)(2,1)S(1)} %get-tuple-element.94), channel_id=1, source_target_pairs={{0,236},{2,238},{4,224},{6,226},{8,228},{10,230},{12,232},{14,234}... | collective-permute-start | bytes 589832 | tf_op jit(solution)/shard_map/ppermute | solution.py:39
  237.0 0.8 collective-permute-start.26
  237.8 5.1 %collective-permute-done.22.refs_1_ = bf16[24,4096]{1,0:T(8,128)(2,1)S(1)} collective-permute-done((bf16[24,4096]{1,0:T(8,128)(2,1)S(1)}, bf16[24,4096]{1,0:T(8,128)(2,1)S(1)}, u32[]{:S(2)}, u32[]{:S(2)}) %collective-permute-start.22) | collective-permute-done | bytes 196640 | tf_op jit(solution)/shard_map/ppermute | solution.py:39
  243.0 17.9 %collective-permute-done.23.refs_2_ = bf16[24,4096]{1,0:T(8,128)(2,1)S(1)} collective-permute-done((bf16[24,4096]{1,0:T(8,128)(2,1)S(1)}, bf16[24,4096]{1,0:T(8,128)(2,1)S(1)}, u32[]{:S(2)}, u32[]{:S(2)}) %collective-permute-start.23) | collective-permute-done | bytes 196640 | tf_op jit(solution)/shard_map/ppermute | solution.py:39
  260.9 15.1 %collective-permute-done.28.refs_7_ = bf16[24,4096]{1,0:T(8,128)(2,1)S(1)} collective-permute-done((bf16[24,4096]{1,0:T(8,128)(2,1)S(1)}, bf16[24,4096]{1,0:T(8,128)(2,1)S(1)}, u32[]{:S(2)}, u32[]{:S(2)}) %collective-permute-start.28) | collective-permute-done | bytes 196640 | tf_op jit(solution)/shard_map/ppermute | solution.py:39
  276.0 0.5 shard_map.99
  276.5 1.1 maximum_bitcast_fusion
  (76 shorter events, 2.3 us)
Async XLA Ops:
  0.6 4.3 %copy-start.1 = (bf16[1,2,128,2048]{3,2,1,0:T(8,128)(2,1)S(1)}, bf16[1,2,128,2048]{3,2,1,0:T(8,128)(2,1)}, u32[]{:S(2)}) copy-start(bf16[1,2,128,2048]{3,2,1,0:T(8,128)(2,1)} %upstream_ref.9) | copy-start | bytes 3145732
  0.6 4.3 %copy-start = (bf16[1,2,128,2048]{3,2,1,0:T(8,128)(2,1)S(1)}, bf16[1,2,128,2048]{3,2,1,0:T(8,128)(2,1)}, u32[]{:S(2)}) copy-start(bf16[1,2,128,2048]{3,2,1,0:T(8,128)(2,1)} %inputs_ref.9) | copy-start | bytes 3145732
  7.9 93.0 %all-to-all-start = ((bf16[16,24,4096]{2,1,0:T(8,128)(2,1)}), bf16[16,24,4096]{2,1,0:T(8,128)(2,1)}, u32[]{:S(2)}, u32[]{:S(2)}) async-start(bf16[16,24,4096]{2,1,0:T(8,128)(2,1)} %shard_map.86), calls=%async_computation | async-start | bytes 6291456 | tf_op jit(solution)/shard_map/all_to_all | solution.py:329
  20.7 33.4 %collective-permute-start.1 = (bf16[24,16384]{1,0:T(8,128)(2,1)}, bf16[24,16384]{1,0:T(8,128)(2,1)S(1)}, u32[]{:S(2)}, u32[]{:S(2)}) collective-permute-start(bf16[24,16384]{1,0:T(8,128)(2,1)} %shard_map.89), channel_id=1, source_target_pairs={{0,16},{2,18},{4,20},{6,22},{8,24},{10,26},{12,28},{14,30},{16,0},... | collective-permute-start | bytes 2359304 | tf_op jit(solution)/shard_map/ppermute | solution.py:24
  54.1 1.1 copy-start.3
  57.4 53.4 %collective-permute-start.2 = (bf16[24,8192]{1,0:T(8,128)(2,1)}, bf16[24,8192]{1,0:T(8,128)(2,1)}, u32[]{:S(2)}, u32[]{:S(2)}) collective-permute-start(bf16[24,8192]{1,0:T(8,128)(2,1)} %get-tuple-element.52), channel_id=1, source_target_pairs={{0,8},{2,10},{4,12},{6,14},{8,0},{10,2},{12,4},{14,6},{16,24},{18,... | collective-permute-start | bytes 1179656 | tf_op jit(solution)/shard_map/ppermute | solution.py:46
  62.6 52.7 %collective-permute-start.3 = (bf16[24,8192]{1,0:T(8,128)(2,1)}, bf16[24,8192]{1,0:T(8,128)(2,1)}, u32[]{:S(2)}, u32[]{:S(2)}) collective-permute-start(bf16[24,8192]{1,0:T(8,128)(2,1)} %get-tuple-element.53), channel_id=1, source_target_pairs={{0,2},{2,4},{4,6},{6,8},{8,10},{10,12},{12,14},{14,0},{16,18},{18,... | collective-permute-start | bytes 1179656 | tf_op jit(solution)/shard_map/ppermute | solution.py:46
  63.2 52.1 %collective-permute-start.4 = (bf16[24,8192]{1,0:T(8,128)(2,1)}, bf16[24,8192]{1,0:T(8,128)(2,1)}, u32[]{:S(2)}, u32[]{:S(2)}) collective-permute-start(bf16[24,8192]{1,0:T(8,128)(2,1)} %get-tuple-element.54), channel_id=1, source_target_pairs={{0,14},{2,0},{4,2},{6,4},{8,6},{10,8},{12,10},{14,12},{16,30},{18,... | collective-permute-start | bytes 1179656 | tf_op jit(solution)/shard_map/ppermute | solution.py:46
  67.2 50.0 %collective-permute-start.6 = (bf16[24,16384]{1,0:T(8,128)(2,1)}, bf16[24,16384]{1,0:T(8,128)(2,1)S(1)}, u32[]{:S(2)}, u32[]{:S(2)}) collective-permute-start(bf16[24,16384]{1,0:T(8,128)(2,1)} %shard_map.93), channel_id=1, source_target_pairs={{0,16},{2,18},{4,20},{6,22},{8,24},{10,26},{12,28},{14,30},{16,0},... | collective-permute-start | bytes 2359304 | tf_op jit(solution)/shard_map/ppermute | solution.py:24
  70.3 40.5 %collective-permute-start = (bf16[384,128]{1,0:T(8,128)(2,1)S(1)}, bf16[384,128]{1,0:T(8,128)(2,1)S(1)}, u32[]{:S(2)}, u32[]{:S(2)}) collective-permute-start(bf16[384,128]{1,0:T(8,128)(2,1)S(1)} %fusion.6), channel_id=1, source_target_pairs={{0,224},{32,0},{64,32},{96,64},{128,96},{160,128},{192,160},{224,1... | collective-permute-start | bytes 294920 | tf_op jit(solution)/shard_map/ppermute | solution.py:24
  101.0 1.9 copy-start.5
  102.9 1.9 copy-start.7
  104.8 65.4 %copy-start.6 = (bf16[1,1,2048,768]{3,2,1,0:T(8,128)(2,1)S(1)}, bf16[1,1,2048,768]{3,2,1,0:T(8,128)(2,1)}, u32[]{:S(2)}) copy-start(bf16[1,1,2048,768]{3,2,1,0:T(8,128)(2,1)} %param.11) | copy-start | bytes 9437188
  115.3 20.0 %collective-permute-start.5 = (bf16[24,16384]{1,0:T(8,128)(2,1)S(1)}, bf16[24,16384]{1,0:T(8,128)(2,1)S(1)}, u32[]{:S(2)}, u32[]{:S(2)}) collective-permute-start(bf16[24,16384]{1,0:T(8,128)(2,1)S(1)} %get-tuple-element.56), channel_id=1, source_target_pairs={{0,16},{2,18},{4,20},{6,22},{8,24},{10,26},{12,28},{14,30},{16,0},... | collective-permute-start | bytes 2359304 | tf_op jit(solution)/shard_map/ppermute | solution.py:24
  117.1 1.1 copy-start.4
  119.9 29.7 %collective-permute-start.7 = (bf16[24,8192]{1,0:T(8,128)(2,1)S(1)}, bf16[24,8192]{1,0:T(8,128)(2,1)S(1)}, u32[]{:S(2)}, u32[]{:S(2)}) collective-permute-start(bf16[24,8192]{1,0:T(8,128)(2,1)S(1)} %get-tuple-element.62), channel_id=1, source_target_pairs={{0,4},{2,6},{4,8},{6,10},{8,12},{10,14},{12,0},{14,2},{16,20},{18,... | collective-permute-start | bytes 1179656 | tf_op jit(solution)/shard_map/ppermute | solution.py:46
  123.4 26.2 %collective-permute-start.8 = (bf16[24,8192]{1,0:T(8,128)(2,1)S(1)}, bf16[24,8192]{1,0:T(8,128)(2,1)S(1)}, u32[]{:S(2)}, u32[]{:S(2)}) collective-permute-start(bf16[24,8192]{1,0:T(8,128)(2,1)S(1)} %get-tuple-element.63), channel_id=1, source_target_pairs={{0,12},{2,14},{4,0},{6,2},{8,4},{10,6},{12,8},{14,10},{16,28},{18,... | collective-permute-start | bytes 1179656 | tf_op jit(solution)/shard_map/ppermute | solution.py:46
  126.2 40.0 %collective-permute-start.9 = (bf16[24,8192]{1,0:T(8,128)(2,1)S(1)}, bf16[24,8192]{1,0:T(8,128)(2,1)S(1)}, u32[]{:S(2)}, u32[]{:S(2)}) collective-permute-start(bf16[24,8192]{1,0:T(8,128)(2,1)S(1)} %get-tuple-element.64), channel_id=1, source_target_pairs={{0,6},{2,8},{4,10},{6,12},{8,14},{10,0},{12,2},{14,4},{16,22},{18,... | collective-permute-start | bytes 1179656 | tf_op jit(solution)/shard_map/ppermute | solution.py:46
  129.9 40.3 %collective-permute-start.10 = (bf16[24,8192]{1,0:T(8,128)(2,1)S(1)}, bf16[24,8192]{1,0:T(8,128)(2,1)S(1)}, u32[]{:S(2)}, u32[]{:S(2)}) collective-permute-start(bf16[24,8192]{1,0:T(8,128)(2,1)S(1)} %get-tuple-element.65), channel_id=1, source_target_pairs={{0,10},{2,12},{4,14},{6,0},{8,2},{10,4},{12,6},{14,8},{16,26},{18,... | collective-permute-start | bytes 1179656 | tf_op jit(solution)/shard_map/ppermute | solution.py:46
  138.3 0.7 copy-start.11
  139.0 38.2 %copy-start.9 = (bf16[24,4096]{1,0:T(8,128)(2,1)}, bf16[24,4096]{1,0:T(8,128)(2,1)S(1)}, u32[]{:S(2)}) copy-start(bf16[24,4096]{1,0:T(8,128)(2,1)S(1)} %get-tuple-element.84) | copy-start | bytes 589828
  139.0 43.9 %collective-permute-start.11 = (bf16[24,4096]{1,0:T(8,128)(2,1)S(1)}, bf16[24,4096]{1,0:T(8,128)(2,1)S(1)}, u32[]{:S(2)}, u32[]{:S(2)}) collective-permute-start(bf16[24,4096]{1,0:T(8,128)(2,1)S(1)} %get-tuple-element.75), channel_id=1, source_target_pairs={{0,14},{2,0},{4,2},{6,4},{8,6},{10,8},{12,10},{14,12},{16,30},{18,... | collective-permute-start | bytes 589832 | tf_op jit(solution)/shard_map/ppermute | solution.py:46
  149.6 33.3 %collective-permute-start.12 = (bf16[24,4096]{1,0:T(8,128)(2,1)S(1)}, bf16[24,4096]{1,0:T(8,128)(2,1)S(1)}, u32[]{:S(2)}, u32[]{:S(2)}) collective-permute-start(bf16[24,4096]{1,0:T(8,128)(2,1)S(1)} %get-tuple-element.76), channel_id=1, source_target_pairs={{0,2},{2,4},{4,6},{6,8},{8,10},{10,12},{12,14},{14,0},{16,18},{18,... | collective-permute-start | bytes 589832 | tf_op jit(solution)/shard_map/ppermute | solution.py:46
  149.6 33.3 %collective-permute-start.13 = (bf16[24,4096]{1,0:T(8,128)(2,1)S(1)}, bf16[24,4096]{1,0:T(8,128)(2,1)S(1)}, u32[]{:S(2)}, u32[]{:S(2)}) collective-permute-start(bf16[24,4096]{1,0:T(8,128)(2,1)S(1)} %get-tuple-element.77), channel_id=1, source_target_pairs={{0,12},{2,14},{4,0},{6,2},{8,4},{10,6},{12,8},{14,10},{16,28},{18,... | collective-permute-start | bytes 589832 | tf_op jit(solution)/shard_map/ppermute | solution.py:46
  166.2 16.6 %collective-permute-start.14 = (bf16[24,4096]{1,0:T(8,128)(2,1)S(1)}, bf16[24,4096]{1,0:T(8,128)(2,1)S(1)}, u32[]{:S(2)}, u32[]{:S(2)}) collective-permute-start(bf16[24,4096]{1,0:T(8,128)(2,1)S(1)} %get-tuple-element.78), channel_id=1, source_target_pairs={{0,4},{2,6},{4,8},{6,10},{8,12},{10,14},{12,0},{14,2},{16,20},{18,... | collective-permute-start | bytes 589832 | tf_op jit(solution)/shard_map/ppermute | solution.py:46
  170.2 1.9 copy-start.8
  177.2 5.9 %copy-start.13 = (s32[16]{0:T(128)S(1)}, s32[16]{0:T(128)}, u32[]{:S(2)}) copy-start(s32[16]{0:T(128)} %get-tuple-element.112) | copy-start | bytes 196
  177.2 6.6 %copy-start.12 = (bf16[24,4096]{1,0:T(8,128)(2,1)S(1)}, bf16[24,4096]{1,0:T(8,128)(2,1)}, u32[]{:S(2)}) copy-start(bf16[24,4096]{1,0:T(8,128)(2,1)} %copy-done.11) | copy-start | bytes 589828
  177.2 9.5 %copy-start.10 = (bf16[24,4096]{1,0:T(8,128)(2,1)S(1)}, bf16[24,4096]{1,0:T(8,128)(2,1)}, u32[]{:S(2)}) copy-start(bf16[24,4096]{1,0:T(8,128)(2,1)} %copy-done.9) | copy-start | bytes 589828
  182.9 30.8 %collective-permute-start.20 = (f32[768,2048]{1,0:T(8,128)}, f32[768,2048]{1,0:T(8,128)}, u32[]{:S(2)}, u32[]{:S(2)}) collective-permute-start(f32[768,2048]{1,0:T(8,128)} %shard_map.96), channel_id=1, source_target_pairs={{0,1},{1,0},{2,3},{3,2},{4,5},{5,4},{6,7},{7,6},{8,9},{9,8},{10,11... | collective-permute-start | bytes 18874376 | tf_op jit(solution)/shard_map/ppermute | solution.py:24
  183.8 11.4 %collective-permute-start.15 = (bf16[24,4096]{1,0:T(8,128)(2,1)S(1)}, bf16[24,4096]{1,0:T(8,128)(2,1)S(1)}, u32[]{:S(2)}, u32[]{:S(2)}) collective-permute-start(bf16[24,4096]{1,0:T(8,128)(2,1)S(1)} %copy-done.12), channel_id=1, source_target_pairs={{0,8},{2,10},{4,12},{6,14},{8,0},{10,2},{12,4},{14,6},{16,24},{18,... | collective-permute-start | bytes 589832 | tf_op jit(solution)/shard_map/ppermute | solution.py:46
  186.8 21.3 %collective-permute-start.16 = (bf16[24,4096]{1,0:T(8,128)(2,1)S(1)}, bf16[24,4096]{1,0:T(8,128)(2,1)S(1)}, u32[]{:S(2)}, u32[]{:S(2)}) collective-permute-start(bf16[24,4096]{1,0:T(8,128)(2,1)S(1)} %copy-done.10), channel_id=1, source_target_pairs={{0,10},{2,12},{4,14},{6,0},{8,2},{10,4},{12,6},{14,8},{16,26},{18,... | collective-permute-start | bytes 589832 | tf_op jit(solution)/shard_map/ppermute | solution.py:46
  192.0 20.2 %collective-permute-start.17 = (bf16[24,4096]{1,0:T(8,128)(2,1)S(1)}, bf16[24,4096]{1,0:T(8,128)(2,1)S(1)}, u32[]{:S(2)}, u32[]{:S(2)}) collective-permute-start(bf16[24,4096]{1,0:T(8,128)(2,1)S(1)} %get-tuple-element.85), channel_id=1, source_target_pairs={{0,6},{2,8},{4,10},{6,12},{8,14},{10,0},{12,2},{14,4},{16,22},{18,... | collective-permute-start | bytes 589832 | tf_op jit(solution)/shard_map/ppermute | solution.py:46
  192.2 27.2 %collective-permute-start.19 = (bf16[24,16384]{1,0:T(8,128)(2,1)S(1)}, bf16[24,16384]{1,0:T(8,128)(2,1)S(1)}, u32[]{:S(2)}, u32[]{:S(2)}) collective-permute-start(bf16[24,16384]{1,0:T(8,128)(2,1)S(1)} %get-tuple-element.88), channel_id=1, source_target_pairs={{0,16},{2,18},{4,20},{6,22},{8,24},{10,26},{12,28},{14,30},{16,0},... | collective-permute-start | bytes 2359304 | tf_op jit(solution)/shard_map/ppermute | solution.py:24
  212.8 21.0 %collective-permute-start.18 = (bf16[128,2048]{1,0:T(8,128)(2,1)S(1)}, bf16[128,2048]{1,0:T(8,128)(2,1)S(1)}, u32[]{:S(2)}, u32[]{:S(2)}) collective-permute-start(bf16[128,2048]{1,0:T(8,128)(2,1)S(1)} %shard_map.97), channel_id=1, source_target_pairs={{0,224},{32,0},{64,32},{96,64},{128,96},{160,128},{192,160},{224,1... | collective-permute-start | bytes 1572872 | tf_op jit(solution)/shard_map/ppermute | solution.py:24
  219.3 57.2 %copy-start.2 = (bf16[768,2048]{1,0:T(8,128)(2,1)}, bf16[768,2048]{1,0:T(8,128)(2,1)S(1)}, u32[]{:S(2)}) copy-start(bf16[768,2048]{1,0:T(8,128)(2,1)S(1)} %add_convert_fusion.refs_2_) | copy-start | bytes 9437188
  222.3 14.7 %collective-permute-start.21 = (bf16[24,4096]{1,0:T(8,128)(2,1)S(1)}, bf16[24,4096]{1,0:T(8,128)(2,1)S(1)}, u32[]{:S(2)}, u32[]{:S(2)}) collective-permute-start(bf16[24,4096]{1,0:T(8,128)(2,1)S(1)} %get-tuple-element.90), channel_id=1, source_target_pairs={{0,224},{2,226},{4,228},{6,230},{8,232},{10,234},{12,236},{14,238}... | collective-permute-start | bytes 589832 | tf_op jit(solution)/shard_map/ppermute | solution.py:39
  223.5 19.4 %collective-permute-start.22 = (bf16[24,4096]{1,0:T(8,128)(2,1)S(1)}, bf16[24,4096]{1,0:T(8,128)(2,1)S(1)}, u32[]{:S(2)}, u32[]{:S(2)}) collective-permute-start(bf16[24,4096]{1,0:T(8,128)(2,1)S(1)} %get-tuple-element.91), channel_id=1, source_target_pairs={{0,232},{2,234},{4,236},{6,238},{8,224},{10,226},{12,228},{14,230}... | collective-permute-start | bytes 589832 | tf_op jit(solution)/shard_map/ppermute | solution.py:39
  228.4 32.5 %collective-permute-start.23 = (bf16[24,4096]{1,0:T(8,128)(2,1)S(1)}, bf16[24,4096]{1,0:T(8,128)(2,1)S(1)}, u32[]{:S(2)}, u32[]{:S(2)}) collective-permute-start(bf16[24,4096]{1,0:T(8,128)(2,1)S(1)} %get-tuple-element.92), channel_id=1, source_target_pairs={{0,238},{2,224},{4,226},{6,228},{8,230},{10,232},{12,234},{14,236}... | collective-permute-start | bytes 589832 | tf_op jit(solution)/shard_map/ppermute | solution.py:39
  233.6 27.3 %collective-permute-start.24 = (bf16[24,4096]{1,0:T(8,128)(2,1)S(1)}, bf16[24,4096]{1,0:T(8,128)(2,1)S(1)}, u32[]{:S(2)}, u32[]{:S(2)}) collective-permute-start(bf16[24,4096]{1,0:T(8,128)(2,1)S(1)} %get-tuple-element.93), channel_id=1, source_target_pairs={{0,226},{2,228},{4,230},{6,232},{8,234},{10,236},{12,238},{14,224}... | collective-permute-start | bytes 589832 | tf_op jit(solution)/shard_map/ppermute | solution.py:39
  233.8 27.2 %collective-permute-start.25 = (bf16[24,4096]{1,0:T(8,128)(2,1)S(1)}, bf16[24,4096]{1,0:T(8,128)(2,1)S(1)}, u32[]{:S(2)}, u32[]{:S(2)}) collective-permute-start(bf16[24,4096]{1,0:T(8,128)(2,1)S(1)} %get-tuple-element.94), channel_id=1, source_target_pairs={{0,236},{2,238},{4,224},{6,226},{8,228},{10,230},{12,232},{14,234}... | collective-permute-start | bytes 589832 | tf_op jit(solution)/shard_map/ppermute | solution.py:39
  237.0 23.9 %collective-permute-start.26 = (bf16[24,4096]{1,0:T(8,128)(2,1)S(1)}, bf16[24,4096]{1,0:T(8,128)(2,1)S(1)}, u32[]{:S(2)}, u32[]{:S(2)}) collective-permute-start(bf16[24,4096]{1,0:T(8,128)(2,1)S(1)} %get-tuple-element.95), channel_id=1, source_target_pairs={{0,228},{2,230},{4,232},{6,234},{8,236},{10,238},{12,224},{14,226}... | collective-permute-start | bytes 589832 | tf_op jit(solution)/shard_map/ppermute | solution.py:39
  242.9 18.0 %collective-permute-start.27 = (bf16[24,4096]{1,0:T(8,128)(2,1)S(1)}, bf16[24,4096]{1,0:T(8,128)(2,1)S(1)}, u32[]{:S(2)}, u32[]{:S(2)}) collective-permute-start(bf16[24,4096]{1,0:T(8,128)(2,1)S(1)} %get-tuple-element.96), channel_id=1, source_target_pairs={{0,234},{2,236},{4,238},{6,224},{8,226},{10,228},{12,230},{14,232}... | collective-permute-start | bytes 589832 | tf_op jit(solution)/shard_map/ppermute | solution.py:39
  260.9 15.1 %collective-permute-start.28 = (bf16[24,4096]{1,0:T(8,128)(2,1)S(1)}, bf16[24,4096]{1,0:T(8,128)(2,1)S(1)}, u32[]{:S(2)}, u32[]{:S(2)}) collective-permute-start(bf16[24,4096]{1,0:T(8,128)(2,1)S(1)} %get-tuple-element.97), channel_id=1, source_target_pairs={{0,230},{2,232},{4,234},{6,236},{8,238},{10,224},{12,226},{14,228}... | collective-permute-start | bytes 589832 | tf_op jit(solution)/shard_map/ppermute | solution.py:39

commit v3 on v2

--- a/solution.py
+++ b/solution.py
@@ -13,7 +13,7 @@
 AWAY = (0, 4, 1, 7, 2, 6, 3, 5)
 EARLY = 4
 MEANWHILE = (2, 3, 4, 5)
-LAST = (0, 2, 3, 4, 5, 1, 6, 7)
+LAST = (2, 3, 0, 4, 5, 1, 6, 7)
 BF16 = jnp.bfloat16
 MIB = 1024 * 1024
 
@@ -364,8 +364,9 @@
     blocks = send_pack(0, EARLY)
     second = {i: along_ring(blocks[i], AWAY[i]) for i in range(1, EARLY)}
     own_0, away_0, hidden_0, scaled_0 = expert_rows(first, me, weight_in, weight_out)
-    (own_0, away_0, behind), second = together((own_0, away_0, behind), second, range(1, EARLY))
-    blocks += send_pack(EARLY, ring)
+    held = (own_0, away_0, behind, send_pack(EARLY, ring))
+    (own_0, away_0, behind, late), second = together(held, second, range(1, EARLY))
+    blocks += late
     second[0] = blocks[0]
     second.update({i: along_ring(blocks[i], AWAY[i]) for i in range(EARLY, ring)})
     back = pair_up(own_0, swap_columns(away_0), ring)
@@ -380,15 +381,16 @@
     (own_1, away_1, partial_value, held), back_0 = together(held, back_0, MEANWHILE)
     back_0.update({i: along_ring(held[n], -AWAY[i]) for n, i in enumerate(rest)})
     back_0[0] = back[0]
+    held = (partial_value, swap_columns(away_1))
+    (partial_value, away_1), back_0 = together(held, back_0, rest)
+    back = pair_up(own_1, away_1, ring)
     proj_grad = (partial_value + from_behind(partial_value, "dp", 1)).astype(BF16)
-    after = [proj_grad] + [back_0[i] for i in rest]
-    back = pair_up(own_1, swap_columns(away_1), ring, after)
     back_1 = [along_ring_behind(back[i], -AWAY[i]) for i in LAST]
     back_1 = [back_1[LAST.index(i)] for i in range(ring)]
 
     placing = jnp.take(slots_0[0].reshape(groups, CAP, -1), near, axis=0).reshape(groups * CAP, -1)
     grad_0 = from_behind(combine(placing, [back_0[i] for i in range(ring)]), "pipe", -1)
-    grad_1 = combine(behind, back_1, [grad_0])
+    grad_1 = combine(behind, back_1, [grad_0, proj_grad])
     return (jnp.stack([grad_0, grad_1])[None], proj_grad[None, None])
 
 

time: 278 us -> 267 us (0.960)
  waiting for transfers between devices: 143 us -> 127 us
  starting transfers between devices: 77.6 us -> 81 us
    ppermute x7, waiting for transfers between devices: 35.2 us -> 56.1 us  [from_behind(): return lax.ppermute(value, axis, pairs)]
    all_to_all x1, waiting for transfers between devices: 29.8 us -> 10.3 us  [swap_groups(): lax.all_to_all(value, 'expert', split_axis=0, concat_axis=0, tiled=True)]
    ppermute x8, waiting for transfers between devices: 38.1 us -> 25.6 us  [along_ring_behind(): return lax.ppermute(value, ('pipe', 'expert'), pairs)]
    ppermute x8, starting transfers between devices: 15.6 us -> 21.4 us  [along_ring_behind(): return lax.ppermute(value, ('pipe', 'expert'), pairs)]
    ppermute x14, starting transfers between devices: 42.2 us -> 36.6 us  [along_ring(): return lax.ppermute(value, 'expert', pairs)]
    ppermute x14, waiting for transfers between devices: 39.9 us -> 35.4 us  [along_ring(): return lax.ppermute(value, 'expert', pairs)]
    ppermute x7, starting transfers between devices: 8.39 us -> 11.6 us  [from_behind(): return lax.ppermute(value, axis, pairs)]
    unnamed x28 -> x22, local copies, waits for them, and re-layouts: 8.65 us -> 8.95 us
  transfers between devices with their start and end apart: 30 -> 30, of which waited for: 13 -> 16; matrix products, arithmetic and copies ran while one was open for 2% -> 3% of each run, Pallas kernels for 12% -> 12%
where the time goes in v3:
time: 267 us; the launch traced here: 265 us
  waiting for transfers between devices  127 us (48%)
  starting transfers between devices  81 us (30%)
  Pallas kernels  35.5 us (13%)
  local copies, waits for them, and re-layouts  10.9 us (4%)
  other arithmetic  9.42 us (4%)
    ppermute x7, waiting for transfers between devices, from_behind(): return lax.ppermute(value, axis, pairs)  56.1 us
    ppermute x14, starting transfers between devices, along_ring(): return lax.ppermute(value, 'expert', pairs)  36.6 us
    ppermute x14, waiting for transfers between devices, along_ring(): return lax.ppermute(value, 'expert', pairs)  35.4 us
    ppermute x8, waiting for transfers between devices, along_ring_behind(): return lax.ppermute(value, ('pipe', 'expert'), pairs)  25.6 us
    ppermute x8, starting transfers between devices, along_ring_behind(): return lax.ppermute(value, ('pipe', 'expert'), pairs)  21.4 us
    ppermute x7, starting transfers between devices, from_behind(): return lax.ppermute(value, axis, pairs)  11.6 us
    all_to_all x1, starting transfers between devices, swap_groups(): lax.all_to_all(value, 'expert', split_axis=0, concat_axis=0, tiled=True)  11.4 us
    pallas_call x2, Pallas kernels, expert_rows(): pl.pallas_call(kernel, in_specs=[pl.BlockSpec(memory_space=pltpu.VMEM)] *...  11.1 us
  transfers between devices with their start and end apart: 30, of which 16 were waited for; matrix products, arithmetic and copies ran while one was open for 3% of the time, Pallas kernels for 12%

profile of v3, /device:TPU:14, one launch (start us, length us, event | category | flops | bytes accessed | tf_op | source)
XLA Modules:
  0.0 265.1 jit_solution(907896492843566542)
XLA Ops:
  0.7 0.8 compare_and_fusion
  1.6 0.7 slice_bitcast_fusion
  2.4 0.7 bitcast_convert_fusion
  4.5 3.0 %shard_map.86 = bf16[16,24,4096]{2,1,0:T(8,128)(2,1)} custom-call(bf16[2,384,128]{2,1,0:T(8,128)(2,1)S(1)} %pad_maximum_fusion.slots_ref, bf16[1,2,128,2048]{3,2,1,0:T(8,128)(2,1)S(1)} %copy-done, bf16[1,2,128,2048]{3,2,1,0:T(8,128)(2,1)S(1)} %copy-done.1), custom_call_target="tpu_custom_call" | custom-call | flops 402653184 | bytes 4194304 | tf_op jit(solution)/shard_map/pallas_call | solution.py:103
  7.4 11.4 %all-to-all-start = ((bf16[16,24,4096]{2,1,0:T(8,128)(2,1)}), bf16[16,24,4096]{2,1,0:T(8,128)(2,1)}, u32[]{:S(2)}, u32[]{:S(2)}) async-start(bf16[16,24,4096]{2,1,0:T(8,128)(2,1)} %shard_map.86), calls=%async_computation | async-start | bytes 6291456 | tf_op jit(solution)/shard_map/all_to_all | solution.py:329
  18.9 1.3 shard_map.92
  20.4 1.3 shard_map.89
  21.7 3.4 %collective-permute-start.1 = (bf16[24,16384]{1,0:T(8,128)(2,1)}, bf16[24,16384]{1,0:T(8,128)(2,1)S(1)}, u32[]{:S(2)}, u32[]{:S(2)}) collective-permute-start(bf16[24,16384]{1,0:T(8,128)(2,1)} %shard_map.89), channel_id=1, source_target_pairs={{0,16},{2,18},{4,20},{6,22},{8,24},{10,26},{12,28},{14,30},{16,0},... | collective-permute-start | bytes 2359304 | tf_op jit(solution)/shard_map/ppermute | solution.py:24
  25.0 1.3 shard_map.91.refs_0_
  26.3 30.0 %collective-permute-done.2.refs_1_ = bf16[24,16384]{1,0:T(8,128)(2,1)S(1)} collective-permute-done((bf16[24,16384]{1,0:T(8,128)(2,1)}, bf16[24,16384]{1,0:T(8,128)(2,1)S(1)}, u32[]{:S(2)}, u32[]{:S(2)}) %collective-permute-start.2) | collective-permute-done | bytes 786464 | tf_op jit(solution)/shard_map/ppermute | solution.py:24
  56.4 1.1 copy-done.3
  57.5 2.1 shard_map.93
  59.6 3.1 %collective-permute-start.3 = (bf16[24,8192]{1,0:T(8,128)(2,1)}, bf16[24,8192]{1,0:T(8,128)(2,1)S(1)}, u32[]{:S(2)}, u32[]{:S(2)}) collective-permute-start(bf16[24,8192]{1,0:T(8,128)(2,1)} %get-tuple-element.65), channel_id=1, source_target_pairs={{0,8},{2,10},{4,12},{6,14},{8,0},{10,2},{12,4},{14,6},{16,24},{18,... | collective-permute-start | bytes 1179656 | tf_op jit(solution)/shard_map/ppermute | solution.py:46
  62.7 0.9 collective-permute-start.4
  63.6 2.3 collective-permute-start.5
  66.0 0.9 collective-permute-start
  66.9 1.3 shard_map.88.refs_0_
  68.2 19.0 %collective-permute-done.1.refs_1_ = bf16[24,16384]{1,0:T(8,128)(2,1)S(1)} collective-permute-done((bf16[24,16384]{1,0:T(8,128)(2,1)}, bf16[24,16384]{1,0:T(8,128)(2,1)S(1)}, u32[]{:S(2)}, u32[]{:S(2)}) %collective-permute-start.1) | collective-permute-done | bytes 786464 | tf_op jit(solution)/shard_map/ppermute | solution.py:24
  87.2 1.1 copy-done.4
  88.3 1.6 shard_map.90
  90.0 10.3 %all-to-all-done.refs_0_ = bf16[16,24,4096]{2,1,0:T(8,128)(2,1)} async-done(((bf16[16,24,4096]{2,1,0:T(8,128)(2,1)}), bf16[16,24,4096]{2,1,0:T(8,128)(2,1)}, u32[]{:S(2)}, u32[]{:S(2)}) %all-to-all-start) | async-done | bytes 3145760 | tf_op jit(solution)/shard_map/all_to_all | solution.py:329
  100.2 1.9 copy-done.5
  102.1 1.9 copy-done.7
  104.0 6.0 %shard_map.87 = (bf16[24,16384]{1,0:T(8,128)(2,1)S(1)}, bf16[24,16384]{1,0:T(8,128)(2,1)S(1)}, bf16[384,768]{1,0:T(8,128)(2,1)S(1)}, bf16[384,2048]{1,0:T(8,128)(2,1)S(1)}) custom-call(bf16[16,24,4096]{2,1,0:T(8,128)(2,1)} %all-to-all-done.refs_0_, bf16[2048,768]{1,0:T(8,128)(2,1)S(1)} %bitcast.80, bf16[768,2048]{1,0:T(8,128)(2,1)S(1)} %bitcast.82, ...), custom_call_target="tpu_custom_call" | custom-call | flops 3623878656 | bytes 12582912 | tf_op jit(solution)/shard_map/pallas_call | solution.py:235
  110.1 4.7 %collective-permute-done.4.refs_2_ = bf16[24,8192]{1,0:T(8,128)(2,1)} collective-permute-done((bf16[24,8192]{1,0:T(8,128)(2,1)}, bf16[24,8192]{1,0:T(8,128)(2,1)}, u32[]{:S(2)}, u32[]{:S(2)}) %collective-permute-start.4) | collective-permute-done | bytes 393248 | tf_op jit(solution)/shard_map/ppermute | solution.py:46
  115.3 3.6 %collective-permute-start.7 = (bf16[24,8192]{1,0:T(8,128)(2,1)S(1)}, bf16[24,8192]{1,0:T(8,128)(2,1)S(1)}, u32[]{:S(2)}, u32[]{:S(2)}) collective-permute-start(bf16[24,8192]{1,0:T(8,128)(2,1)S(1)} %get-tuple-element.75), channel_id=1, source_target_pairs={{0,4},{2,6},{4,8},{6,10},{8,12},{10,14},{12,0},{14,2},{16,20},{18,... | collective-permute-start | bytes 1179656 | tf_op jit(solution)/shard_map/ppermute | solution.py:46
  118.9 2.8 %collective-permute-start.8 = (bf16[24,8192]{1,0:T(8,128)(2,1)S(1)}, bf16[24,8192]{1,0:T(8,128)(2,1)S(1)}, u32[]{:S(2)}, u32[]{:S(2)}) collective-permute-start(bf16[24,8192]{1,0:T(8,128)(2,1)S(1)} %get-tuple-element.76), channel_id=1, source_target_pairs={{0,12},{2,14},{4,0},{6,2},{8,4},{10,6},{12,8},{14,10},{16,28},{18,... | collective-permute-start | bytes 1179656 | tf_op jit(solution)/shard_map/ppermute | solution.py:46
  121.7 3.4 %collective-permute-start.9 = (bf16[24,8192]{1,0:T(8,128)(2,1)S(1)}, bf16[24,8192]{1,0:T(8,128)(2,1)S(1)}, u32[]{:S(2)}, u32[]{:S(2)}) collective-permute-start(bf16[24,8192]{1,0:T(8,128)(2,1)S(1)} %get-tuple-element.77), channel_id=1, source_target_pairs={{0,6},{2,8},{4,10},{6,12},{8,14},{10,0},{12,2},{14,4},{16,22},{18,... | collective-permute-start | bytes 1179656 | tf_op jit(solution)/shard_map/ppermute | solution.py:46
  125.1 2.7 %collective-permute-start.10 = (bf16[24,8192]{1,0:T(8,128)(2,1)S(1)}, bf16[24,8192]{1,0:T(8,128)(2,1)S(1)}, u32[]{:S(2)}, u32[]{:S(2)}) collective-permute-start(bf16[24,8192]{1,0:T(8,128)(2,1)S(1)} %get-tuple-element.78), channel_id=1, source_target_pairs={{0,10},{2,12},{4,14},{6,0},{8,2},{10,4},{12,6},{14,8},{16,26},{18,... | collective-permute-start | bytes 1179656 | tf_op jit(solution)/shard_map/ppermute | solution.py:46
  127.7 7.1 %collective-permute-done.6.refs_1_ = bf16[24,16384]{1,0:T(8,128)(2,1)S(1)} collective-permute-done((bf16[24,16384]{1,0:T(8,128)(2,1)S(1)}, bf16[24,16384]{1,0:T(8,128)(2,1)S(1)}, u32[]{:S(2)}, u32[]{:S(2)}) %collective-permute-start.6) | collective-permute-done | bytes 786464 | tf_op jit(solution)/shard_map/ppermute | solution.py:24
  134.8 2.9 %shard_map.94 = (bf16[24,4096]{1,0:T(8,128)(2,1)S(1)}, bf16[24,4096]{1,0:T(8,128)(2,1)S(1)}, bf16[24,4096]{1,0:T(8,128)(2,1)S(1)}, bf16[24,4096]{1,0:T(8,128)(2,...) custom-call(bf16[24,16384]{1,0:T(8,128)(2,1)S(1)} %get-tuple-element, ...), custom_call_target="tpu_custom_call" | custom-call | bytes 3145728 | tf_op jit(solution)/shard_map/pallas_call | solution.py:151
  137.7 2.6 collective-permute-start.11
  140.4 6.0 %collective-permute-done.7.refs_4_ = bf16[24,8192]{1,0:T(8,128)(2,1)S(1)} collective-permute-done((bf16[24,8192]{1,0:T(8,128)(2,1)S(1)}, bf16[24,8192]{1,0:T(8,128)(2,1)S(1)}, u32[]{:S(2)}, u32[]{:S(2)}) %collective-permute-start.7) | collective-permute-done | bytes 393248 | tf_op jit(solution)/shard_map/ppermute | solution.py:46
  146.4 4.2 %collective-permute-start.13 = (bf16[24,4096]{1,0:T(8,128)(2,1)S(1)}, bf16[24,4096]{1,0:T(8,128)(2,1)S(1)}, u32[]{:S(2)}, u32[]{:S(2)}) collective-permute-start(bf16[24,4096]{1,0:T(8,128)(2,1)S(1)} %get-tuple-element.90), channel_id=1, source_target_pairs={{0,12},{2,14},{4,0},{6,2},{8,4},{10,6},{12,8},{14,10},{16,28},{18,... | collective-permute-start | bytes 589832 | tf_op jit(solution)/shard_map/ppermute | solution.py:46
  150.5 10.6 %collective-permute-done.9.refs_6_ = bf16[24,8192]{1,0:T(8,128)(2,1)S(1)} collective-permute-done((bf16[24,8192]{1,0:T(8,128)(2,1)S(1)}, bf16[24,8192]{1,0:T(8,128)(2,1)S(1)}, u32[]{:S(2)}, u32[]{:S(2)}) %collective-permute-start.9) | collective-permute-done | bytes 393248 | tf_op jit(solution)/shard_map/ppermute | solution.py:46
  161.1 3.2 %collective-permute-start.14 = (bf16[24,4096]{1,0:T(8,128)(2,1)S(1)}, bf16[24,4096]{1,0:T(8,128)(2,1)S(1)}, u32[]{:S(2)}, u32[]{:S(2)}) collective-permute-start(bf16[24,4096]{1,0:T(8,128)(2,1)S(1)} %get-tuple-element.91), channel_id=1, source_target_pairs={{0,4},{2,6},{4,8},{6,10},{8,12},{10,14},{12,0},{14,2},{16,20},{18,... | collective-permute-start | bytes 589832 | tf_op jit(solution)/shard_map/ppermute | solution.py:46
  164.3 0.8 collective-permute-done.10.refs_7_
  165.1 1.9 copy-done.8
  167.0 1.0 copy-done.10
  168.0 5.1 %shard_map.95 = (bf16[24,16384]{1,0:T(8,128)(2,1)S(1)}, bf16[24,16384]{1,0:T(8,128)(2,1)S(1)}, bf16[384,768]{1,0:T(8,128)(2,1)S(1)}, bf16[384,2048]{1,0:T(8,128)(2,1)S(1)}) custom-call(bf16[24,8192]{1,0:T(8,128)(2,1)S(1)} %get-tuple-element.71.refs_0_, bf16[24,8192]{1,0:T(8,128)(2,1)S(1)} %copy-done.10, bf16[24,8192]{1,0:T(8,128)(2,1)} %collective-permute-done.4.refs_2_, ...), custom_call_target="tpu_custom_call" | custom-call | flops 3623878656 | bytes 12582912 | tf_op jit(solution)/shard_map/pallas_call | solution.py:235
  173.1 5.6 %shard_map.96 = f32[768,2048]{1,0:T(8,128)} custom-call(bf16[384,768]{1,0:T(8,128)(2,1)S(1)} %get-tuple-element.81.refs_0_, bf16[384,768]{1,0:T(8,128)(2,1)S(1)} %get-tuple-element.82.refs_1_, bf16[384,2048]{1,0:T(8,128)(2,1)S(1)} %get-tuple-element.83.refs_2_, bf16[384,2048]{1,0:T(8,128)(2,1)S(1)} %get-tuple-element.84.refs_3_), custom_call_target="tpu_custom_call" | custom-call | flops 2415919104 | bytes 10616832 | tf_op jit(solution)/shard_map/pallas_call | solution.py:311
  178.8 4.1 %collective-permute-start.15 = (bf16[24,16384]{1,0:T(8,128)(2,1)S(1)}, bf16[24,16384]{1,0:T(8,128)(2,1)S(1)}, u32[]{:S(2)}, u32[]{:S(2)}) collective-permute-start(bf16[24,16384]{1,0:T(8,128)(2,1)S(1)} %get-tuple-element.93), channel_id=1, source_target_pairs={{0,16},{2,18},{4,20},{6,22},{8,24},{10,26},{12,28},{14,30},{16,0},... | collective-permute-start | bytes 2359304 | tf_op jit(solution)/shard_map/ppermute | solution.py:24
  182.9 4.1 %collective-permute-start.16 = (bf16[24,4096]{1,0:T(8,128)(2,1)S(1)}, bf16[24,4096]{1,0:T(8,128)(2,1)S(1)}, u32[]{:S(2)}, u32[]{:S(2)}) collective-permute-start(bf16[24,4096]{1,0:T(8,128)(2,1)S(1)} %get-tuple-element.94), channel_id=1, source_target_pairs={{0,8},{2,10},{4,12},{6,14},{8,0},{10,2},{12,4},{14,6},{16,24},{18,... | collective-permute-start | bytes 589832 | tf_op jit(solution)/shard_map/ppermute | solution.py:46
  187.0 2.5 collective-permute-start.17
  189.5 1.3 collective-permute-start.18
  190.8 11.1 %collective-permute-done.16.refs_1_ = bf16[24,4096]{1,0:T(8,128)(2,1)S(1)} collective-permute-done((bf16[24,4096]{1,0:T(8,128)(2,1)S(1)}, bf16[24,4096]{1,0:T(8,128)(2,1)S(1)}, u32[]{:S(2)}, u32[]{:S(2)}) %collective-permute-start.16) | collective-permute-done | bytes 196640 | tf_op jit(solution)/shard_map/ppermute | solution.py:46
  201.9 1.5 collective-permute-done.17.refs_6_
  203.5 0.6 collective-permute-done.18.refs_7_
  204.9 2.9 %shard_map.98 = (bf16[24,4096]{1,0:T(8,128)(2,1)S(1)}, bf16[24,4096]{1,0:T(8,128)(2,1)S(1)}, bf16[24,4096]{1,0:T(8,128)(2,1)S(1)}, bf16[24,4096]{1,0:T(8,128)(2,...) custom-call(bf16[24,16384]{1,0:T(8,128)(2,1)S(1)} %get-tuple-element, ...), custom_call_target="tpu_custom_call" | custom-call | bytes 3145728 | tf_op jit(solution)/shard_map/pallas_call | solution.py:151
  207.9 1.7 collective-permute-start.20
  209.6 6.0 %collective-permute-start.21 = (bf16[24,4096]{1,0:T(8,128)(2,1)S(1)}, bf16[24,4096]{1,0:T(8,128)(2,1)S(1)}, u32[]{:S(2)}, u32[]{:S(2)}) collective-permute-start(bf16[24,4096]{1,0:T(8,128)(2,1)S(1)} %get-tuple-element.108), channel_id=1, source_target_pairs={{0,232},{2,234},{4,236},{6,238},{8,224},{10,226},{12,228},{14,230}... | collective-permute-start | bytes 589832 | tf_op jit(solution)/shard_map/ppermute | solution.py:39
  215.5 2.4 collective-permute-start.22
  218.0 1.1 collective-permute-start.23
  219.7 2.5 collective-permute-start.19
  222.1 1.3 collective-permute-done.21.refs_1_
  223.4 4.7 %collective-permute-start.24 = (bf16[24,4096]{1,0:T(8,128)(2,1)S(1)}, bf16[24,4096]{1,0:T(8,128)(2,1)S(1)}, u32[]{:S(2)}, u32[]{:S(2)}) collective-permute-start(bf16[24,4096]{1,0:T(8,128)(2,1)S(1)} %get-tuple-element.111), channel_id=1, source_target_pairs={{0,236},{2,238},{4,224},{6,226},{8,228},{10,230},{12,232},{14,234}... | collective-permute-start | bytes 589832 | tf_op jit(solution)/shard_map/ppermute | solution.py:39
  228.1 8.7 %collective-permute-done.22.refs_2_ = bf16[24,4096]{1,0:T(8,128)(2,1)S(1)} collective-permute-done((bf16[24,4096]{1,0:T(8,128)(2,1)S(1)}, bf16[24,4096]{1,0:T(8,128)(2,1)S(1)}, u32[]{:S(2)}, u32[]{:S(2)}) %collective-permute-start.22) | collective-permute-done | bytes 196640 | tf_op jit(solution)/shard_map/ppermute | solution.py:39
  236.8 4.6 %collective-permute-start.26 = (bf16[24,4096]{1,0:T(8,128)(2,1)S(1)}, bf16[24,4096]{1,0:T(8,128)(2,1)S(1)}, u32[]{:S(2)}, u32[]{:S(2)}) collective-permute-start(bf16[24,4096]{1,0:T(8,128)(2,1)S(1)} %get-tuple-element.113), channel_id=1, source_target_pairs={{0,234},{2,236},{4,238},{6,224},{8,226},{10,228},{12,230},{14,232}... | collective-permute-start | bytes 589832 | tf_op jit(solution)/shard_map/ppermute | solution.py:39
  241.4 1.0 collective-permute-start.27
  242.4 5.6 %add_convert_fusion.refs_9_ = bf16[768,2048]{1,0:T(8,128)(2,1)S(1)} fusion(f32[768,2048]{1,0:T(8,128)} %shard_map.96, f32[768,2048]{1,0:T(8,128)} %collective-permute-done.28), kind=kLoop, calls=%fused_computation.1 | loop fusion | flops 3145728 | bytes 15728640 | tf_op jit(solution)/shard_map/convert_element_type | solution.py:387
  248.1 5.4 %collective-permute-done.25.refs_5_ = bf16[24,4096]{1,0:T(8,128)(2,1)S(1)} collective-permute-done((bf16[24,4096]{1,0:T(8,128)(2,1)S(1)}, bf16[24,4096]{1,0:T(8,128)(2,1)S(1)}, u32[]{:S(2)}, u32[]{:S(2)}) %collective-permute-start.25) | collective-permute-done | bytes 196640 | tf_op jit(solution)/shard_map/ppermute | solution.py:39
  253.5 6.0 %collective-permute-done.26.refs_6_ = bf16[24,4096]{1,0:T(8,128)(2,1)S(1)} collective-permute-done((bf16[24,4096]{1,0:T(8,128)(2,1)S(1)}, bf16[24,4096]{1,0:T(8,128)(2,1)S(1)}, u32[]{:S(2)}, u32[]{:S(2)}) %collective-permute-start.26) | collective-permute-done | bytes 196640 | tf_op jit(solution)/shard_map/ppermute | solution.py:39
  259.4 4.2 %collective-permute-done.27.refs_7_ = bf16[24,4096]{1,0:T(8,128)(2,1)S(1)} collective-permute-done((bf16[24,4096]{1,0:T(8,128)(2,1)S(1)}, bf16[24,4096]{1,0:T(8,128)(2,1)S(1)}, u32[]{:S(2)}, u32[]{:S(2)}) %collective-permute-start.27) | collective-permute-done | bytes 196640 | tf_op jit(solution)/shard_map/ppermute | solution.py:39
  264.1 1.1 maximum_bitcast_fusion
  (70 shorter events, 4.2 us)
Async XLA Ops:
  0.6 3.8 %copy-start.1 = (bf16[1,2,128,2048]{3,2,1,0:T(8,128)(2,1)S(1)}, bf16[1,2,128,2048]{3,2,1,0:T(8,128)(2,1)}, u32[]{:S(2)}) copy-start(bf16[1,2,128,2048]{3,2,1,0:T(8,128)(2,1)} %upstream_ref.9) | copy-start | bytes 3145732
  0.6 3.8 %copy-start = (bf16[1,2,128,2048]{3,2,1,0:T(8,128)(2,1)S(1)}, bf16[1,2,128,2048]{3,2,1,0:T(8,128)(2,1)}, u32[]{:S(2)}) copy-start(bf16[1,2,128,2048]{3,2,1,0:T(8,128)(2,1)} %inputs_ref.9) | copy-start | bytes 3145732
  7.4 92.8 %all-to-all-start = ((bf16[16,24,4096]{2,1,0:T(8,128)(2,1)}), bf16[16,24,4096]{2,1,0:T(8,128)(2,1)}, u32[]{:S(2)}, u32[]{:S(2)}) async-start(bf16[16,24,4096]{2,1,0:T(8,128)(2,1)} %shard_map.86), calls=%async_computation | async-start | bytes 6291456 | tf_op jit(solution)/shard_map/all_to_all | solution.py:329
  20.2 36.1 %collective-permute-start.2 = (bf16[24,16384]{1,0:T(8,128)(2,1)}, bf16[24,16384]{1,0:T(8,128)(2,1)S(1)}, u32[]{:S(2)}, u32[]{:S(2)}) collective-permute-start(bf16[24,16384]{1,0:T(8,128)(2,1)} %shard_map.92), channel_id=1, source_target_pairs={{0,16},{2,18},{4,20},{6,22},{8,24},{10,26},{12,28},{14,30},{16,0},... | collective-permute-start | bytes 2359304 | tf_op jit(solution)/shard_map/ppermute | solution.py:24
  21.7 65.5 %collective-permute-start.1 = (bf16[24,16384]{1,0:T(8,128)(2,1)}, bf16[24,16384]{1,0:T(8,128)(2,1)S(1)}, u32[]{:S(2)}, u32[]{:S(2)}) collective-permute-start(bf16[24,16384]{1,0:T(8,128)(2,1)} %shard_map.89), channel_id=1, source_target_pairs={{0,16},{2,18},{4,20},{6,22},{8,24},{10,26},{12,28},{14,30},{16,0},... | collective-permute-start | bytes 2359304 | tf_op jit(solution)/shard_map/ppermute | solution.py:24
  56.4 1.1 copy-start.3
  59.6 50.4 %collective-permute-start.3 = (bf16[24,8192]{1,0:T(8,128)(2,1)}, bf16[24,8192]{1,0:T(8,128)(2,1)S(1)}, u32[]{:S(2)}, u32[]{:S(2)}) collective-permute-start(bf16[24,8192]{1,0:T(8,128)(2,1)} %get-tuple-element.65), channel_id=1, source_target_pairs={{0,8},{2,10},{4,12},{6,14},{8,0},{10,2},{12,4},{14,6},{16,24},{18,... | collective-permute-start | bytes 1179656 | tf_op jit(solution)/shard_map/ppermute | solution.py:46
  62.7 52.1 %collective-permute-start.4 = (bf16[24,8192]{1,0:T(8,128)(2,1)}, bf16[24,8192]{1,0:T(8,128)(2,1)}, u32[]{:S(2)}, u32[]{:S(2)}) collective-permute-start(bf16[24,8192]{1,0:T(8,128)(2,1)} %get-tuple-element.66), channel_id=1, source_target_pairs={{0,2},{2,4},{4,6},{6,8},{8,10},{10,12},{12,14},{14,0},{16,18},{18,... | collective-permute-start | bytes 1179656 | tf_op jit(solution)/shard_map/ppermute | solution.py:46
  63.6 51.2 %collective-permute-start.5 = (bf16[24,8192]{1,0:T(8,128)(2,1)}, bf16[24,8192]{1,0:T(8,128)(2,1)}, u32[]{:S(2)}, u32[]{:S(2)}) collective-permute-start(bf16[24,8192]{1,0:T(8,128)(2,1)} %get-tuple-element.67), channel_id=1, source_target_pairs={{0,14},{2,0},{4,2},{6,4},{8,6},{10,8},{12,10},{14,12},{16,30},{18,... | collective-permute-start | bytes 1179656 | tf_op jit(solution)/shard_map/ppermute | solution.py:46
  66.0 44.0 %collective-permute-start = (bf16[384,128]{1,0:T(8,128)(2,1)S(1)}, bf16[384,128]{1,0:T(8,128)(2,1)S(1)}, u32[]{:S(2)}, u32[]{:S(2)}) collective-permute-start(bf16[384,128]{1,0:T(8,128)(2,1)S(1)} %fusion.6), channel_id=1, source_target_pairs={{0,224},{32,0},{64,32},{96,64},{128,96},{160,128},{192,160},{224,1... | collective-permute-start | bytes 294920 | tf_op jit(solution)/shard_map/ppermute | solution.py:24
  87.2 1.1 copy-start.4
  100.2 1.9 copy-start.5
  102.1 1.9 copy-start.7
  104.0 61.1 %copy-start.6 = (bf16[1,1,2048,768]{3,2,1,0:T(8,128)(2,1)S(1)}, bf16[1,1,2048,768]{3,2,1,0:T(8,128)(2,1)}, u32[]{:S(2)}) copy-start(bf16[1,1,2048,768]{3,2,1,0:T(8,128)(2,1)} %param.11) | copy-start | bytes 9437188
  110.0 36.3 %copy-start.9 = (bf16[24,8192]{1,0:T(8,128)(2,1)}, bf16[24,8192]{1,0:T(8,128)(2,1)S(1)}, u32[]{:S(2)}) copy-start(bf16[24,8192]{1,0:T(8,128)(2,1)S(1)} %collective-permute-done.3.refs_1_) | copy-start | bytes 1179652
  114.8 20.0 %collective-permute-start.6 = (bf16[24,16384]{1,0:T(8,128)(2,1)S(1)}, bf16[24,16384]{1,0:T(8,128)(2,1)S(1)}, u32[]{:S(2)}, u32[]{:S(2)}) collective-permute-start(bf16[24,16384]{1,0:T(8,128)(2,1)S(1)} %get-tuple-element.69), channel_id=1, source_target_pairs={{0,16},{2,18},{4,20},{6,22},{8,24},{10,26},{12,28},{14,30},{16,0},... | collective-permute-start | bytes 2359304 | tf_op jit(solution)/shard_map/ppermute | solution.py:24
  115.3 31.0 %collective-permute-start.7 = (bf16[24,8192]{1,0:T(8,128)(2,1)S(1)}, bf16[24,8192]{1,0:T(8,128)(2,1)S(1)}, u32[]{:S(2)}, u32[]{:S(2)}) collective-permute-start(bf16[24,8192]{1,0:T(8,128)(2,1)S(1)} %get-tuple-element.75), channel_id=1, source_target_pairs={{0,4},{2,6},{4,8},{6,10},{8,12},{10,14},{12,0},{14,2},{16,20},{18,... | collective-permute-start | bytes 1179656 | tf_op jit(solution)/shard_map/ppermute | solution.py:46
  118.9 27.5 %collective-permute-start.8 = (bf16[24,8192]{1,0:T(8,128)(2,1)S(1)}, bf16[24,8192]{1,0:T(8,128)(2,1)S(1)}, u32[]{:S(2)}, u32[]{:S(2)}) collective-permute-start(bf16[24,8192]{1,0:T(8,128)(2,1)S(1)} %get-tuple-element.76), channel_id=1, source_target_pairs={{0,12},{2,14},{4,0},{6,2},{8,4},{10,6},{12,8},{14,10},{16,28},{18,... | collective-permute-start | bytes 1179656 | tf_op jit(solution)/shard_map/ppermute | solution.py:46
  121.7 39.4 %collective-permute-start.9 = (bf16[24,8192]{1,0:T(8,128)(2,1)S(1)}, bf16[24,8192]{1,0:T(8,128)(2,1)S(1)}, u32[]{:S(2)}, u32[]{:S(2)}) collective-permute-start(bf16[24,8192]{1,0:T(8,128)(2,1)S(1)} %get-tuple-element.77), channel_id=1, source_target_pairs={{0,6},{2,8},{4,10},{6,12},{8,14},{10,0},{12,2},{14,4},{16,22},{18,... | collective-permute-start | bytes 1179656 | tf_op jit(solution)/shard_map/ppermute | solution.py:46
  125.1 40.0 %collective-permute-start.10 = (bf16[24,8192]{1,0:T(8,128)(2,1)S(1)}, bf16[24,8192]{1,0:T(8,128)(2,1)S(1)}, u32[]{:S(2)}, u32[]{:S(2)}) collective-permute-start(bf16[24,8192]{1,0:T(8,128)(2,1)S(1)} %get-tuple-element.78), channel_id=1, source_target_pairs={{0,10},{2,12},{4,14},{6,0},{8,2},{10,4},{12,6},{14,8},{16,26},{18,... | collective-permute-start | bytes 1179656 | tf_op jit(solution)/shard_map/ppermute | solution.py:46
  137.7 41.0 %collective-permute-start.11 = (bf16[24,4096]{1,0:T(8,128)(2,1)S(1)}, bf16[24,4096]{1,0:T(8,128)(2,1)S(1)}, u32[]{:S(2)}, u32[]{:S(2)}) collective-permute-start(bf16[24,4096]{1,0:T(8,128)(2,1)S(1)} %get-tuple-element.88), channel_id=1, source_target_pairs={{0,14},{2,0},{4,2},{6,4},{8,6},{10,8},{12,10},{14,12},{16,30},{18,... | collective-permute-start | bytes 589832 | tf_op jit(solution)/shard_map/ppermute | solution.py:46
  146.3 32.4 %collective-permute-start.12 = (bf16[24,4096]{1,0:T(8,128)(2,1)S(1)}, bf16[24,4096]{1,0:T(8,128)(2,1)S(1)}, u32[]{:S(2)}, u32[]{:S(2)}) collective-permute-start(bf16[24,4096]{1,0:T(8,128)(2,1)S(1)} %get-tuple-element.89), channel_id=1, source_target_pairs={{0,2},{2,4},{4,6},{6,8},{8,10},{10,12},{12,14},{14,0},{16,18},{18,... | collective-permute-start | bytes 589832 | tf_op jit(solution)/shard_map/ppermute | solution.py:46
  146.4 32.4 %collective-permute-start.13 = (bf16[24,4096]{1,0:T(8,128)(2,1)S(1)}, bf16[24,4096]{1,0:T(8,128)(2,1)S(1)}, u32[]{:S(2)}, u32[]{:S(2)}) collective-permute-start(bf16[24,4096]{1,0:T(8,128)(2,1)S(1)} %get-tuple-element.90), channel_id=1, source_target_pairs={{0,12},{2,14},{4,0},{6,2},{8,4},{10,6},{12,8},{14,10},{16,28},{18,... | collective-permute-start | bytes 589832 | tf_op jit(solution)/shard_map/ppermute | solution.py:46
  161.1 17.7 %collective-permute-start.14 = (bf16[24,4096]{1,0:T(8,128)(2,1)S(1)}, bf16[24,4096]{1,0:T(8,128)(2,1)S(1)}, u32[]{:S(2)}, u32[]{:S(2)}) collective-permute-start(bf16[24,4096]{1,0:T(8,128)(2,1)S(1)} %get-tuple-element.91), channel_id=1, source_target_pairs={{0,4},{2,6},{4,8},{6,10},{8,12},{10,14},{12,0},{14,2},{16,20},{18,... | collective-permute-start | bytes 589832 | tf_op jit(solution)/shard_map/ppermute | solution.py:46
  165.1 1.9 copy-start.8
  167.0 1.0 copy-start.10
  178.8 25.3 %collective-permute-start.15 = (bf16[24,16384]{1,0:T(8,128)(2,1)S(1)}, bf16[24,16384]{1,0:T(8,128)(2,1)S(1)}, u32[]{:S(2)}, u32[]{:S(2)}) collective-permute-start(bf16[24,16384]{1,0:T(8,128)(2,1)S(1)} %get-tuple-element.93), channel_id=1, source_target_pairs={{0,16},{2,18},{4,20},{6,22},{8,24},{10,26},{12,28},{14,30},{16,0},... | collective-permute-start | bytes 2359304 | tf_op jit(solution)/shard_map/ppermute | solution.py:24
  182.9 19.0 %collective-permute-start.16 = (bf16[24,4096]{1,0:T(8,128)(2,1)S(1)}, bf16[24,4096]{1,0:T(8,128)(2,1)S(1)}, u32[]{:S(2)}, u32[]{:S(2)}) collective-permute-start(bf16[24,4096]{1,0:T(8,128)(2,1)S(1)} %get-tuple-element.94), channel_id=1, source_target_pairs={{0,8},{2,10},{4,12},{6,14},{8,0},{10,2},{12,4},{14,6},{16,24},{18,... | collective-permute-start | bytes 589832 | tf_op jit(solution)/shard_map/ppermute | solution.py:46
  187.0 16.4 %collective-permute-start.17 = (bf16[24,4096]{1,0:T(8,128)(2,1)S(1)}, bf16[24,4096]{1,0:T(8,128)(2,1)S(1)}, u32[]{:S(2)}, u32[]{:S(2)}) collective-permute-start(bf16[24,4096]{1,0:T(8,128)(2,1)S(1)} %get-tuple-element.95), channel_id=1, source_target_pairs={{0,10},{2,12},{4,14},{6,0},{8,2},{10,4},{12,6},{14,8},{16,26},{18,... | collective-permute-start | bytes 589832 | tf_op jit(solution)/shard_map/ppermute | solution.py:46
  189.5 14.6 %collective-permute-start.18 = (bf16[24,4096]{1,0:T(8,128)(2,1)S(1)}, bf16[24,4096]{1,0:T(8,128)(2,1)S(1)}, u32[]{:S(2)}, u32[]{:S(2)}) collective-permute-start(bf16[24,4096]{1,0:T(8,128)(2,1)S(1)} %get-tuple-element.96), channel_id=1, source_target_pairs={{0,6},{2,8},{4,10},{6,12},{8,14},{10,0},{12,2},{14,4},{16,22},{18,... | collective-permute-start | bytes 589832 | tf_op jit(solution)/shard_map/ppermute | solution.py:46
  204.1 37.3 %collective-permute-start.28 = (f32[768,2048]{1,0:T(8,128)}, f32[768,2048]{1,0:T(8,128)}, u32[]{:S(2)}, u32[]{:S(2)}) collective-permute-start(f32[768,2048]{1,0:T(8,128)} %shard_map.96), channel_id=1, source_target_pairs={{0,1},{1,0},{2,3},{3,2},{4,5},{5,4},{6,7},{7,6},{8,9},{9,8},{10,11... | collective-permute-start | bytes 18874376 | tf_op jit(solution)/shard_map/ppermute | solution.py:24
  207.9 11.8 %collective-permute-start.20 = (bf16[24,4096]{1,0:T(8,128)(2,1)S(1)}, bf16[24,4096]{1,0:T(8,128)(2,1)S(1)}, u32[]{:S(2)}, u32[]{:S(2)}) collective-permute-start(bf16[24,4096]{1,0:T(8,128)(2,1)S(1)} %get-tuple-element.107), channel_id=1, source_target_pairs={{0,224},{2,226},{4,228},{6,230},{8,232},{10,234},{12,236},{14,238}... | collective-permute-start | bytes 589832 | tf_op jit(solution)/shard_map/ppermute | solution.py:39
  209.6 13.8 %collective-permute-start.21 = (bf16[24,4096]{1,0:T(8,128)(2,1)S(1)}, bf16[24,4096]{1,0:T(8,128)(2,1)S(1)}, u32[]{:S(2)}, u32[]{:S(2)}) collective-permute-start(bf16[24,4096]{1,0:T(8,128)(2,1)S(1)} %get-tuple-element.108), channel_id=1, source_target_pairs={{0,232},{2,234},{4,236},{6,238},{8,224},{10,226},{12,228},{14,230}... | collective-permute-start | bytes 589832 | tf_op jit(solution)/shard_map/ppermute | solution.py:39
  215.5 21.3 %collective-permute-start.22 = (bf16[24,4096]{1,0:T(8,128)(2,1)S(1)}, bf16[24,4096]{1,0:T(8,128)(2,1)S(1)}, u32[]{:S(2)}, u32[]{:S(2)}) collective-permute-start(bf16[24,4096]{1,0:T(8,128)(2,1)S(1)} %get-tuple-element.109), channel_id=1, source_target_pairs={{0,238},{2,224},{4,226},{6,228},{8,230},{10,232},{12,234},{14,236}... | collective-permute-start | bytes 589832 | tf_op jit(solution)/shard_map/ppermute | solution.py:39
  218.0 18.9 %collective-permute-start.23 = (bf16[24,4096]{1,0:T(8,128)(2,1)S(1)}, bf16[24,4096]{1,0:T(8,128)(2,1)S(1)}, u32[]{:S(2)}, u32[]{:S(2)}) collective-permute-start(bf16[24,4096]{1,0:T(8,128)(2,1)S(1)} %get-tuple-element.110), channel_id=1, source_target_pairs={{0,226},{2,228},{4,230},{6,232},{8,234},{10,236},{12,238},{14,224}... | collective-permute-start | bytes 589832 | tf_op jit(solution)/shard_map/ppermute | solution.py:39
  219.7 43.9 %collective-permute-start.19 = (bf16[128,2048]{1,0:T(8,128)(2,1)S(1)}, bf16[128,2048]{1,0:T(8,128)(2,1)S(1)}, u32[]{:S(2)}, u32[]{:S(2)}) collective-permute-start(bf16[128,2048]{1,0:T(8,128)(2,1)S(1)} %shard_map.97), channel_id=1, source_target_pairs={{0,224},{32,0},{64,32},{96,64},{128,96},{160,128},{192,160},{224,1... | collective-permute-start | bytes 1572872 | tf_op jit(solution)/shard_map/ppermute | solution.py:24
  223.4 24.6 %collective-permute-start.24 = (bf16[24,4096]{1,0:T(8,128)(2,1)S(1)}, bf16[24,4096]{1,0:T(8,128)(2,1)S(1)}, u32[]{:S(2)}, u32[]{:S(2)}) collective-permute-start(bf16[24,4096]{1,0:T(8,128)(2,1)S(1)} %get-tuple-element.111), channel_id=1, source_target_pairs={{0,236},{2,238},{4,224},{6,226},{8,228},{10,230},{12,232},{14,234}... | collective-permute-start | bytes 589832 | tf_op jit(solution)/shard_map/ppermute | solution.py:39
  236.8 16.6 %collective-permute-start.25 = (bf16[24,4096]{1,0:T(8,128)(2,1)S(1)}, bf16[24,4096]{1,0:T(8,128)(2,1)S(1)}, u32[]{:S(2)}, u32[]{:S(2)}) collective-permute-start(bf16[24,4096]{1,0:T(8,128)(2,1)S(1)} %get-tuple-element.112), channel_id=1, source_target_pairs={{0,228},{2,230},{4,232},{6,234},{8,236},{10,238},{12,224},{14,226}... | collective-permute-start | bytes 589832 | tf_op jit(solution)/shard_map/ppermute | solution.py:39
  236.8 22.6 %collective-permute-start.26 = (bf16[24,4096]{1,0:T(8,128)(2,1)S(1)}, bf16[24,4096]{1,0:T(8,128)(2,1)S(1)}, u32[]{:S(2)}, u32[]{:S(2)}) collective-permute-start(bf16[24,4096]{1,0:T(8,128)(2,1)S(1)} %get-tuple-element.113), channel_id=1, source_target_pairs={{0,234},{2,236},{4,238},{6,224},{8,226},{10,228},{12,230},{14,232}... | collective-permute-start | bytes 589832 | tf_op jit(solution)/shard_map/ppermute | solution.py:39
  241.4 22.2 %collective-permute-start.27 = (bf16[24,4096]{1,0:T(8,128)(2,1)S(1)}, bf16[24,4096]{1,0:T(8,128)(2,1)S(1)}, u32[]{:S(2)}, u32[]{:S(2)}) collective-permute-start(bf16[24,4096]{1,0:T(8,128)(2,1)S(1)} %get-tuple-element.114), channel_id=1, source_target_pairs={{0,230},{2,232},{4,234},{6,236},{8,238},{10,224},{12,226},{14,228}... | collective-permute-start | bytes 589832 | tf_op jit(solution)/shard_map/ppermute | solution.py:39
  248.0 17.1 %copy-start.2 = (bf16[768,2048]{1,0:T(8,128)(2,1)}, bf16[768,2048]{1,0:T(8,128)(2,1)S(1)}, u32[]{:S(2)}) copy-start(bf16[768,2048]{1,0:T(8,128)(2,1)S(1)} %add_convert_fusion.refs_9_) | copy-start | bytes 9437188

commit v4 on v3

--- a/solution.py
+++ b/solution.py
@@ -13,7 +13,7 @@
 AWAY = (0, 4, 1, 7, 2, 6, 3, 5)
 EARLY = 4
 MEANWHILE = (2, 3, 4, 5)
-LAST = (2, 3, 0, 4, 5, 1, 6, 7)
+LAST = (6, 7, 4, 5, 0, 1, 2, 3)
 BF16 = jnp.bfloat16
 MIB = 1024 * 1024
 
@@ -117,6 +117,91 @@
         ),
         compiler_params=pltpu.CompilerParams(vmem_limit_bytes=24 * MIB),
     )(slots, inputs, upstream)
+
+
+def route_and_take(routes, gate_weights, inputs, upstream, micro, groups, local_count):
+    tokens, width = inputs.shape[2:]
+    top = routes.shape[3]
+    rows = groups * CAP
+    piece = 512
+    tile = width // 2
+    tiles = width // tile
+
+    def kernel(routes_ref, gate_ref, inputs_ref, upstream_ref, out_ref, slots_ref):
+        @pl.when(pl.program_id(0) == 0)
+        def _():
+            experts = routes_ref[0, 0].astype(jnp.float32)
+            gates = gate_ref[0, 0].astype(jnp.float32)
+            targets = lax.broadcasted_iota(jnp.int32, (groups, tokens), 0) * local_count
+            targets = targets.astype(jnp.float32)
+            routed = jnp.zeros((groups, tokens), jnp.float32)
+            weight = jnp.zeros((groups, tokens), jnp.float32)
+            for k in range(top):
+                match = experts[k : k + 1] == targets
+                routed = jnp.where(match, 1.0, routed)
+                weight = weight + jnp.where(match, gates[k : k + 1], 0.0)
+            upto = jnp.where(
+                lax.broadcasted_iota(jnp.int32, (tokens, tokens), 0)
+                <= lax.broadcasted_iota(jnp.int32, (tokens, tokens), 1),
+                1.0,
+                0.0,
+            ).astype(BF16)
+            rank = jnp.dot(routed.astype(BF16), upto, preferred_element_type=jnp.float32)
+            slot = jnp.where(routed > 0.5, rank, 0.0)
+            ids = lax.broadcasted_iota(jnp.int32, (CAP, tokens), 0).astype(jnp.float32) + 1.0
+            for n in range(0, groups, 2):
+                chosen = [slot[n + k : n + k + 1] == ids for k in range(2)]
+                ones = [jnp.where(pick, 1.0, 0.0) for pick in chosen]
+                gated = [
+                    jnp.where(pick, weight[n + k : n + k + 1], 0.0) for k, pick in enumerate(chosen)
+                ]
+                at = slice(n * CAP, (n + 2) * CAP)
+                slots_ref[0, at, :] = jnp.concatenate(ones, axis=0).astype(BF16)
+                slots_ref[1, at, :] = jnp.concatenate(gated, axis=0).astype(BF16)
+
+        def take(which, rows_ref):
+            for start in range(0, tile, piece):
+                taken = jnp.dot(
+                    slots_ref[which],
+                    rows_ref[0, 0, :, start : start + piece],
+                    preferred_element_type=jnp.float32,
+                )
+                for n in range(groups):
+                    block = taken[n * CAP : (n + 1) * CAP].astype(BF16)
+                    out_ref[n, :, start : start + piece] = block
+
+        @pl.when(pl.program_id(0) < tiles)
+        def _():
+            take(0, inputs_ref)
+
+        @pl.when(pl.program_id(0) >= tiles)
+        def _():
+            take(1, upstream_ref)
+
+    return pl.pallas_call(
+        kernel,
+        grid=(2 * tiles,),
+        in_specs=[
+            pl.BlockSpec((1, 1, top, tokens), lambda i: (0, micro, 0, 0)),
+            pl.BlockSpec((1, 1, top, tokens), lambda i: (0, micro, 0, 0)),
+            pl.BlockSpec((1, 1, tokens, tile), lambda i: (0, micro, 0, jnp.minimum(i, tiles - 1))),
+            pl.BlockSpec((1, 1, tokens, tile), lambda i: (0, micro, 0, jnp.maximum(i - tiles, 0))),
+        ],
+        out_specs=pl.BlockSpec((groups, CAP, tile), lambda i: (0, 0, i)),
+        out_shape=pltpu.HBM((groups, CAP, 2 * width), BF16),
+        scratch_shapes=[pltpu.VMEM((2, rows, tokens), BF16)],
+        cost_estimate=pl.CostEstimate(
+            flops=4 * rows * tokens * width,
+            bytes_accessed=4 * width * (rows + tokens),
+            transcendentals=0,
+        ),
+        compiler_params=pltpu.CompilerParams(vmem_limit_bytes=24 * MIB),
+    )(
+        jnp.swapaxes(routes, 2, 3),
+        jnp.swapaxes(gate_weights, 2, 3),
+        pltpu.with_memory_space_constraint(inputs, pltpu.HBM),
+        pltpu.with_memory_space_constraint(upstream, pltpu.HBM),
+    )
 
 
 def pack(arrays, moves, out_widths, after=()):
@@ -341,8 +426,10 @@
     place = (jnp.array(AWAY * COLUMNS, jnp.int32) + me) % ring
     near = (order // ring + me // ring) % COLUMNS * ring + place
 
-    slots_0 = build_slots(routes[0, 0], gate_weights[0, 0], order * local_count)
-    first = swap_groups(take_rows(slots_0, inputs, upstream, 0, False))
+    first = swap_groups(
+        route_and_take(routes, gate_weights, inputs, upstream, 0, groups, local_count)
+    )
+    placing = build_slots(routes[0, 0], gate_weights[0, 0], near * local_count)[0]
 
     slots_1 = build_slots(routes[0, 1], gate_weights[0, 1], near * local_count)
     behind = from_behind(slots_1[0], "pipe", -1)
@@ -364,8 +451,8 @@
     blocks = send_pack(0, EARLY)
     second = {i: along_ring(blocks[i], AWAY[i]) for i in range(1, EARLY)}
     own_0, away_0, hidden_0, scaled_0 = expert_rows(first, me, weight_in, weight_out)
-    held = (own_0, away_0, behind, send_pack(EARLY, ring))
-    (own_0, away_0, behind, late), second = together(held, second, range(1, EARLY))
+    held = (own_0, away_0, behind, placing, slots_1[0], send_pack(EARLY, ring))
+    (own_0, away_0, behind, placing, _, late), second = together(held, second, range(1, EARLY))
     blocks += late
     second[0] = blocks[0]
     second.update({i: along_ring(blocks[i], AWAY[i]) for i in range(EARLY, ring)})
@@ -377,18 +464,17 @@
     )
     back_0 = {i: along_ring(back[i], -AWAY[i]) for i in MEANWHILE}
     partial_value = weight_grad([hidden_0, hidden_1], [scaled_0, scaled_1], [])
-    held = (own_1, away_1, partial_value, [back[i] for i in rest])
-    (own_1, away_1, partial_value, held), back_0 = together(held, back_0, MEANWHILE)
+    held = (own_1, away_1, [back[i] for i in rest])
+    (own_1, away_1, held), back_0 = together(held, back_0, MEANWHILE)
     back_0.update({i: along_ring(held[n], -AWAY[i]) for n, i in enumerate(rest)})
     back_0[0] = back[0]
     held = (partial_value, swap_columns(away_1))
     (partial_value, away_1), back_0 = together(held, back_0, rest)
-    back = pair_up(own_1, away_1, ring)
+    back, partial_value = lax.optimization_barrier((pair_up(own_1, away_1, ring), partial_value))
     proj_grad = (partial_value + from_behind(partial_value, "dp", 1)).astype(BF16)
     back_1 = [along_ring_behind(back[i], -AWAY[i]) for i in LAST]
     back_1 = [back_1[LAST.index(i)] for i in range(ring)]
 
-    placing = jnp.take(slots_0[0].reshape(groups, CAP, -1), near, axis=0).reshape(groups * CAP, -1)
     grad_0 = from_behind(combine(placing, [back_0[i] for i in range(ring)]), "pipe", -1)
     grad_1 = combine(behind, back_1, [grad_0, proj_grad])
     return (jnp.stack([grad_0, grad_1])[None], proj_grad[None, None])

time: 267 us -> 265 us (level)
  waiting for transfers between devices: 127 us -> 122 us
  starting transfers between devices: 81 us -> 84.4 us
  other arithmetic: 9.42 us -> 6.42 us
    ppermute x8, starting transfers between devices: 21.4 us -> 26.9 us  [along_ring_behind(): return lax.ppermute(value, ('pipe', 'expert'), pairs)]
    pallas_call x0 -> x1, Pallas kernels: none -> 4.6 us  [route_and_take(): pl.pallas_call(kernel, grid=(2 * tiles,), in_specs=[pl.BlockSpec((1, 1, t...]
    ppermute x8, waiting for transfers between devices: 25.6 us -> 22.2 us  [along_ring_behind(): return lax.ppermute(value, ('pipe', 'expert'), pairs)]
    pallas_call x5 -> x4, Pallas kernels: 8.18 us -> 5.22 us  [take_rows(): pl.pallas_call(kernel, grid=(2 * tiles,), in_specs=[pl.BlockSpec((1, rows...]
    unnamed x22 -> x44, local copies, waits for them, and re-layouts: 8.95 us -> 10.5 us
  transfers between devices with their start and end apart: 30 -> 30, of which waited for: 16 -> 16; matrix products, arithmetic and copies ran while one was open for 3% -> 2% of each run, Pallas kernels for 12% -> 11%
where the time goes in v4:
time: 265 us; the launch traced here: 262 us
  waiting for transfers between devices  122 us (46%)
  starting transfers between devices  84.4 us (32%)
  Pallas kernels  36.5 us (14%)
  local copies, waits for them, and re-layouts  10.9 us (4%)
  other arithmetic  6.42 us (2%)
    ppermute x7, waiting for transfers between devices, from_behind(): return lax.ppermute(value, axis, pairs)  55.2 us
    ppermute x14, waiting for transfers between devices, along_ring(): return lax.ppermute(value, 'expert', pairs)  36.9 us
    ppermute x14, starting transfers between devices, along_ring(): return lax.ppermute(value, 'expert', pairs)  35.9 us
    ppermute x8, starting transfers between devices, along_ring_behind(): return lax.ppermute(value, ('pipe', 'expert'), pairs)  26.9 us
    ppermute x8, waiting for transfers between devices, along_ring_behind(): return lax.ppermute(value, ('pipe', 'expert'), pairs)  22.2 us
    all_to_all x1, starting transfers between devices, swap_groups(): lax.all_to_all(value, 'expert', split_axis=0, concat_axis=0, tiled=True)  11.6 us
    pallas_call x2, Pallas kernels, expert_rows(): pl.pallas_call(kernel, in_specs=[pl.BlockSpec(memory_space=pltpu.VMEM)] *...  11.2 us
    unnamed x44, local copies, waits for them, and re-layouts  10.5 us
  transfers between devices with their start and end apart: 30, of which 16 were waited for; matrix products, arithmetic and copies ran while one was open for 2% of the time, Pallas kernels for 11%

profile of v4, /device:TPU:14, one launch (start us, length us, event | category | flops | bytes accessed | tf_op | source)
XLA Modules:
  0.0 261.6 jit_solution(9286216321986838397)
XLA Ops:
  0.6 0.7 copy-done.5
  1.3 0.7 copy-done.7
  2.0 4.6 %shard_map.86 = bf16[16,24,4096]{2,1,0:T(8,128)(2,1)} custom-call(s32[1,2,8,128]{3,2,1,0:T(8,128)S(1)} %bitcast.66, bf16[1,2,8,128]{3,2,1,0:T(8,128)(2,1)S(1)} %bitcast.67, bf16[1,2,128,2048]{3,2,1,0:T(8,128)(2,1)} %inputs_ref.9, bf16[1,2,128,2048]{3,2,1,0:T(8,128)(2,1)} %upstream_ref.9), custom_call_target="tpu_custom_call" | custom-call | flops 402653184 | bytes 4194304 | tf_op jit(solution)/shard_map/pallas_call | solution.py:181
  6.6 11.6 %all-to-all-start = ((bf16[16,24,4096]{2,1,0:T(8,128)(2,1)}), bf16[16,24,4096]{2,1,0:T(8,128)(2,1)}, u32[]{:S(2)}, u32[]{:S(2)}) async-start(bf16[16,24,4096]{2,1,0:T(8,128)(2,1)} %shard_map.86), calls=%async_computation | async-start | bytes 6291456 | tf_op jit(solution)/shard_map/all_to_all | solution.py:414
  19.3 1.3 shard_map.92
  20.8 1.3 shard_map.89
  22.1 3.4 %collective-permute-start.1 = (bf16[24,16384]{1,0:T(8,128)(2,1)}, bf16[24,16384]{1,0:T(8,128)(2,1)S(1)}, u32[]{:S(2)}, u32[]{:S(2)}) collective-permute-start(bf16[24,16384]{1,0:T(8,128)(2,1)} %shard_map.89), channel_id=1, source_target_pairs={{0,16},{2,18},{4,20},{6,22},{8,24},{10,26},{12,28},{14,30},{16,0},... | collective-permute-start | bytes 2359304 | tf_op jit(solution)/shard_map/ppermute | solution.py:24
  25.8 1.3 shard_map.91.refs_0_
  27.1 31.3 %collective-permute-done.2.refs_1_ = bf16[24,16384]{1,0:T(8,128)(2,1)} collective-permute-done((bf16[24,16384]{1,0:T(8,128)(2,1)}, bf16[24,16384]{1,0:T(8,128)(2,1)}, u32[]{:S(2)}, u32[]{:S(2)}) %collective-permute-start.2) | collective-permute-done | bytes 786464 | tf_op jit(solution)/shard_map/ppermute | solution.py:24
  58.3 1.1 copy-done.3
  59.5 2.4 shard_map.93
  62.4 0.8 collective-permute-start.4
  63.2 2.5 collective-permute-start.5
  65.7 0.8 fusion.4
  66.5 0.8 collective-permute-start
  67.3 1.3 shard_map.88.refs_0_
  68.6 16.9 %collective-permute-done.1.refs_1_ = bf16[24,16384]{1,0:T(8,128)(2,1)S(1)} collective-permute-done((bf16[24,16384]{1,0:T(8,128)(2,1)}, bf16[24,16384]{1,0:T(8,128)(2,1)S(1)}, u32[]{:S(2)}, u32[]{:S(2)}) %collective-permute-start.1) | collective-permute-done | bytes 786464 | tf_op jit(solution)/shard_map/ppermute | solution.py:24
  85.5 1.1 copy-done.4
  86.7 1.6 shard_map.90
  88.3 0.7 copy-done.13
  89.0 0.7 copy-done.15
  89.8 0.8 copy-done.17
  90.6 0.7 copy-done.19
  91.3 8.2 %all-to-all-done.refs_0_ = bf16[16,24,4096]{2,1,0:T(8,128)(2,1)} async-done(((bf16[16,24,4096]{2,1,0:T(8,128)(2,1)}), bf16[16,24,4096]{2,1,0:T(8,128)(2,1)}, u32[]{:S(2)}, u32[]{:S(2)}) %all-to-all-start) | async-done | bytes 3145760 | tf_op jit(solution)/shard_map/all_to_all | solution.py:414
  99.5 1.9 copy-done.9
  101.4 1.9 copy-done.11
  103.3 6.0 %shard_map.87 = (bf16[24,16384]{1,0:T(8,128)(2,1)S(1)}, bf16[24,16384]{1,0:T(8,128)(2,1)S(1)}, bf16[384,768]{1,0:T(8,128)(2,1)S(1)}, bf16[384,2048]{1,0:T(8,128)(2,1)S(1)}) custom-call(bf16[16,24,4096]{2,1,0:T(8,128)(2,1)} %all-to-all-done.refs_0_, bf16[2048,768]{1,0:T(8,128)(2,1)S(1)} %bitcast.68, bf16[768,2048]{1,0:T(8,128)(2,1)S(1)} %bitcast.70, ...), custom_call_target="tpu_custom_call" | custom-call | flops 3623878656 | bytes 12582912 | tf_op jit(solution)/shard_map/pallas_call | solution.py:320
  109.3 4.8 %collective-permute-done.4.refs_2_ = bf16[24,8192]{1,0:T(8,128)(2,1)} collective-permute-done((bf16[24,8192]{1,0:T(8,128)(2,1)}, bf16[24,8192]{1,0:T(8,128)(2,1)}, u32[]{:S(2)}, u32[]{:S(2)}) %collective-permute-start.4) | collective-permute-done | bytes 393248 | tf_op jit(solution)/shard_map/ppermute | solution.py:46
  114.7 3.5 %collective-permute-start.7 = (bf16[24,8192]{1,0:T(8,128)(2,1)S(1)}, bf16[24,8192]{1,0:T(8,128)(2,1)S(1)}, u32[]{:S(2)}, u32[]{:S(2)}) collective-permute-start(bf16[24,8192]{1,0:T(8,128)(2,1)S(1)} %copy-done.20), channel_id=1, source_target_pairs={{0,4},{2,6},{4,8},{6,10},{8,12},{10,14},{12,0},{14,2},{16,20},{18,... | collective-permute-start | bytes 1179656 | tf_op jit(solution)/shard_map/ppermute | solution.py:46
  118.2 2.8 %collective-permute-start.8 = (bf16[24,8192]{1,0:T(8,128)(2,1)S(1)}, bf16[24,8192]{1,0:T(8,128)(2,1)S(1)}, u32[]{:S(2)}, u32[]{:S(2)}) collective-permute-start(bf16[24,8192]{1,0:T(8,128)(2,1)S(1)} %copy-done.18), channel_id=1, source_target_pairs={{0,12},{2,14},{4,0},{6,2},{8,4},{10,6},{12,8},{14,10},{16,28},{18,... | collective-permute-start | bytes 1179656 | tf_op jit(solution)/shard_map/ppermute | solution.py:46
  121.0 3.4 %collective-permute-start.9 = (bf16[24,8192]{1,0:T(8,128)(2,1)S(1)}, bf16[24,8192]{1,0:T(8,128)(2,1)S(1)}, u32[]{:S(2)}, u32[]{:S(2)}) collective-permute-start(bf16[24,8192]{1,0:T(8,128)(2,1)S(1)} %copy-done.16), channel_id=1, source_target_pairs={{0,6},{2,8},{4,10},{6,12},{8,14},{10,0},{12,2},{14,4},{16,22},{18,... | collective-permute-start | bytes 1179656 | tf_op jit(solution)/shard_map/ppermute | solution.py:46
  124.5 2.6 %collective-permute-start.10 = (bf16[24,8192]{1,0:T(8,128)(2,1)S(1)}, bf16[24,8192]{1,0:T(8,128)(2,1)S(1)}, u32[]{:S(2)}, u32[]{:S(2)}) collective-permute-start(bf16[24,8192]{1,0:T(8,128)(2,1)S(1)} %copy-done.14), channel_id=1, source_target_pairs={{0,10},{2,12},{4,14},{6,0},{8,2},{10,4},{12,6},{14,8},{16,26},{18,... | collective-permute-start | bytes 1179656 | tf_op jit(solution)/shard_map/ppermute | solution.py:46
  127.1 7.0 %collective-permute-done.6.refs_1_ = bf16[24,16384]{1,0:T(8,128)(2,1)S(1)} collective-permute-done((bf16[24,16384]{1,0:T(8,128)(2,1)S(1)}, bf16[24,16384]{1,0:T(8,128)(2,1)S(1)}, u32[]{:S(2)}, u32[]{:S(2)}) %collective-permute-start.6) | collective-permute-done | bytes 786464 | tf_op jit(solution)/shard_map/ppermute | solution.py:24
  134.2 2.9 %shard_map.94 = (bf16[24,4096]{1,0:T(8,128)(2,1)S(1)}, bf16[24,4096]{1,0:T(8,128)(2,1)S(1)}, bf16[24,4096]{1,0:T(8,128)(2,1)S(1)}, bf16[24,4096]{1,0:T(8,128)(2,...) custom-call(bf16[24,16384]{1,0:T(8,128)(2,1)S(1)} %get-tuple-element, ...), custom_call_target="tpu_custom_call" | custom-call | bytes 3145728 | tf_op jit(solution)/shard_map/pallas_call | solution.py:236
  137.1 2.7 %collective-permute-start.11 = (bf16[24,4096]{1,0:T(8,128)(2,1)S(1)}, bf16[24,4096]{1,0:T(8,128)(2,1)S(1)}, u32[]{:S(2)}, u32[]{:S(2)}) collective-permute-start(bf16[24,4096]{1,0:T(8,128)(2,1)S(1)} %get-tuple-element.98), channel_id=1, source_target_pairs={{0,14},{2,0},{4,2},{6,4},{8,6},{10,8},{12,10},{14,12},{16,30},{18,... | collective-permute-start | bytes 589832 | tf_op jit(solution)/shard_map/ppermute | solution.py:46
  139.8 6.1 %collective-permute-done.7.refs_4_ = bf16[24,8192]{1,0:T(8,128)(2,1)S(1)} collective-permute-done((bf16[24,8192]{1,0:T(8,128)(2,1)S(1)}, bf16[24,8192]{1,0:T(8,128)(2,1)S(1)}, u32[]{:S(2)}, u32[]{:S(2)}) %collective-permute-start.7) | collective-permute-done | bytes 393248 | tf_op jit(solution)/shard_map/ppermute | solution.py:46
  145.9 5.0 %collective-permute-start.13 = (bf16[24,4096]{1,0:T(8,128)(2,1)S(1)}, bf16[24,4096]{1,0:T(8,128)(2,1)S(1)}, u32[]{:S(2)}, u32[]{:S(2)}) collective-permute-start(bf16[24,4096]{1,0:T(8,128)(2,1)S(1)} %get-tuple-element.100), channel_id=1, source_target_pairs={{0,12},{2,14},{4,0},{6,2},{8,4},{10,6},{12,8},{14,10},{16,28},{18,... | collective-permute-start | bytes 589832 | tf_op jit(solution)/shard_map/ppermute | solution.py:46
  150.9 9.7 %collective-permute-done.9.refs_6_ = bf16[24,8192]{1,0:T(8,128)(2,1)S(1)} collective-permute-done((bf16[24,8192]{1,0:T(8,128)(2,1)S(1)}, bf16[24,8192]{1,0:T(8,128)(2,1)S(1)}, u32[]{:S(2)}, u32[]{:S(2)}) %collective-permute-start.9) | collective-permute-done | bytes 393248 | tf_op jit(solution)/shard_map/ppermute | solution.py:46
  160.6 3.2 %collective-permute-start.14 = (bf16[24,4096]{1,0:T(8,128)(2,1)S(1)}, bf16[24,4096]{1,0:T(8,128)(2,1)S(1)}, u32[]{:S(2)}, u32[]{:S(2)}) collective-permute-start(bf16[24,4096]{1,0:T(8,128)(2,1)S(1)} %get-tuple-element.101), channel_id=1, source_target_pairs={{0,4},{2,6},{4,8},{6,10},{8,12},{10,14},{12,0},{14,2},{16,20},{18,... | collective-permute-start | bytes 589832 | tf_op jit(solution)/shard_map/ppermute | solution.py:46
  163.8 1.1 collective-permute-done.10.refs_7_
  164.9 5.2 %shard_map.95 = (bf16[24,16384]{1,0:T(8,128)(2,1)S(1)}, bf16[24,16384]{1,0:T(8,128)(2,1)S(1)}, bf16[384,768]{1,0:T(8,128)(2,1)S(1)}, bf16[384,2048]{1,0:T(8,128)(2,1)S(1)}) custom-call(bf16[24,8192]{1,0:T(8,128)(2,1)S(1)} %get-tuple-element.82.refs_0_, bf16[24,8192]{1,0:T(8,128)(2,1)} %collective-permute-done.3.refs_1_, ...), custom_call_target="tpu_custom_call" | custom-call | flops 3623878656 | bytes 12582912 | tf_op jit(solution)/shard_map/pallas_call | solution.py:320
  170.1 2.2 collective-permute-done.11.refs_2_
  172.3 0.9 collective-permute-done.13.refs_4_
  173.2 3.9 %collective-permute-start.15 = (bf16[24,16384]{1,0:T(8,128)(2,1)S(1)}, bf16[24,16384]{1,0:T(8,128)(2,1)S(1)}, u32[]{:S(2)}, u32[]{:S(2)}) collective-permute-start(bf16[24,16384]{1,0:T(8,128)(2,1)S(1)} %get-tuple-element.102), channel_id=1, source_target_pairs={{0,16},{2,18},{4,20},{6,22},{8,24},{10,26},{12,28},{14,30},{16,0},... | collective-permute-start | bytes 2359304 | tf_op jit(solution)/shard_map/ppermute | solution.py:24
  177.1 5.0 %collective-permute-start.16 = (bf16[24,4096]{1,0:T(8,128)(2,1)S(1)}, bf16[24,4096]{1,0:T(8,128)(2,1)S(1)}, u32[]{:S(2)}, u32[]{:S(2)}) collective-permute-start(bf16[24,4096]{1,0:T(8,128)(2,1)S(1)} %get-tuple-element.103), channel_id=1, source_target_pairs={{0,8},{2,10},{4,12},{6,14},{8,0},{10,2},{12,4},{14,6},{16,24},{18,... | collective-permute-start | bytes 589832 | tf_op jit(solution)/shard_map/ppermute | solution.py:46
  182.1 3.2 %collective-permute-start.17 = (bf16[24,4096]{1,0:T(8,128)(2,1)S(1)}, bf16[24,4096]{1,0:T(8,128)(2,1)S(1)}, u32[]{:S(2)}, u32[]{:S(2)}) collective-permute-start(bf16[24,4096]{1,0:T(8,128)(2,1)S(1)} %get-tuple-element.104), channel_id=1, source_target_pairs={{0,10},{2,12},{4,14},{6,0},{8,2},{10,4},{12,6},{14,8},{16,26},{18,... | collective-permute-start | bytes 589832 | tf_op jit(solution)/shard_map/ppermute | solution.py:46
  185.3 0.6 collective-permute-start.18
  185.9 4.6 %shard_map.96 = f32[768,2048]{1,0:T(8,128)S(1)} custom-call(bf16[384,768]{1,0:T(8,128)(2,1)S(1)} %get-tuple-element.81.refs_0_, bf16[384,768]{1,0:T(8,128)(2,1)S(1)} %get-tuple-element.90.refs_1_, bf16[384,2048]{1,0:T(8,128)(2,1)S(1)} %get-tuple-element.91.refs_2_, bf16[384,2048]{1,0:T(8,128)(2,1)S(1)} %get-tuple-element.92.refs_3_), custom_call_target="tpu_custom_call" | custom-call | flops 2415919104 | bytes 10616832 | tf_op jit(solution)/shard_map/pallas_call | solution.py:396
  190.5 3.4 %collective-permute-done.16.refs_1_ = bf16[24,4096]{1,0:T(8,128)(2,1)S(1)} collective-permute-done((bf16[24,4096]{1,0:T(8,128)(2,1)S(1)}, bf16[24,4096]{1,0:T(8,128)(2,1)S(1)}, u32[]{:S(2)}, u32[]{:S(2)}) %collective-permute-start.16) | collective-permute-done | bytes 196640 | tf_op jit(solution)/shard_map/ppermute | solution.py:46
  193.9 8.6 %collective-permute-done.17.refs_6_ = bf16[24,4096]{1,0:T(8,128)(2,1)S(1)} collective-permute-done((bf16[24,4096]{1,0:T(8,128)(2,1)S(1)}, bf16[24,4096]{1,0:T(8,128)(2,1)S(1)}, u32[]{:S(2)}, u32[]{:S(2)}) %collective-permute-start.17) | collective-permute-done | bytes 196640 | tf_op jit(solution)/shard_map/ppermute | solution.py:46
  202.6 2.9 %shard_map.98 = (bf16[24,4096]{1,0:T(8,128)(2,1)S(1)}, bf16[24,4096]{1,0:T(8,128)(2,1)S(1)}, bf16[24,4096]{1,0:T(8,128)(2,1)S(1)}, bf16[24,4096]{1,0:T(8,128)(2,...) custom-call(bf16[24,16384]{1,0:T(8,128)(2,1)S(1)} %get-tuple-element, ...), custom_call_target="tpu_custom_call" | custom-call | bytes 3145728 | tf_op jit(solution)/shard_map/pallas_call | solution.py:236
  205.6 2.4 collective-permute-start.20
  208.0 4.4 %collective-permute-start.21 = (bf16[24,4096]{1,0:T(8,128)(2,1)S(1)}, bf16[24,4096]{1,0:T(8,128)(2,1)S(1)}, u32[]{:S(2)}, u32[]{:S(2)}) collective-permute-start(bf16[24,4096]{1,0:T(8,128)(2,1)S(1)} %get-tuple-element.126), channel_id=1, source_target_pairs={{0,232},{2,234},{4,236},{6,238},{8,224},{10,226},{12,228},{14,230}... | collective-permute-start | bytes 589832 | tf_op jit(solution)/shard_map/ppermute | solution.py:39
  212.4 1.0 collective-permute-start.22
  213.3 5.1 %collective-permute-start.23 = (bf16[24,4096]{1,0:T(8,128)(2,1)S(1)}, bf16[24,4096]{1,0:T(8,128)(2,1)S(1)}, u32[]{:S(2)}, u32[]{:S(2)}) collective-permute-start(bf16[24,4096]{1,0:T(8,128)(2,1)S(1)} %get-tuple-element.128), channel_id=1, source_target_pairs={{0,226},{2,228},{4,230},{6,232},{8,234},{10,236},{12,238},{14,224}... | collective-permute-start | bytes 589832 | tf_op jit(solution)/shard_map/ppermute | solution.py:39
  219.0 1.2 collective-permute-start.19
  220.1 6.6 %collective-permute-done.21.refs_1_ = bf16[24,4096]{1,0:T(8,128)(2,1)S(1)} collective-permute-done((bf16[24,4096]{1,0:T(8,128)(2,1)S(1)}, bf16[24,4096]{1,0:T(8,128)(2,1)S(1)}, u32[]{:S(2)}, u32[]{:S(2)}) %collective-permute-start.21) | collective-permute-done | bytes 196640 | tf_op jit(solution)/shard_map/ppermute | solution.py:39
  226.8 4.6 %collective-permute-done.22.refs_2_ = bf16[24,4096]{1,0:T(8,128)(2,1)S(1)} collective-permute-done((bf16[24,4096]{1,0:T(8,128)(2,1)S(1)}, bf16[24,4096]{1,0:T(8,128)(2,1)S(1)}, u32[]{:S(2)}, u32[]{:S(2)}) %collective-permute-start.22) | collective-permute-done | bytes 196640 | tf_op jit(solution)/shard_map/ppermute | solution.py:39
  231.4 6.4 %collective-permute-start.26 = (bf16[24,4096]{1,0:T(8,128)(2,1)S(1)}, bf16[24,4096]{1,0:T(8,128)(2,1)S(1)}, u32[]{:S(2)}, u32[]{:S(2)}) collective-permute-start(bf16[24,4096]{1,0:T(8,128)(2,1)S(1)} %get-tuple-element.131), channel_id=1, source_target_pairs={{0,234},{2,236},{4,238},{6,224},{8,226},{10,228},{12,230},{14,232}... | collective-permute-start | bytes 589832 | tf_op jit(solution)/shard_map/ppermute | solution.py:39
  237.9 7.5 %collective-permute-start.27 = (bf16[24,4096]{1,0:T(8,128)(2,1)S(1)}, bf16[24,4096]{1,0:T(8,128)(2,1)S(1)}, u32[]{:S(2)}, u32[]{:S(2)}) collective-permute-start(bf16[24,4096]{1,0:T(8,128)(2,1)S(1)} %get-tuple-element.132), channel_id=1, source_target_pairs={{0,230},{2,232},{4,234},{6,236},{8,238},{10,224},{12,226},{14,228}... | collective-permute-start | bytes 589832 | tf_op jit(solution)/shard_map/ppermute | solution.py:39
  245.3 3.7 %add_convert_fusion.refs_9_ = bf16[768,2048]{1,0:T(8,128)(2,1)S(1)} fusion(f32[768,2048]{1,0:T(8,128)S(1)} %shard_map.96, f32[768,2048]{1,0:T(8,128)} %collective-permute-done.28), kind=kLoop, calls=%fused_computation | loop fusion | flops 3145728 | bytes 15728640 | tf_op jit(solution)/shard_map/convert_element_type | solution.py:474
  249.1 4.9 %collective-permute-done.26.refs_6_ = bf16[24,4096]{1,0:T(8,128)(2,1)S(1)} collective-permute-done((bf16[24,4096]{1,0:T(8,128)(2,1)S(1)}, bf16[24,4096]{1,0:T(8,128)(2,1)S(1)}, u32[]{:S(2)}, u32[]{:S(2)}) %collective-permute-start.26) | collective-permute-done | bytes 196640 | tf_op jit(solution)/shard_map/ppermute | solution.py:39
  254.0 6.1 %collective-permute-done.27.refs_7_ = bf16[24,4096]{1,0:T(8,128)(2,1)S(1)} collective-permute-done((bf16[24,4096]{1,0:T(8,128)(2,1)S(1)}, bf16[24,4096]{1,0:T(8,128)(2,1)S(1)}, u32[]{:S(2)}, u32[]{:S(2)}) %collective-permute-start.27) | collective-permute-done | bytes 196640 | tf_op jit(solution)/shard_map/ppermute | solution.py:39
  260.6 1.1 maximum_bitcast_fusion
  (80 shorter events, 3.8 us)
Async XLA Ops:
  0.6 0.7 copy-start.5
  1.3 0.7 copy-start.7
  6.6 11.8 %copy-start.21 = (s32[16]{0:T(128)S(1)}, s32[16]{0:T(128)}, u32[]{:S(2)}) copy-start(s32[16]{0:T(128)} %constant.69.clone) | copy-start | bytes 196
  6.6 11.8 %copy-start.6 = (s32[1,2,128,8]{2,3,1,0:T(8,128)S(1)}, s32[1,2,128,8]{2,3,1,0:T(8,128)}, u32[]{:S(2)}) copy-start(s32[1,2,128,8]{2,3,1,0:T(8,128)} %param.9) | copy-start | bytes 24580
  6.6 12.2 %copy-start.8 = (bf16[1,2,128,8]{2,3,1,0:T(8,128)(2,1)S(1)}, bf16[1,2,128,8]{2,3,1,0:T(8,128)(2,1)}, u32[]{:S(2)}) copy-start(bf16[1,2,128,8]{2,3,1,0:T(8,128)(2,1)} %param.10) | copy-start | bytes 12292
  6.6 12.7 %copy-start = (bf16[1,2,128,2048]{3,2,1,0:T(8,128)(2,1)S(1)}, bf16[1,2,128,2048]{3,2,1,0:T(8,128)(2,1)}, u32[]{:S(2)}) copy-start(bf16[1,2,128,2048]{3,2,1,0:T(8,128)(2,1)} %inputs_ref.9) | copy-start | bytes 3145732
  6.6 12.7 %copy-start.1 = (bf16[1,2,128,2048]{3,2,1,0:T(8,128)(2,1)S(1)}, bf16[1,2,128,2048]{3,2,1,0:T(8,128)(2,1)}, u32[]{:S(2)}) copy-start(bf16[1,2,128,2048]{3,2,1,0:T(8,128)(2,1)} %upstream_ref.9) | copy-start | bytes 3145732
  6.6 92.8 %all-to-all-start = ((bf16[16,24,4096]{2,1,0:T(8,128)(2,1)}), bf16[16,24,4096]{2,1,0:T(8,128)(2,1)}, u32[]{:S(2)}, u32[]{:S(2)}) async-start(bf16[16,24,4096]{2,1,0:T(8,128)(2,1)} %shard_map.86), calls=%async_computation | async-start | bytes 6291456 | tf_op jit(solution)/shard_map/all_to_all | solution.py:414
  20.7 37.7 %collective-permute-start.2 = (bf16[24,16384]{1,0:T(8,128)(2,1)}, bf16[24,16384]{1,0:T(8,128)(2,1)}, u32[]{:S(2)}, u32[]{:S(2)}) collective-permute-start(bf16[24,16384]{1,0:T(8,128)(2,1)} %shard_map.92), channel_id=1, source_target_pairs={{0,16},{2,18},{4,20},{6,22},{8,24},{10,26},{12,28},{14,30},{16,0},... | collective-permute-start | bytes 2359304 | tf_op jit(solution)/shard_map/ppermute | solution.py:24
  22.1 63.4 %collective-permute-start.1 = (bf16[24,16384]{1,0:T(8,128)(2,1)}, bf16[24,16384]{1,0:T(8,128)(2,1)S(1)}, u32[]{:S(2)}, u32[]{:S(2)}) collective-permute-start(bf16[24,16384]{1,0:T(8,128)(2,1)} %shard_map.89), channel_id=1, source_target_pairs={{0,16},{2,18},{4,20},{6,22},{8,24},{10,26},{12,28},{14,30},{16,0},... | collective-permute-start | bytes 2359304 | tf_op jit(solution)/shard_map/ppermute | solution.py:24
  58.3 1.1 copy-start.3
  61.9 47.4 %collective-permute-start.3 = (bf16[24,8192]{1,0:T(8,128)(2,1)}, bf16[24,8192]{1,0:T(8,128)(2,1)}, u32[]{:S(2)}, u32[]{:S(2)}) collective-permute-start(bf16[24,8192]{1,0:T(8,128)(2,1)} %get-tuple-element.74), channel_id=1, source_target_pairs={{0,8},{2,10},{4,12},{6,14},{8,0},{10,2},{12,4},{14,6},{16,24},{18,... | collective-permute-start | bytes 1179656 | tf_op jit(solution)/shard_map/ppermute | solution.py:46
  62.4 51.7 %collective-permute-start.4 = (bf16[24,8192]{1,0:T(8,128)(2,1)}, bf16[24,8192]{1,0:T(8,128)(2,1)}, u32[]{:S(2)}, u32[]{:S(2)}) collective-permute-start(bf16[24,8192]{1,0:T(8,128)(2,1)} %get-tuple-element.75), channel_id=1, source_target_pairs={{0,2},{2,4},{4,6},{6,8},{8,10},{10,12},{12,14},{14,0},{16,18},{18,... | collective-permute-start | bytes 1179656 | tf_op jit(solution)/shard_map/ppermute | solution.py:46
  63.2 50.9 %collective-permute-start.5 = (bf16[24,8192]{1,0:T(8,128)(2,1)}, bf16[24,8192]{1,0:T(8,128)(2,1)}, u32[]{:S(2)}, u32[]{:S(2)}) collective-permute-start(bf16[24,8192]{1,0:T(8,128)(2,1)} %get-tuple-element.76), channel_id=1, source_target_pairs={{0,14},{2,0},{4,2},{6,4},{8,6},{10,8},{12,10},{14,12},{16,30},{18,... | collective-permute-start | bytes 1179656 | tf_op jit(solution)/shard_map/ppermute | solution.py:46
  66.5 42.8 %collective-permute-start = (bf16[384,128]{1,0:T(8,128)(2,1)}, bf16[384,128]{1,0:T(8,128)(2,1)S(1)}, u32[]{:S(2)}, u32[]{:S(2)}) collective-permute-start(bf16[384,128]{1,0:T(8,128)(2,1)} %get-tuple-element.143), channel_id=1, source_target_pairs={{0,224},{32,0},{64,32},{96,64},{128,96},{160,128},{192,160},{224,1... | collective-permute-start | bytes 294920 | tf_op jit(solution)/shard_map/ppermute | solution.py:24
  85.5 1.1 copy-start.4
  88.3 0.7 copy-start.13
  89.0 0.7 copy-start.15
  89.8 0.8 copy-start.17
  90.6 0.7 copy-start.19
  99.5 1.9 copy-start.9
  101.4 1.9 copy-start.11
  103.2 11.5 %copy-start.20 = (bf16[24,8192]{1,0:T(8,128)(2,1)S(1)}, bf16[24,8192]{1,0:T(8,128)(2,1)}, u32[]{:S(2)}) copy-start(bf16[24,8192]{1,0:T(8,128)(2,1)} %copy-done.19) | copy-start | bytes 1179652
  103.3 15.0 %copy-start.18 = (bf16[24,8192]{1,0:T(8,128)(2,1)S(1)}, bf16[24,8192]{1,0:T(8,128)(2,1)}, u32[]{:S(2)}) copy-start(bf16[24,8192]{1,0:T(8,128)(2,1)} %copy-done.17) | copy-start | bytes 1179652
  103.3 17.8 %copy-start.16 = (bf16[24,8192]{1,0:T(8,128)(2,1)S(1)}, bf16[24,8192]{1,0:T(8,128)(2,1)}, u32[]{:S(2)}) copy-start(bf16[24,8192]{1,0:T(8,128)(2,1)} %copy-done.15) | copy-start | bytes 1179652
  103.3 21.2 %copy-start.14 = (bf16[24,8192]{1,0:T(8,128)(2,1)S(1)}, bf16[24,8192]{1,0:T(8,128)(2,1)}, u32[]{:S(2)}) copy-start(bf16[24,8192]{1,0:T(8,128)(2,1)} %copy-done.13) | copy-start | bytes 1179652
  103.3 61.7 %copy-start.10 = (bf16[1,1,2048,768]{3,2,1,0:T(8,128)(2,1)S(1)}, bf16[1,1,2048,768]{3,2,1,0:T(8,128)(2,1)}, u32[]{:S(2)}) copy-start(bf16[1,1,2048,768]{3,2,1,0:T(8,128)(2,1)} %param.11) | copy-start | bytes 9437188
  103.3 61.7 %copy-start.12 = (bf16[1,1,768,2048]{3,2,1,0:T(8,128)(2,1)S(1)}, bf16[1,1,768,2048]{3,2,1,0:T(8,128)(2,1)}, u32[]{:S(2)}) copy-start(bf16[1,1,768,2048]{3,2,1,0:T(8,128)(2,1)} %param.12) | copy-start | bytes 9437188
  114.1 20.0 %collective-permute-start.6 = (bf16[24,16384]{1,0:T(8,128)(2,1)S(1)}, bf16[24,16384]{1,0:T(8,128)(2,1)S(1)}, u32[]{:S(2)}, u32[]{:S(2)}) collective-permute-start(bf16[24,16384]{1,0:T(8,128)(2,1)S(1)} %get-tuple-element.79), channel_id=1, source_target_pairs={{0,16},{2,18},{4,20},{6,22},{8,24},{10,26},{12,28},{14,30},{16,0},... | collective-permute-start | bytes 2359304 | tf_op jit(solution)/shard_map/ppermute | solution.py:24
  114.7 31.2 %collective-permute-start.7 = (bf16[24,8192]{1,0:T(8,128)(2,1)S(1)}, bf16[24,8192]{1,0:T(8,128)(2,1)S(1)}, u32[]{:S(2)}, u32[]{:S(2)}) collective-permute-start(bf16[24,8192]{1,0:T(8,128)(2,1)S(1)} %copy-done.20), channel_id=1, source_target_pairs={{0,4},{2,6},{4,8},{6,10},{8,12},{10,14},{12,0},{14,2},{16,20},{18,... | collective-permute-start | bytes 1179656 | tf_op jit(solution)/shard_map/ppermute | solution.py:46
  118.2 27.7 %collective-permute-start.8 = (bf16[24,8192]{1,0:T(8,128)(2,1)S(1)}, bf16[24,8192]{1,0:T(8,128)(2,1)S(1)}, u32[]{:S(2)}, u32[]{:S(2)}) collective-permute-start(bf16[24,8192]{1,0:T(8,128)(2,1)S(1)} %copy-done.18), channel_id=1, source_target_pairs={{0,12},{2,14},{4,0},{6,2},{8,4},{10,6},{12,8},{14,10},{16,28},{18,... | collective-permute-start | bytes 1179656 | tf_op jit(solution)/shard_map/ppermute | solution.py:46
  121.0 39.5 %collective-permute-start.9 = (bf16[24,8192]{1,0:T(8,128)(2,1)S(1)}, bf16[24,8192]{1,0:T(8,128)(2,1)S(1)}, u32[]{:S(2)}, u32[]{:S(2)}) collective-permute-start(bf16[24,8192]{1,0:T(8,128)(2,1)S(1)} %copy-done.16), channel_id=1, source_target_pairs={{0,6},{2,8},{4,10},{6,12},{8,14},{10,0},{12,2},{14,4},{16,22},{18,... | collective-permute-start | bytes 1179656 | tf_op jit(solution)/shard_map/ppermute | solution.py:46
  124.5 40.5 %collective-permute-start.10 = (bf16[24,8192]{1,0:T(8,128)(2,1)S(1)}, bf16[24,8192]{1,0:T(8,128)(2,1)S(1)}, u32[]{:S(2)}, u32[]{:S(2)}) collective-permute-start(bf16[24,8192]{1,0:T(8,128)(2,1)S(1)} %copy-done.14), channel_id=1, source_target_pairs={{0,10},{2,12},{4,14},{6,0},{8,2},{10,4},{12,6},{14,8},{16,26},{18,... | collective-permute-start | bytes 1179656 | tf_op jit(solution)/shard_map/ppermute | solution.py:46
  137.1 35.2 %collective-permute-start.11 = (bf16[24,4096]{1,0:T(8,128)(2,1)S(1)}, bf16[24,4096]{1,0:T(8,128)(2,1)S(1)}, u32[]{:S(2)}, u32[]{:S(2)}) collective-permute-start(bf16[24,4096]{1,0:T(8,128)(2,1)S(1)} %get-tuple-element.98), channel_id=1, source_target_pairs={{0,14},{2,0},{4,2},{6,4},{8,6},{10,8},{12,10},{14,12},{16,30},{18,... | collective-permute-start | bytes 589832 | tf_op jit(solution)/shard_map/ppermute | solution.py:46
  145.9 26.4 %collective-permute-start.12 = (bf16[24,4096]{1,0:T(8,128)(2,1)S(1)}, bf16[24,4096]{1,0:T(8,128)(2,1)S(1)}, u32[]{:S(2)}, u32[]{:S(2)}) collective-permute-start(bf16[24,4096]{1,0:T(8,128)(2,1)S(1)} %get-tuple-element.99), channel_id=1, source_target_pairs={{0,2},{2,4},{4,6},{6,8},{8,10},{10,12},{12,14},{14,0},{16,18},{18,... | collective-permute-start | bytes 589832 | tf_op jit(solution)/shard_map/ppermute | solution.py:46
  145.9 27.3 %collective-permute-start.13 = (bf16[24,4096]{1,0:T(8,128)(2,1)S(1)}, bf16[24,4096]{1,0:T(8,128)(2,1)S(1)}, u32[]{:S(2)}, u32[]{:S(2)}) collective-permute-start(bf16[24,4096]{1,0:T(8,128)(2,1)S(1)} %get-tuple-element.100), channel_id=1, source_target_pairs={{0,12},{2,14},{4,0},{6,2},{8,4},{10,6},{12,8},{14,10},{16,28},{18,... | collective-permute-start | bytes 589832 | tf_op jit(solution)/shard_map/ppermute | solution.py:46
  160.6 12.6 %collective-permute-start.14 = (bf16[24,4096]{1,0:T(8,128)(2,1)S(1)}, bf16[24,4096]{1,0:T(8,128)(2,1)S(1)}, u32[]{:S(2)}, u32[]{:S(2)}) collective-permute-start(bf16[24,4096]{1,0:T(8,128)(2,1)S(1)} %get-tuple-element.101), channel_id=1, source_target_pairs={{0,4},{2,6},{4,8},{6,10},{8,12},{10,14},{12,0},{14,2},{16,20},{18,... | collective-permute-start | bytes 589832 | tf_op jit(solution)/shard_map/ppermute | solution.py:46
  173.2 29.4 %collective-permute-start.15 = (bf16[24,16384]{1,0:T(8,128)(2,1)S(1)}, bf16[24,16384]{1,0:T(8,128)(2,1)S(1)}, u32[]{:S(2)}, u32[]{:S(2)}) collective-permute-start(bf16[24,16384]{1,0:T(8,128)(2,1)S(1)} %get-tuple-element.102), channel_id=1, source_target_pairs={{0,16},{2,18},{4,20},{6,22},{8,24},{10,26},{12,28},{14,30},{16,0},... | collective-permute-start | bytes 2359304 | tf_op jit(solution)/shard_map/ppermute | solution.py:24
  177.1 16.9 %collective-permute-start.16 = (bf16[24,4096]{1,0:T(8,128)(2,1)S(1)}, bf16[24,4096]{1,0:T(8,128)(2,1)S(1)}, u32[]{:S(2)}, u32[]{:S(2)}) collective-permute-start(bf16[24,4096]{1,0:T(8,128)(2,1)S(1)} %get-tuple-element.103), channel_id=1, source_target_pairs={{0,8},{2,10},{4,12},{6,14},{8,0},{10,2},{12,4},{14,6},{16,24},{18,... | collective-permute-start | bytes 589832 | tf_op jit(solution)/shard_map/ppermute | solution.py:46
  182.1 20.5 %collective-permute-start.17 = (bf16[24,4096]{1,0:T(8,128)(2,1)S(1)}, bf16[24,4096]{1,0:T(8,128)(2,1)S(1)}, u32[]{:S(2)}, u32[]{:S(2)}) collective-permute-start(bf16[24,4096]{1,0:T(8,128)(2,1)S(1)} %get-tuple-element.104), channel_id=1, source_target_pairs={{0,10},{2,12},{4,14},{6,0},{8,2},{10,4},{12,6},{14,8},{16,26},{18,... | collective-permute-start | bytes 589832 | tf_op jit(solution)/shard_map/ppermute | solution.py:46
  185.3 17.3 %collective-permute-start.18 = (bf16[24,4096]{1,0:T(8,128)(2,1)S(1)}, bf16[24,4096]{1,0:T(8,128)(2,1)S(1)}, u32[]{:S(2)}, u32[]{:S(2)}) collective-permute-start(bf16[24,4096]{1,0:T(8,128)(2,1)S(1)} %get-tuple-element.105), channel_id=1, source_target_pairs={{0,6},{2,8},{4,10},{6,12},{8,14},{10,0},{12,2},{14,4},{16,22},{18,... | collective-permute-start | bytes 589832 | tf_op jit(solution)/shard_map/ppermute | solution.py:46
  205.5 32.3 %collective-permute-start.28 = (f32[768,2048]{1,0:T(8,128)S(1)}, f32[768,2048]{1,0:T(8,128)}, u32[]{:S(2)}, u32[]{:S(2)}) collective-permute-start(f32[768,2048]{1,0:T(8,128)S(1)} %shard_map.96), channel_id=1, source_target_pairs={{0,1},{1,0},{2,3},{3,2},{4,5},{5,4},{6,7},{7,6},{8,9},{9,8},{10,11... | collective-permute-start | bytes 18874376 | tf_op jit(solution)/shard_map/ppermute | solution.py:24
  205.6 13.4 %collective-permute-start.20 = (bf16[24,4096]{1,0:T(8,128)(2,1)S(1)}, bf16[24,4096]{1,0:T(8,128)(2,1)S(1)}, u32[]{:S(2)}, u32[]{:S(2)}) collective-permute-start(bf16[24,4096]{1,0:T(8,128)(2,1)S(1)} %get-tuple-element.125), channel_id=1, source_target_pairs={{0,224},{2,226},{4,228},{6,230},{8,232},{10,234},{12,236},{14,238}... | collective-permute-start | bytes 589832 | tf_op jit(solution)/shard_map/ppermute | solution.py:39
  208.0 18.8 %collective-permute-start.21 = (bf16[24,4096]{1,0:T(8,128)(2,1)S(1)}, bf16[24,4096]{1,0:T(8,128)(2,1)S(1)}, u32[]{:S(2)}, u32[]{:S(2)}) collective-permute-start(bf16[24,4096]{1,0:T(8,128)(2,1)S(1)} %get-tuple-element.126), channel_id=1, source_target_pairs={{0,232},{2,234},{4,236},{6,238},{8,224},{10,226},{12,228},{14,230}... | collective-permute-start | bytes 589832 | tf_op jit(solution)/shard_map/ppermute | solution.py:39
  212.4 18.9 %collective-permute-start.22 = (bf16[24,4096]{1,0:T(8,128)(2,1)S(1)}, bf16[24,4096]{1,0:T(8,128)(2,1)S(1)}, u32[]{:S(2)}, u32[]{:S(2)}) collective-permute-start(bf16[24,4096]{1,0:T(8,128)(2,1)S(1)} %get-tuple-element.127), channel_id=1, source_target_pairs={{0,238},{2,224},{4,226},{6,228},{8,230},{10,232},{12,234},{14,236}... | collective-permute-start | bytes 589832 | tf_op jit(solution)/shard_map/ppermute | solution.py:39
  213.3 18.1 %collective-permute-start.23 = (bf16[24,4096]{1,0:T(8,128)(2,1)S(1)}, bf16[24,4096]{1,0:T(8,128)(2,1)S(1)}, u32[]{:S(2)}, u32[]{:S(2)}) collective-permute-start(bf16[24,4096]{1,0:T(8,128)(2,1)S(1)} %get-tuple-element.128), channel_id=1, source_target_pairs={{0,226},{2,228},{4,230},{6,232},{8,234},{10,236},{12,238},{14,224}... | collective-permute-start | bytes 589832 | tf_op jit(solution)/shard_map/ppermute | solution.py:39
  219.0 41.1 %collective-permute-start.19 = (bf16[128,2048]{1,0:T(8,128)(2,1)S(1)}, bf16[128,2048]{1,0:T(8,128)(2,1)S(1)}, u32[]{:S(2)}, u32[]{:S(2)}) collective-permute-start(bf16[128,2048]{1,0:T(8,128)(2,1)S(1)} %shard_map.97), channel_id=1, source_target_pairs={{0,224},{32,0},{64,32},{96,64},{128,96},{160,128},{192,160},{224,1... | collective-permute-start | bytes 1572872 | tf_op jit(solution)/shard_map/ppermute | solution.py:24
  226.8 22.3 %collective-permute-start.24 = (bf16[24,4096]{1,0:T(8,128)(2,1)S(1)}, bf16[24,4096]{1,0:T(8,128)(2,1)S(1)}, u32[]{:S(2)}, u32[]{:S(2)}) collective-permute-start(bf16[24,4096]{1,0:T(8,128)(2,1)S(1)} %get-tuple-element.129), channel_id=1, source_target_pairs={{0,236},{2,238},{4,224},{6,226},{8,228},{10,230},{12,232},{14,234}... | collective-permute-start | bytes 589832 | tf_op jit(solution)/shard_map/ppermute | solution.py:39
  231.3 17.8 %collective-permute-start.25 = (bf16[24,4096]{1,0:T(8,128)(2,1)S(1)}, bf16[24,4096]{1,0:T(8,128)(2,1)S(1)}, u32[]{:S(2)}, u32[]{:S(2)}) collective-permute-start(bf16[24,4096]{1,0:T(8,128)(2,1)S(1)} %get-tuple-element.130), channel_id=1, source_target_pairs={{0,228},{2,230},{4,232},{6,234},{8,236},{10,238},{12,224},{14,226}... | collective-permute-start | bytes 589832 | tf_op jit(solution)/shard_map/ppermute | solution.py:39
  231.4 22.6 %collective-permute-start.26 = (bf16[24,4096]{1,0:T(8,128)(2,1)S(1)}, bf16[24,4096]{1,0:T(8,128)(2,1)S(1)}, u32[]{:S(2)}, u32[]{:S(2)}) collective-permute-start(bf16[24,4096]{1,0:T(8,128)(2,1)S(1)} %get-tuple-element.131), channel_id=1, source_target_pairs={{0,234},{2,236},{4,238},{6,224},{8,226},{10,228},{12,230},{14,232}... | collective-permute-start | bytes 589832 | tf_op jit(solution)/shard_map/ppermute | solution.py:39
  237.9 22.2 %collective-permute-start.27 = (bf16[24,4096]{1,0:T(8,128)(2,1)S(1)}, bf16[24,4096]{1,0:T(8,128)(2,1)S(1)}, u32[]{:S(2)}, u32[]{:S(2)}) collective-permute-start(bf16[24,4096]{1,0:T(8,128)(2,1)S(1)} %get-tuple-element.132), channel_id=1, source_target_pairs={{0,230},{2,232},{4,234},{6,236},{8,238},{10,224},{12,226},{14,228}... | collective-permute-start | bytes 589832 | tf_op jit(solution)/shard_map/ppermute | solution.py:39
  249.1 12.6 %copy-start.2 = (bf16[768,2048]{1,0:T(8,128)(2,1)}, bf16[768,2048]{1,0:T(8,128)(2,1)S(1)}, u32[]{:S(2)}) copy-start(bf16[768,2048]{1,0:T(8,128)(2,1)S(1)} %add_convert_fusion.refs_9_) | copy-start | bytes 9437188

commit v5 on v4

--- a/solution.py
+++ b/solution.py
@@ -13,7 +13,7 @@
 AWAY = (0, 4, 1, 7, 2, 6, 3, 5)
 EARLY = 4
 MEANWHILE = (2, 3, 4, 5)
-LAST = (6, 7, 4, 5, 0, 1, 2, 3)
+BEFORE = (4, 5, 6, 7)
 BF16 = jnp.bfloat16
 MIB = 1024 * 1024
 
@@ -28,11 +28,10 @@
     return from_behind(value, "expert", lax.axis_size("expert") // COLUMNS)
 
 
-def along_ring_behind(value, steps):
+def swap_columns_behind(value):
     sections, groups = lax.axis_size("pipe"), lax.axis_size("expert")
-    ring = groups // COLUMNS
     pairs = [
-        (s * groups + e, (s - 1) % sections * groups + e // ring * ring + (e + steps) % ring)
+        (s * groups + e, (s - 1) % sections * groups + (e + groups // COLUMNS) % groups)
         for s in range(sections)
         for e in range(groups)
     ]
@@ -245,16 +244,15 @@
     )(*arrays, *after)
 
 
-def pair_up(own, crossed, ring, after=()):
-    size = own.shape[1] // ring
-    moves = []
-    for d in range(ring):
-        moves.append((0, d * size, d, 0, size))
-        moves.append((1, d * size, d, size, size))
-    return pack([own, crossed], moves, [2 * size] * ring, after)
-
-
-def expert_rows(blocks, me, weight_in, weight_out, after=()):
+def pair_up(arrays, ring):
+    size = arrays[0].shape[1] // ring
+    moves = [
+        (n, d * size, d, n * size, size) for d in range(ring) for n in range(len(arrays))
+    ]
+    return pack(arrays, moves, [len(arrays) * size] * ring)
+
+
+def expert_rows(blocks, me, weight_in, weight_out, cuts, after=()):
     width, hid = weight_in.shape
     one = not isinstance(blocks, list)
     arrays = [blocks] if one else blocks
@@ -264,10 +262,11 @@
     tile = 256
     piece = 512
     ring = number // COLUMNS
+    share = width // cuts
 
     def kernel(*refs):
         in_ref, out_ref, me_ref = refs[count : count + 3]
-        backs = refs[count + 3 + len(after) :][:COLUMNS]
+        backs = refs[count + 3 + len(after) :][: COLUMNS * cuts]
         mine, place = me_ref[0] // ring, me_ref[0] % ring
         hidden_ref, scaled_ref, stacked_ref, pre_grad_ref = refs[-4:]
 
@@ -312,10 +311,10 @@
             )
             for n in range(number):
                 rows_back = returned[n * CAP : (n + 1) * CAP].astype(BF16)
-                to = n // COLUMNS * width + start
-                backs[n % COLUMNS][:, to : to + tile] = rows_back
-
-    shapes = [(CAP, ring * width)] * COLUMNS
+                to = n // COLUMNS * share + start % share
+                backs[start // share * COLUMNS + n % COLUMNS][:, to : to + tile] = rows_back
+
+    shapes = [(CAP, ring * share)] * (COLUMNS * cuts)
     shapes = shapes + [(rows, hid), (rows, width)]
     return pl.pallas_call(
         kernel,
@@ -334,10 +333,9 @@
     )(*arrays, weight_in, weight_out, me.reshape(1), *after)
 
 
-def combine(placing, arrived, after=()):
+def combine(placing, arrived, first, width, after=()):
     rows, tokens = placing.shape
     count = len(arrived)
-    width = arrived[0].shape[1] // COLUMNS
     piece = 512
 
     def kernel(placing_ref, *refs):
@@ -345,8 +343,8 @@
         for start in range(0, width, piece):
             stacked = jnp.concatenate(
                 [
-                    refs[d][:, c * width + start : c * width + start + piece].astype(jnp.float32)
-                    for c in range(COLUMNS)
+                    refs[d][:, column : column + piece].astype(jnp.float32)
+                    for column in (first + start, first + width + start)
                     for d in range(count)
                 ],
                 axis=0,
@@ -450,33 +448,45 @@
 
     blocks = send_pack(0, EARLY)
     second = {i: along_ring(blocks[i], AWAY[i]) for i in range(1, EARLY)}
-    own_0, away_0, hidden_0, scaled_0 = expert_rows(first, me, weight_in, weight_out)
+    own_0, away_0, hidden_0, scaled_0 = expert_rows(first, me, weight_in, weight_out, 1)
     held = (own_0, away_0, behind, placing, slots_1[0], send_pack(EARLY, ring))
-    (own_0, away_0, behind, placing, _, late), second = together(held, second, range(1, EARLY))
+    (own_0, away_0, behind, placing, placing_1, late), second = together(held, second, range(1, EARLY))
     blocks += late
     second[0] = blocks[0]
     second.update({i: along_ring(blocks[i], AWAY[i]) for i in range(EARLY, ring)})
-    back = pair_up(own_0, swap_columns(away_0), ring)
+    back = pair_up([own_0, swap_columns(away_0)], ring)
     rest = [i for i in range(1, ring) if i not in MEANWHILE]
 
-    own_1, away_1, hidden_1, scaled_1 = expert_rows(
-        [second[i] for i in range(ring)], me, weight_in, weight_out, back[:1]
+    *cut_1, hidden_1, scaled_1 = expert_rows(
+        [second[i] for i in range(ring)], me, weight_in, weight_out, 2, back[:1]
     )
     back_0 = {i: along_ring(back[i], -AWAY[i]) for i in MEANWHILE}
-    partial_value = weight_grad([hidden_0, hidden_1], [scaled_0, scaled_1], [])
-    held = (own_1, away_1, [back[i] for i in rest])
-    (own_1, away_1, held), back_0 = together(held, back_0, MEANWHILE)
+    held = (cut_1, [back[i] for i in rest])
+    (cut_1, held), back_0 = together(held, back_0, MEANWHILE)
     back_0.update({i: along_ring(held[n], -AWAY[i]) for n, i in enumerate(rest)})
     back_0[0] = back[0]
-    held = (partial_value, swap_columns(away_1))
-    (partial_value, away_1), back_0 = together(held, back_0, rest)
-    back, partial_value = lax.optimization_barrier((pair_up(own_1, away_1, ring), partial_value))
+    partial_value = weight_grad([hidden_0, hidden_1], [scaled_0, scaled_1], [])
+    own_left, away_left, own_right, away_right = cut_1
+    moved = [
+        own_left,
+        swap_columns(away_left),
+        from_behind(own_right, "pipe", -1),
+        swap_columns_behind(away_right),
+    ]
+    (partial_value, moved), back_0 = together((partial_value, moved), back_0, rest)
+    back = pair_up(moved, ring)
+    back_1 = {i: along_ring(back[i], -AWAY[i]) for i in range(1, ring)}
+    back_1[0] = back[0]
+
+    grad_0 = combine(placing, [back_0[i] for i in range(ring)], 0, width)
+    (grad_0, partial_value), back_1 = together((grad_0, partial_value), back_1, BEFORE)
+    back_1 = [back_1[i] for i in range(ring)]
+    grad_0 = from_behind(grad_0, "pipe", -1)
     proj_grad = (partial_value + from_behind(partial_value, "dp", 1)).astype(BF16)
-    back_1 = [along_ring_behind(back[i], -AWAY[i]) for i in LAST]
-    back_1 = [back_1[LAST.index(i)] for i in range(ring)]
-
-    grad_0 = from_behind(combine(placing, [back_0[i] for i in range(ring)]), "pipe", -1)
-    grad_1 = combine(behind, back_1, [grad_0, proj_grad])
+    left = combine(placing_1, back_1, 0, width // 2, [grad_0, proj_grad])
+    right = combine(behind, back_1, width, width // 2, [left])
+    left = from_behind(left, "pipe", -1)
+    grad_1 = jnp.concatenate([left, right], axis=1)
     return (jnp.stack([grad_0, grad_1])[None], proj_grad[None, None])
 
 

time: 265 us -> 267 us (level)
  waiting for transfers between devices: 122 us -> 129 us
    ppermute x8 -> x1, starting transfers between devices: 26.9 us -> 0.19 us  [swap_columns_behind(): return lax.ppermute(value, ('pipe', 'expert'), pairs)]
    ppermute x14 -> x21, starting transfers between devices: 35.9 us -> 59.8 us  [along_ring(): return lax.ppermute(value, 'expert', pairs)]
    ppermute x8 -> x1, waiting for transfers between devices: 22.2 us -> 0.01 us  [swap_columns_behind(): return lax.ppermute(value, ('pipe', 'expert'), pairs)]
    ppermute x7 -> x9, waiting for transfers between devices: 55.2 us -> 70.5 us  [from_behind(): return lax.ppermute(value, axis, pairs)]
    ppermute x14 -> x21, waiting for transfers between devices: 36.9 us -> 47.7 us  [along_ring(): return lax.ppermute(value, 'expert', pairs)]
    all_to_all x1, waiting for transfers between devices: 8.17 us -> 11.2 us  [swap_groups(): lax.all_to_all(value, 'expert', split_axis=0, concat_axis=0, tiled=True)]
    ppermute x7 -> x9, starting transfers between devices: 10.1 us -> 11 us  [from_behind(): return lax.ppermute(value, axis, pairs)]
    unnamed x44 -> x32, local copies, waits for them, and re-layouts: 10.5 us -> 10.1 us
  transfers between devices with their start and end apart: 30 -> 32, of which waited for: 16 -> 18; matrix products, arithmetic and copies ran while one was open for 2% -> 2% of each run, Pallas kernels for 11% -> 11%
where the time goes in v5:
time: 267 us; the launch traced here: 266 us
  waiting for transfers between devices  129 us (48%)
  starting transfers between devices  82.6 us (31%)
  Pallas kernels  36.9 us (14%)
  local copies, waits for them, and re-layouts  10.6 us (4%)
  other arithmetic  5.82 us (2%)
    ppermute x9, waiting for transfers between devices, from_behind(): return lax.ppermute(value, axis, pairs)  70.5 us
    ppermute x21, starting transfers between devices, along_ring(): return lax.ppermute(value, 'expert', pairs)  59.8 us
    ppermute x21, waiting for transfers between devices, along_ring(): return lax.ppermute(value, 'expert', pairs)  47.7 us
    all_to_all x1, starting transfers between devices, swap_groups(): lax.all_to_all(value, 'expert', split_axis=0, concat_axis=0, tiled=True)  11.6 us
    all_to_all x1, waiting for transfers between devices, swap_groups(): lax.all_to_all(value, 'expert', split_axis=0, concat_axis=0, tiled=True)  11.2 us
    pallas_call x2, Pallas kernels, expert_rows(): pl.pallas_call(kernel, in_specs=[pl.BlockSpec(memory_space=pltpu.VMEM)] *...  11.1 us
    ppermute x9, starting transfers between devices, from_behind(): return lax.ppermute(value, axis, pairs)  11 us
    unnamed x32, local copies, waits for them, and re-layouts  10.1 us
  transfers between devices with their start and end apart: 32, of which 18 were waited for; matrix products, arithmetic and copies ran while one was open for 2% of the time, Pallas kernels for 11%

profile of v5, /device:TPU:14, one launch (start us, length us, event | category | flops | bytes accessed | tf_op | source)
XLA Modules:
  0.0 266.2 jit_solution(659094676620202782)
XLA Ops:
  0.6 0.7 copy-done.5
  1.3 0.7 copy-done.7
  2.0 4.6 %shard_map.86 = bf16[16,24,4096]{2,1,0:T(8,128)(2,1)} custom-call(s32[1,2,8,128]{3,2,1,0:T(8,128)S(1)} %bitcast.66, bf16[1,2,8,128]{3,2,1,0:T(8,128)(2,1)S(1)} %bitcast.67, bf16[1,2,128,2048]{3,2,1,0:T(8,128)(2,1)} %inputs_ref.9, bf16[1,2,128,2048]{3,2,1,0:T(8,128)(2,1)} %upstream_ref.9), custom_call_target="tpu_custom_call" | custom-call | flops 402653184 | bytes 4194304 | tf_op jit(solution)/shard_map/pallas_call | solution.py:180
  6.6 11.6 %all-to-all-start = ((bf16[16,24,4096]{2,1,0:T(8,128)(2,1)}), bf16[16,24,4096]{2,1,0:T(8,128)(2,1)}, u32[]{:S(2)}, u32[]{:S(2)}) async-start(bf16[16,24,4096]{2,1,0:T(8,128)(2,1)} %shard_map.86), calls=%async_computation | async-start | bytes 6291456 | tf_op jit(solution)/shard_map/all_to_all | solution.py:412
  19.3 1.4 shard_map.92
  20.9 1.3 shard_map.89
  22.2 3.4 %collective-permute-start.1 = (bf16[24,16384]{1,0:T(8,128)(2,1)}, bf16[24,16384]{1,0:T(8,128)(2,1)S(1)}, u32[]{:S(2)}, u32[]{:S(2)}) collective-permute-start(bf16[24,16384]{1,0:T(8,128)(2,1)} %shard_map.89), channel_id=1, source_target_pairs={{0,16},{2,18},{4,20},{6,22},{8,24},{10,26},{12,28},{14,30},{16,0},... | collective-permute-start | bytes 2359304 | tf_op jit(solution)/shard_map/ppermute | solution.py:24
  25.8 1.3 shard_map.91.refs_0_
  27.1 31.2 %collective-permute-done.2.refs_1_ = bf16[24,16384]{1,0:T(8,128)(2,1)} collective-permute-done((bf16[24,16384]{1,0:T(8,128)(2,1)}, bf16[24,16384]{1,0:T(8,128)(2,1)}, u32[]{:S(2)}, u32[]{:S(2)}) %collective-permute-start.2) | collective-permute-done | bytes 786464 | tf_op jit(solution)/shard_map/ppermute | solution.py:24
  58.3 1.1 copy-done.3
  59.5 2.4 shard_map.93
  61.9 0.8 copy-done.13
  62.7 0.5 collective-permute-start.3
  63.2 0.8 collective-permute-start.4
  64.0 2.4 collective-permute-start.5
  66.6 0.9 collective-permute-start
  67.5 1.3 shard_map.88.refs_0_
  68.8 16.7 %collective-permute-done.1.refs_1_ = bf16[24,16384]{1,0:T(8,128)(2,1)S(1)} collective-permute-done((bf16[24,16384]{1,0:T(8,128)(2,1)}, bf16[24,16384]{1,0:T(8,128)(2,1)S(1)}, u32[]{:S(2)}, u32[]{:S(2)}) %collective-permute-start.1) | collective-permute-done | bytes 786464 | tf_op jit(solution)/shard_map/ppermute | solution.py:24
  85.5 1.1 copy-done.4
  86.7 1.6 shard_map.90
  88.3 11.2 %all-to-all-done.refs_0_ = bf16[16,24,4096]{2,1,0:T(8,128)(2,1)} async-done(((bf16[16,24,4096]{2,1,0:T(8,128)(2,1)}), bf16[16,24,4096]{2,1,0:T(8,128)(2,1)}, u32[]{:S(2)}, u32[]{:S(2)}) %all-to-all-start) | async-done | bytes 3145760 | tf_op jit(solution)/shard_map/all_to_all | solution.py:412
  99.5 1.9 copy-done.9
  101.4 1.9 copy-done.11
  103.3 6.0 %shard_map.87 = (bf16[24,16384]{1,0:T(8,128)(2,1)S(1)}, bf16[24,16384]{1,0:T(8,128)(2,1)S(1)}, bf16[384,768]{1,0:T(8,128)(2,1)S(1)}, bf16[384,2048]{1,0:T(8,128)(2,1)S(1)}) custom-call(bf16[16,24,4096]{2,1,0:T(8,128)(2,1)} %all-to-all-done.refs_0_, bf16[2048,768]{1,0:T(8,128)(2,1)S(1)} %bitcast.68, bf16[768,2048]{1,0:T(8,128)(2,1)S(1)} %bitcast.70, ...), custom_call_target="tpu_custom_call" | custom-call | flops 3623878656 | bytes 12582912 | tf_op jit(solution)/shard_map/pallas_call | solution.py:319
  109.2 4.9 %collective-permute-done.4.refs_2_ = bf16[24,8192]{1,0:T(8,128)(2,1)} collective-permute-done((bf16[24,8192]{1,0:T(8,128)(2,1)}, bf16[24,8192]{1,0:T(8,128)(2,1)}, u32[]{:S(2)}, u32[]{:S(2)}) %collective-permute-start.4) | collective-permute-done | bytes 393248 | tf_op jit(solution)/shard_map/ppermute | solution.py:45
  114.1 0.6 collective-permute-start.6
  114.7 3.4 %collective-permute-start.7 = (bf16[24,8192]{1,0:T(8,128)(2,1)S(1)}, bf16[24,8192]{1,0:T(8,128)(2,1)S(1)}, u32[]{:S(2)}, u32[]{:S(2)}) collective-permute-start(bf16[24,8192]{1,0:T(8,128)(2,1)S(1)} %get-tuple-element.91), channel_id=1, source_target_pairs={{0,4},{2,6},{4,8},{6,10},{8,12},{10,14},{12,0},{14,2},{16,20},{18,... | collective-permute-start | bytes 1179656 | tf_op jit(solution)/shard_map/ppermute | solution.py:45
  118.1 2.8 %collective-permute-start.8 = (bf16[24,8192]{1,0:T(8,128)(2,1)S(1)}, bf16[24,8192]{1,0:T(8,128)(2,1)S(1)}, u32[]{:S(2)}, u32[]{:S(2)}) collective-permute-start(bf16[24,8192]{1,0:T(8,128)(2,1)S(1)} %get-tuple-element.92), channel_id=1, source_target_pairs={{0,12},{2,14},{4,0},{6,2},{8,4},{10,6},{12,8},{14,10},{16,28},{18,... | collective-permute-start | bytes 1179656 | tf_op jit(solution)/shard_map/ppermute | solution.py:45
  120.9 3.5 %collective-permute-start.9 = (bf16[24,8192]{1,0:T(8,128)(2,1)S(1)}, bf16[24,8192]{1,0:T(8,128)(2,1)S(1)}, u32[]{:S(2)}, u32[]{:S(2)}) collective-permute-start(bf16[24,8192]{1,0:T(8,128)(2,1)S(1)} %get-tuple-element.93), channel_id=1, source_target_pairs={{0,6},{2,8},{4,10},{6,12},{8,14},{10,0},{12,2},{14,4},{16,22},{18,... | collective-permute-start | bytes 1179656 | tf_op jit(solution)/shard_map/ppermute | solution.py:45
  124.4 2.6 collective-permute-start.10
  127.0 7.2 %collective-permute-done.6.refs_1_ = bf16[24,16384]{1,0:T(8,128)(2,1)S(1)} collective-permute-done((bf16[24,16384]{1,0:T(8,128)(2,1)S(1)}, bf16[24,16384]{1,0:T(8,128)(2,1)S(1)}, u32[]{:S(2)}, u32[]{:S(2)}) %collective-permute-start.6) | collective-permute-done | bytes 786464 | tf_op jit(solution)/shard_map/ppermute | solution.py:24
  134.2 2.9 %shard_map.94 = (bf16[24,4096]{1,0:T(8,128)(2,1)S(1)}, bf16[24,4096]{1,0:T(8,128)(2,1)S(1)}, bf16[24,4096]{1,0:T(8,128)(2,1)S(1)}, bf16[24,4096]{1,0:T(8,128)(2,...) custom-call(bf16[24,16384]{1,0:T(8,128)(2,1)S(1)} %get-tuple-element, ...), custom_call_target="tpu_custom_call" | custom-call | bytes 3145728 | tf_op jit(solution)/shard_map/pallas_call | solution.py:235
  137.1 2.7 %collective-permute-start.11 = (bf16[24,4096]{1,0:T(8,128)(2,1)S(1)}, bf16[24,4096]{1,0:T(8,128)(2,1)S(1)}, u32[]{:S(2)}, u32[]{:S(2)}) collective-permute-start(bf16[24,4096]{1,0:T(8,128)(2,1)S(1)} %get-tuple-element.105), channel_id=1, source_target_pairs={{0,14},{2,0},{4,2},{6,4},{8,6},{10,8},{12,10},{14,12},{16,30},{18,... | collective-permute-start | bytes 589832 | tf_op jit(solution)/shard_map/ppermute | solution.py:45
  139.8 4.3 %collective-permute-done.7.refs_4_ = bf16[24,8192]{1,0:T(8,128)(2,1)S(1)} collective-permute-done((bf16[24,8192]{1,0:T(8,128)(2,1)S(1)}, bf16[24,8192]{1,0:T(8,128)(2,1)S(1)}, u32[]{:S(2)}, u32[]{:S(2)}) %collective-permute-start.7) | collective-permute-done | bytes 393248 | tf_op jit(solution)/shard_map/ppermute | solution.py:45
  144.0 6.9 %collective-permute-start.13 = (bf16[24,4096]{1,0:T(8,128)(2,1)S(1)}, bf16[24,4096]{1,0:T(8,128)(2,1)S(1)}, u32[]{:S(2)}, u32[]{:S(2)}) collective-permute-start(bf16[24,4096]{1,0:T(8,128)(2,1)S(1)} %get-tuple-element.107), channel_id=1, source_target_pairs={{0,12},{2,14},{4,0},{6,2},{8,4},{10,6},{12,8},{14,10},{16,28},{18,... | collective-permute-start | bytes 589832 | tf_op jit(solution)/shard_map/ppermute | solution.py:45
  150.9 9.8 %collective-permute-done.9.refs_6_ = bf16[24,8192]{1,0:T(8,128)(2,1)S(1)} collective-permute-done((bf16[24,8192]{1,0:T(8,128)(2,1)S(1)}, bf16[24,8192]{1,0:T(8,128)(2,1)S(1)}, u32[]{:S(2)}, u32[]{:S(2)}) %collective-permute-start.9) | collective-permute-done | bytes 393248 | tf_op jit(solution)/shard_map/ppermute | solution.py:45
  160.7 3.1 %collective-permute-start.14 = (bf16[24,4096]{1,0:T(8,128)(2,1)S(1)}, bf16[24,4096]{1,0:T(8,128)(2,1)S(1)}, u32[]{:S(2)}, u32[]{:S(2)}) collective-permute-start(bf16[24,4096]{1,0:T(8,128)(2,1)S(1)} %get-tuple-element.108), channel_id=1, source_target_pairs={{0,4},{2,6},{4,8},{6,10},{8,12},{10,14},{12,0},{14,2},{16,20},{18,... | collective-permute-start | bytes 589832 | tf_op jit(solution)/shard_map/ppermute | solution.py:45
  163.8 0.8 collective-permute-done.10.refs_7_
  164.6 1.9 copy-done.12
  166.5 5.2 %shard_map.95 = (bf16[24,8192]{1,0:T(8,128)(2,1)S(1)}, bf16[24,8192]{1,0:T(8,128)(2,1)S(1)}, bf16[24,8192]{1,0:T(8,128)(2,1)S(1)}, bf16[24,8192]{1,0:T(8,128)(2,...) custom-call(bf16[24,8192]{1,0:T(8,128)(2,1)S(1)} %copy-done.14, ...), custom_call_target="tpu_custom_call" | custom-call | flops 3623878656 | bytes 12582912 | tf_op jit(solution)/shard_map/pallas_call | solution.py:319
  171.7 0.6 collective-permute-done.11.refs_2_
  172.3 6.7 %collective-permute-start.18 = (bf16[24,4096]{1,0:T(8,128)(2,1)S(1)}, bf16[24,4096]{1,0:T(8,128)(2,1)S(1)}, u32[]{:S(2)}, u32[]{:S(2)}) collective-permute-start(bf16[24,4096]{1,0:T(8,128)(2,1)S(1)} %get-tuple-element.113), channel_id=1, source_target_pairs={{0,8},{2,10},{4,12},{6,14},{8,0},{10,2},{12,4},{14,6},{16,24},{18,... | collective-permute-start | bytes 589832 | tf_op jit(solution)/shard_map/ppermute | solution.py:45
  179.0 3.1 %collective-permute-start.15 = (bf16[24,8192]{1,0:T(8,128)(2,1)S(1)}, bf16[24,8192]{1,0:T(8,128)(2,1)S(1)}, u32[]{:S(2)}, u32[]{:S(2)}) collective-permute-start(bf16[24,8192]{1,0:T(8,128)(2,1)S(1)} %get-tuple-element.110), channel_id=1, source_target_pairs={{0,16},{2,18},{4,20},{6,22},{8,24},{10,26},{12,28},{14,30},{16,0},... | collective-permute-start | bytes 1179656 | tf_op jit(solution)/shard_map/ppermute | solution.py:24
  182.0 0.8 collective-permute-start.16
  183.0 6.3 %collective-permute-start.19 = (bf16[24,4096]{1,0:T(8,128)(2,1)S(1)}, bf16[24,4096]{1,0:T(8,128)(2,1)S(1)}, u32[]{:S(2)}, u32[]{:S(2)}) collective-permute-start(bf16[24,4096]{1,0:T(8,128)(2,1)S(1)} %get-tuple-element.114), channel_id=1, source_target_pairs={{0,10},{2,12},{4,14},{6,0},{8,2},{10,4},{12,6},{14,8},{16,26},{18,... | collective-permute-start | bytes 589832 | tf_op jit(solution)/shard_map/ppermute | solution.py:45
  189.3 1.7 collective-permute-start.20
  191.0 4.6 %shard_map.96 = f32[768,2048]{1,0:T(8,128)S(1)} custom-call(bf16[384,768]{1,0:T(8,128)(2,1)S(1)} %get-tuple-element.86.refs_0_, bf16[384,768]{1,0:T(8,128)(2,1)S(1)} %get-tuple-element.95.refs_1_, bf16[384,2048]{1,0:T(8,128)(2,1)S(1)} %get-tuple-element.96.refs_2_, bf16[384,2048]{1,0:T(8,128)(2,1)S(1)} %get-tuple-element.97.refs_3_), custom_call_target="tpu_custom_call" | custom-call | flops 2415919104 | bytes 10616832 | tf_op jit(solution)/shard_map/pallas_call | solution.py:394
  195.6 6.1 %collective-permute-done.19.refs_6_ = bf16[24,4096]{1,0:T(8,128)(2,1)S(1)} collective-permute-done((bf16[24,4096]{1,0:T(8,128)(2,1)S(1)}, bf16[24,4096]{1,0:T(8,128)(2,1)S(1)}, u32[]{:S(2)}, u32[]{:S(2)}) %collective-permute-start.19) | collective-permute-done | bytes 196640 | tf_op jit(solution)/shard_map/ppermute | solution.py:45
  201.7 1.4 collective-permute-done.20.refs_7_
  203.2 1.2 collective-permute-done.16.refs_2_
  204.3 3.1 %shard_map.98 = (bf16[24,4096]{1,0:T(8,128)(2,1)S(1)}, bf16[24,4096]{1,0:T(8,128)(2,1)S(1)}, bf16[24,4096]{1,0:T(8,128)(2,1)S(1)}, bf16[24,4096]{1,0:T(8,128)(2,...) custom-call(bf16[24,8192]{1,0:T(8,128)(2,1)S(1)} %get-tuple-element., ...), custom_call_target="tpu_custom_call" | custom-call | bytes 3145728 | tf_op jit(solution)/shard_map/pallas_call | solution.py:235
  207.4 1.0 collective-permute-start.21
  208.5 2.0 collective-permute-start.22
  210.4 5.4 %collective-permute-start.23 = (bf16[24,4096]{1,0:T(8,128)(2,1)S(1)}, bf16[24,4096]{1,0:T(8,128)(2,1)S(1)}, u32[]{:S(2)}, u32[]{:S(2)}) collective-permute-start(bf16[24,4096]{1,0:T(8,128)(2,1)S(1)} %get-tuple-element.130), channel_id=1, source_target_pairs={{0,10},{2,12},{4,14},{6,0},{8,2},{10,4},{12,6},{14,8},{16,26},{18,... | collective-permute-start | bytes 589832 | tf_op jit(solution)/shard_map/ppermute | solution.py:45
  216.3 14.1 %collective-permute-done.23.refs_6_ = bf16[24,4096]{1,0:T(8,128)(2,1)S(1)} collective-permute-done((bf16[24,4096]{1,0:T(8,128)(2,1)S(1)}, bf16[24,4096]{1,0:T(8,128)(2,1)S(1)}, u32[]{:S(2)}, u32[]{:S(2)}) %collective-permute-start.23) | collective-permute-done | bytes 196640 | tf_op jit(solution)/shard_map/ppermute | solution.py:45
  230.6 5.4 %collective-permute-start.26 = (bf16[24,4096]{1,0:T(8,128)(2,1)S(1)}, bf16[24,4096]{1,0:T(8,128)(2,1)S(1)}, u32[]{:S(2)}, u32[]{:S(2)}) collective-permute-start(bf16[24,4096]{1,0:T(8,128)(2,1)S(1)} %get-tuple-element.135), channel_id=1, source_target_pairs={{0,8},{2,10},{4,12},{6,14},{8,0},{10,2},{12,4},{14,6},{16,24},{18,... | collective-permute-start | bytes 589832 | tf_op jit(solution)/shard_map/ppermute | solution.py:45
  236.0 2.7 %collective-permute-start.28 = (bf16[24,4096]{1,0:T(8,128)(2,1)S(1)}, bf16[24,4096]{1,0:T(8,128)(2,1)S(1)}, u32[]{:S(2)}, u32[]{:S(2)}) collective-permute-start(bf16[24,4096]{1,0:T(8,128)(2,1)S(1)} %get-tuple-element.137), channel_id=1, source_target_pairs={{0,2},{2,4},{4,6},{6,8},{8,10},{10,12},{12,14},{14,0},{16,18},{18,... | collective-permute-start | bytes 589832 | tf_op jit(solution)/shard_map/ppermute | solution.py:45
  238.7 2.1 collective-permute-start.25
  240.9 3.7 %add_convert_fusion.refs_9_ = bf16[768,2048]{1,0:T(8,128)(2,1)S(1)} fusion(f32[768,2048]{1,0:T(8,128)S(1)} %shard_map.96, f32[768,2048]{1,0:T(8,128)} %collective-permute-done.29), kind=kLoop, calls=%fused_computation | loop fusion | flops 3145728 | bytes 15728640 | tf_op jit(solution)/shard_map/convert_element_type | solution.py:485
  244.6 3.6 %collective-permute-done.27.refs_2_ = bf16[24,4096]{1,0:T(8,128)(2,1)S(1)} collective-permute-done((bf16[24,4096]{1,0:T(8,128)(2,1)S(1)}, bf16[24,4096]{1,0:T(8,128)(2,1)S(1)}, u32[]{:S(2)}, u32[]{:S(2)}) %collective-permute-start.27) | collective-permute-done | bytes 196640 | tf_op jit(solution)/shard_map/ppermute | solution.py:45
  248.2 2.0 collective-permute-done.28.refs_3_
  250.2 6.0 %collective-permute-done.25.refs_8_ = bf16[128,2048]{1,0:T(8,128)(2,1)S(1)} collective-permute-done((bf16[128,2048]{1,0:T(8,128)(2,1)S(1)}, bf16[128,2048]{1,0:T(8,128)(2,1)S(1)}, u32[]{:S(2)}, u32[]{:S(2)}) %collective-permute-start.25) | collective-permute-done | bytes 524320 | tf_op jit(solution)/shard_map/ppermute | solution.py:24
  257.0 8.2 %collective-permute-done.30 = bf16[128,1024]{1,0:T(8,128)(2,1)S(1)} collective-permute-done((bf16[128,1024]{1,0:T(8,128)(2,1)S(1)}, bf16[128,1024]{1,0:T(8,128)(2,1)S(1)}, u32[]{:S(2)}, u32[]{:S(2)}) %collective-permute-start.30) | collective-permute-done | bytes 262176 | tf_op jit(solution)/shard_map/ppermute | solution.py:24
  265.2 1.1 maximum_bitcast_fusion
  (74 shorter events, 3.2 us)
Async XLA Ops:
  0.6 0.7 copy-start.5
  1.3 0.7 copy-start.7
  6.6 11.8 %copy-start.15 = (s32[16]{0:T(128)S(1)}, s32[16]{0:T(128)}, u32[]{:S(2)}) copy-start(s32[16]{0:T(128)} %constant.69.clone) | copy-start | bytes 196
  6.6 11.8 %copy-start.6 = (s32[1,2,128,8]{2,3,1,0:T(8,128)S(1)}, s32[1,2,128,8]{2,3,1,0:T(8,128)}, u32[]{:S(2)}) copy-start(s32[1,2,128,8]{2,3,1,0:T(8,128)} %param.9) | copy-start | bytes 24580
  6.6 12.2 %copy-start.8 = (bf16[1,2,128,8]{2,3,1,0:T(8,128)(2,1)S(1)}, bf16[1,2,128,8]{2,3,1,0:T(8,128)(2,1)}, u32[]{:S(2)}) copy-start(bf16[1,2,128,8]{2,3,1,0:T(8,128)(2,1)} %param.10) | copy-start | bytes 12292
  6.6 12.7 %copy-start = (bf16[1,2,128,2048]{3,2,1,0:T(8,128)(2,1)S(1)}, bf16[1,2,128,2048]{3,2,1,0:T(8,128)(2,1)}, u32[]{:S(2)}) copy-start(bf16[1,2,128,2048]{3,2,1,0:T(8,128)(2,1)} %inputs_ref.9) | copy-start | bytes 3145732
  6.6 12.7 %copy-start.1 = (bf16[1,2,128,2048]{3,2,1,0:T(8,128)(2,1)S(1)}, bf16[1,2,128,2048]{3,2,1,0:T(8,128)(2,1)}, u32[]{:S(2)}) copy-start(bf16[1,2,128,2048]{3,2,1,0:T(8,128)(2,1)} %upstream_ref.9) | copy-start | bytes 3145732
  6.6 92.8 %all-to-all-start = ((bf16[16,24,4096]{2,1,0:T(8,128)(2,1)}), bf16[16,24,4096]{2,1,0:T(8,128)(2,1)}, u32[]{:S(2)}, u32[]{:S(2)}) async-start(bf16[16,24,4096]{2,1,0:T(8,128)(2,1)} %shard_map.86), calls=%async_computation | async-start | bytes 6291456 | tf_op jit(solution)/shard_map/all_to_all | solution.py:412
  20.7 37.6 %collective-permute-start.2 = (bf16[24,16384]{1,0:T(8,128)(2,1)}, bf16[24,16384]{1,0:T(8,128)(2,1)}, u32[]{:S(2)}, u32[]{:S(2)}) collective-permute-start(bf16[24,16384]{1,0:T(8,128)(2,1)} %shard_map.92), channel_id=1, source_target_pairs={{0,16},{2,18},{4,20},{6,22},{8,24},{10,26},{12,28},{14,30},{16,0},... | collective-permute-start | bytes 2359304 | tf_op jit(solution)/shard_map/ppermute | solution.py:24
  22.2 63.4 %collective-permute-start.1 = (bf16[24,16384]{1,0:T(8,128)(2,1)}, bf16[24,16384]{1,0:T(8,128)(2,1)S(1)}, u32[]{:S(2)}, u32[]{:S(2)}) collective-permute-start(bf16[24,16384]{1,0:T(8,128)(2,1)} %shard_map.89), channel_id=1, source_target_pairs={{0,16},{2,18},{4,20},{6,22},{8,24},{10,26},{12,28},{14,30},{16,0},... | collective-permute-start | bytes 2359304 | tf_op jit(solution)/shard_map/ppermute | solution.py:24
  58.3 1.1 copy-start.3
  61.9 0.8 copy-start.13
  62.7 46.6 %collective-permute-start.3 = (bf16[24,8192]{1,0:T(8,128)(2,1)}, bf16[24,8192]{1,0:T(8,128)(2,1)}, u32[]{:S(2)}, u32[]{:S(2)}) collective-permute-start(bf16[24,8192]{1,0:T(8,128)(2,1)} %get-tuple-element.79), channel_id=1, source_target_pairs={{0,8},{2,10},{4,12},{6,14},{8,0},{10,2},{12,4},{14,6},{16,24},{18,... | collective-permute-start | bytes 1179656 | tf_op jit(solution)/shard_map/ppermute | solution.py:45
  63.2 51.0 %collective-permute-start.4 = (bf16[24,8192]{1,0:T(8,128)(2,1)}, bf16[24,8192]{1,0:T(8,128)(2,1)}, u32[]{:S(2)}, u32[]{:S(2)}) collective-permute-start(bf16[24,8192]{1,0:T(8,128)(2,1)} %get-tuple-element.80), channel_id=1, source_target_pairs={{0,2},{2,4},{4,6},{6,8},{8,10},{10,12},{12,14},{14,0},{16,18},{18,... | collective-permute-start | bytes 1179656 | tf_op jit(solution)/shard_map/ppermute | solution.py:45
  64.0 50.2 %collective-permute-start.5 = (bf16[24,8192]{1,0:T(8,128)(2,1)}, bf16[24,8192]{1,0:T(8,128)(2,1)}, u32[]{:S(2)}, u32[]{:S(2)}) collective-permute-start(bf16[24,8192]{1,0:T(8,128)(2,1)} %get-tuple-element.81), channel_id=1, source_target_pairs={{0,14},{2,0},{4,2},{6,4},{8,6},{10,8},{12,10},{14,12},{16,30},{18,... | collective-permute-start | bytes 1179656 | tf_op jit(solution)/shard_map/ppermute | solution.py:45
  66.6 42.6 %collective-permute-start = (bf16[384,128]{1,0:T(8,128)(2,1)S(1)}, bf16[384,128]{1,0:T(8,128)(2,1)S(1)}, u32[]{:S(2)}, u32[]{:S(2)}) collective-permute-start(bf16[384,128]{1,0:T(8,128)(2,1)S(1)} %get-tuple-element.133.placing_ref), channel_id=1, source_target_pairs={{0,224},{32,0},{64,32},{96,64},{128,96},{160,128},{192,160},{224,1... | collective-permute-start | bytes 294920 | tf_op jit(solution)/shard_map/ppermute | solution.py:24
  85.5 1.1 copy-start.4
  99.5 1.9 copy-start.9
  101.4 1.9 copy-start.11
  103.2 61.3 %copy-start.10 = (bf16[1,1,2048,768]{3,2,1,0:T(8,128)(2,1)S(1)}, bf16[1,1,2048,768]{3,2,1,0:T(8,128)(2,1)}, u32[]{:S(2)}) copy-start(bf16[1,1,2048,768]{3,2,1,0:T(8,128)(2,1)} %param.11) | copy-start | bytes 9437188
  103.3 61.3 %copy-start.14 = (bf16[24,8192]{1,0:T(8,128)(2,1)S(1)}, bf16[24,8192]{1,0:T(8,128)(2,1)}, u32[]{:S(2)}) copy-start(bf16[24,8192]{1,0:T(8,128)(2,1)} %copy-done.13) | copy-start | bytes 1179652
  114.1 20.0 %collective-permute-start.6 = (bf16[24,16384]{1,0:T(8,128)(2,1)S(1)}, bf16[24,16384]{1,0:T(8,128)(2,1)S(1)}, u32[]{:S(2)}, u32[]{:S(2)}) collective-permute-start(bf16[24,16384]{1,0:T(8,128)(2,1)S(1)} %get-tuple-element.84), channel_id=1, source_target_pairs={{0,16},{2,18},{4,20},{6,22},{8,24},{10,26},{12,28},{14,30},{16,0},... | collective-permute-start | bytes 2359304 | tf_op jit(solution)/shard_map/ppermute | solution.py:24
  114.7 29.3 %collective-permute-start.7 = (bf16[24,8192]{1,0:T(8,128)(2,1)S(1)}, bf16[24,8192]{1,0:T(8,128)(2,1)S(1)}, u32[]{:S(2)}, u32[]{:S(2)}) collective-permute-start(bf16[24,8192]{1,0:T(8,128)(2,1)S(1)} %get-tuple-element.91), channel_id=1, source_target_pairs={{0,4},{2,6},{4,8},{6,10},{8,12},{10,14},{12,0},{14,2},{16,20},{18,... | collective-permute-start | bytes 1179656 | tf_op jit(solution)/shard_map/ppermute | solution.py:45
  118.1 25.9 %collective-permute-start.8 = (bf16[24,8192]{1,0:T(8,128)(2,1)S(1)}, bf16[24,8192]{1,0:T(8,128)(2,1)S(1)}, u32[]{:S(2)}, u32[]{:S(2)}) collective-permute-start(bf16[24,8192]{1,0:T(8,128)(2,1)S(1)} %get-tuple-element.92), channel_id=1, source_target_pairs={{0,12},{2,14},{4,0},{6,2},{8,4},{10,6},{12,8},{14,10},{16,28},{18,... | collective-permute-start | bytes 1179656 | tf_op jit(solution)/shard_map/ppermute | solution.py:45
  120.9 39.8 %collective-permute-start.9 = (bf16[24,8192]{1,0:T(8,128)(2,1)S(1)}, bf16[24,8192]{1,0:T(8,128)(2,1)S(1)}, u32[]{:S(2)}, u32[]{:S(2)}) collective-permute-start(bf16[24,8192]{1,0:T(8,128)(2,1)S(1)} %get-tuple-element.93), channel_id=1, source_target_pairs={{0,6},{2,8},{4,10},{6,12},{8,14},{10,0},{12,2},{14,4},{16,22},{18,... | collective-permute-start | bytes 1179656 | tf_op jit(solution)/shard_map/ppermute | solution.py:45
  124.4 40.2 %collective-permute-start.10 = (bf16[24,8192]{1,0:T(8,128)(2,1)S(1)}, bf16[24,8192]{1,0:T(8,128)(2,1)S(1)}, u32[]{:S(2)}, u32[]{:S(2)}) collective-permute-start(bf16[24,8192]{1,0:T(8,128)(2,1)S(1)} %get-tuple-element.94), channel_id=1, source_target_pairs={{0,10},{2,12},{4,14},{6,0},{8,2},{10,4},{12,6},{14,8},{16,26},{18,... | collective-permute-start | bytes 1179656 | tf_op jit(solution)/shard_map/ppermute | solution.py:45
  137.1 35.2 %collective-permute-start.11 = (bf16[24,4096]{1,0:T(8,128)(2,1)S(1)}, bf16[24,4096]{1,0:T(8,128)(2,1)S(1)}, u32[]{:S(2)}, u32[]{:S(2)}) collective-permute-start(bf16[24,4096]{1,0:T(8,128)(2,1)S(1)} %get-tuple-element.105), channel_id=1, source_target_pairs={{0,14},{2,0},{4,2},{6,4},{8,6},{10,8},{12,10},{14,12},{16,30},{18,... | collective-permute-start | bytes 589832 | tf_op jit(solution)/shard_map/ppermute | solution.py:45
  144.0 28.2 %collective-permute-start.12 = (bf16[24,4096]{1,0:T(8,128)(2,1)S(1)}, bf16[24,4096]{1,0:T(8,128)(2,1)S(1)}, u32[]{:S(2)}, u32[]{:S(2)}) collective-permute-start(bf16[24,4096]{1,0:T(8,128)(2,1)S(1)} %get-tuple-element.106), channel_id=1, source_target_pairs={{0,2},{2,4},{4,6},{6,8},{8,10},{10,12},{12,14},{14,0},{16,18},{18,... | collective-permute-start | bytes 589832 | tf_op jit(solution)/shard_map/ppermute | solution.py:45
  144.0 28.2 %collective-permute-start.13 = (bf16[24,4096]{1,0:T(8,128)(2,1)S(1)}, bf16[24,4096]{1,0:T(8,128)(2,1)S(1)}, u32[]{:S(2)}, u32[]{:S(2)}) collective-permute-start(bf16[24,4096]{1,0:T(8,128)(2,1)S(1)} %get-tuple-element.107), channel_id=1, source_target_pairs={{0,12},{2,14},{4,0},{6,2},{8,4},{10,6},{12,8},{14,10},{16,28},{18,... | collective-permute-start | bytes 589832 | tf_op jit(solution)/shard_map/ppermute | solution.py:45
  160.7 11.5 %collective-permute-start.14 = (bf16[24,4096]{1,0:T(8,128)(2,1)S(1)}, bf16[24,4096]{1,0:T(8,128)(2,1)S(1)}, u32[]{:S(2)}, u32[]{:S(2)}) collective-permute-start(bf16[24,4096]{1,0:T(8,128)(2,1)S(1)} %get-tuple-element.108), channel_id=1, source_target_pairs={{0,4},{2,6},{4,8},{6,10},{8,12},{10,14},{12,0},{14,2},{16,20},{18,... | collective-permute-start | bytes 589832 | tf_op jit(solution)/shard_map/ppermute | solution.py:45
  164.6 1.9 copy-start.12
  172.3 17.0 %collective-permute-start.18 = (bf16[24,4096]{1,0:T(8,128)(2,1)S(1)}, bf16[24,4096]{1,0:T(8,128)(2,1)S(1)}, u32[]{:S(2)}, u32[]{:S(2)}) collective-permute-start(bf16[24,4096]{1,0:T(8,128)(2,1)S(1)} %get-tuple-element.113), channel_id=1, source_target_pairs={{0,8},{2,10},{4,12},{6,14},{8,0},{10,2},{12,4},{14,6},{16,24},{18,... | collective-permute-start | bytes 589832 | tf_op jit(solution)/shard_map/ppermute | solution.py:45
  179.0 24.2 %collective-permute-start.15 = (bf16[24,8192]{1,0:T(8,128)(2,1)S(1)}, bf16[24,8192]{1,0:T(8,128)(2,1)S(1)}, u32[]{:S(2)}, u32[]{:S(2)}) collective-permute-start(bf16[24,8192]{1,0:T(8,128)(2,1)S(1)} %get-tuple-element.110), channel_id=1, source_target_pairs={{0,16},{2,18},{4,20},{6,22},{8,24},{10,26},{12,28},{14,30},{16,0},... | collective-permute-start | bytes 1179656 | tf_op jit(solution)/shard_map/ppermute | solution.py:24
  182.0 22.3 %collective-permute-start.16 = (bf16[24,8192]{1,0:T(8,128)(2,1)S(1)}, bf16[24,8192]{1,0:T(8,128)(2,1)S(1)}, u32[]{:S(2)}, u32[]{:S(2)}) collective-permute-start(bf16[24,8192]{1,0:T(8,128)(2,1)S(1)} %get-tuple-element.111), channel_id=1, source_target_pairs={{0,224},{32,0},{64,32},{96,64},{128,96},{160,128},{192,160},{224,1... | collective-permute-start | bytes 1179656 | tf_op jit(solution)/shard_map/ppermute | solution.py:24
  182.8 21.5 %collective-permute-start.17 = (bf16[24,8192]{1,0:T(8,128)(2,1)S(1)}, bf16[24,8192]{1,0:T(8,128)(2,1)S(1)}, u32[]{:S(2)}, u32[]{:S(2)}) collective-permute-start(bf16[24,8192]{1,0:T(8,128)(2,1)S(1)} %get-tuple-element.112), channel_id=1, source_target_pairs={{0,240},{2,242},{4,244},{6,246},{8,248},{10,250},{12,252},{14,254}... | collective-permute-start | bytes 1179656 | tf_op jit(solution)/shard_map/ppermute | solution.py:38
  183.0 18.7 %collective-permute-start.19 = (bf16[24,4096]{1,0:T(8,128)(2,1)S(1)}, bf16[24,4096]{1,0:T(8,128)(2,1)S(1)}, u32[]{:S(2)}, u32[]{:S(2)}) collective-permute-start(bf16[24,4096]{1,0:T(8,128)(2,1)S(1)} %get-tuple-element.114), channel_id=1, source_target_pairs={{0,10},{2,12},{4,14},{6,0},{8,2},{10,4},{12,6},{14,8},{16,26},{18,... | collective-permute-start | bytes 589832 | tf_op jit(solution)/shard_map/ppermute | solution.py:45
  189.3 13.9 %collective-permute-start.20 = (bf16[24,4096]{1,0:T(8,128)(2,1)S(1)}, bf16[24,4096]{1,0:T(8,128)(2,1)S(1)}, u32[]{:S(2)}, u32[]{:S(2)}) collective-permute-start(bf16[24,4096]{1,0:T(8,128)(2,1)S(1)} %get-tuple-element.115), channel_id=1, source_target_pairs={{0,6},{2,8},{4,10},{6,12},{8,14},{10,0},{12,2},{14,4},{16,22},{18,... | collective-permute-start | bytes 589832 | tf_op jit(solution)/shard_map/ppermute | solution.py:45
  207.4 8.9 %collective-permute-start.21 = (bf16[24,4096]{1,0:T(8,128)(2,1)S(1)}, bf16[24,4096]{1,0:T(8,128)(2,1)S(1)}, u32[]{:S(2)}, u32[]{:S(2)}) collective-permute-start(bf16[24,4096]{1,0:T(8,128)(2,1)S(1)} %get-tuple-element.128), channel_id=1, source_target_pairs={{0,12},{2,14},{4,0},{6,2},{8,4},{10,6},{12,8},{14,10},{16,28},{18,... | collective-permute-start | bytes 589832 | tf_op jit(solution)/shard_map/ppermute | solution.py:45
  208.5 7.9 %collective-permute-start.22 = (bf16[24,4096]{1,0:T(8,128)(2,1)S(1)}, bf16[24,4096]{1,0:T(8,128)(2,1)S(1)}, u32[]{:S(2)}, u32[]{:S(2)}) collective-permute-start(bf16[24,4096]{1,0:T(8,128)(2,1)S(1)} %get-tuple-element.129), channel_id=1, source_target_pairs={{0,4},{2,6},{4,8},{6,10},{8,12},{10,14},{12,0},{14,2},{16,20},{18,... | collective-permute-start | bytes 589832 | tf_op jit(solution)/shard_map/ppermute | solution.py:45
  210.4 20.0 %collective-permute-start.23 = (bf16[24,4096]{1,0:T(8,128)(2,1)S(1)}, bf16[24,4096]{1,0:T(8,128)(2,1)S(1)}, u32[]{:S(2)}, u32[]{:S(2)}) collective-permute-start(bf16[24,4096]{1,0:T(8,128)(2,1)S(1)} %get-tuple-element.130), channel_id=1, source_target_pairs={{0,10},{2,12},{4,14},{6,0},{8,2},{10,4},{12,6},{14,8},{16,26},{18,... | collective-permute-start | bytes 589832 | tf_op jit(solution)/shard_map/ppermute | solution.py:45
  215.8 14.7 %collective-permute-start.24 = (bf16[24,4096]{1,0:T(8,128)(2,1)S(1)}, bf16[24,4096]{1,0:T(8,128)(2,1)S(1)}, u32[]{:S(2)}, u32[]{:S(2)}) collective-permute-start(bf16[24,4096]{1,0:T(8,128)(2,1)S(1)} %get-tuple-element.131), channel_id=1, source_target_pairs={{0,6},{2,8},{4,10},{6,12},{8,14},{10,0},{12,2},{14,4},{16,22},{18,... | collective-permute-start | bytes 589832 | tf_op jit(solution)/shard_map/ppermute | solution.py:45
  230.6 10.3 %collective-permute-start.29 = (f32[768,2048]{1,0:T(8,128)S(1)}, f32[768,2048]{1,0:T(8,128)}, u32[]{:S(2)}, u32[]{:S(2)}) collective-permute-start(f32[768,2048]{1,0:T(8,128)S(1)} %shard_map.96), channel_id=1, source_target_pairs={{0,1},{1,0},{2,3},{3,2},{4,5},{5,4},{6,7},{7,6},{8,9},{9,8},{10,11... | collective-permute-start | bytes 18874376 | tf_op jit(solution)/shard_map/ppermute | solution.py:24
  230.6 14.0 %collective-permute-start.26 = (bf16[24,4096]{1,0:T(8,128)(2,1)S(1)}, bf16[24,4096]{1,0:T(8,128)(2,1)S(1)}, u32[]{:S(2)}, u32[]{:S(2)}) collective-permute-start(bf16[24,4096]{1,0:T(8,128)(2,1)S(1)} %get-tuple-element.135), channel_id=1, source_target_pairs={{0,8},{2,10},{4,12},{6,14},{8,0},{10,2},{12,4},{14,6},{16,24},{18,... | collective-permute-start | bytes 589832 | tf_op jit(solution)/shard_map/ppermute | solution.py:45
  236.0 12.2 %collective-permute-start.27 = (bf16[24,4096]{1,0:T(8,128)(2,1)S(1)}, bf16[24,4096]{1,0:T(8,128)(2,1)S(1)}, u32[]{:S(2)}, u32[]{:S(2)}) collective-permute-start(bf16[24,4096]{1,0:T(8,128)(2,1)S(1)} %get-tuple-element.136), channel_id=1, source_target_pairs={{0,14},{2,0},{4,2},{6,4},{8,6},{10,8},{12,10},{14,12},{16,30},{18,... | collective-permute-start | bytes 589832 | tf_op jit(solution)/shard_map/ppermute | solution.py:45
  236.0 14.2 %collective-permute-start.28 = (bf16[24,4096]{1,0:T(8,128)(2,1)S(1)}, bf16[24,4096]{1,0:T(8,128)(2,1)S(1)}, u32[]{:S(2)}, u32[]{:S(2)}) collective-permute-start(bf16[24,4096]{1,0:T(8,128)(2,1)S(1)} %get-tuple-element.137), channel_id=1, source_target_pairs={{0,2},{2,4},{4,6},{6,8},{8,10},{10,12},{12,14},{14,0},{16,18},{18,... | collective-permute-start | bytes 589832 | tf_op jit(solution)/shard_map/ppermute | solution.py:45
  238.7 17.5 %collective-permute-start.25 = (bf16[128,2048]{1,0:T(8,128)(2,1)S(1)}, bf16[128,2048]{1,0:T(8,128)(2,1)S(1)}, u32[]{:S(2)}, u32[]{:S(2)}) collective-permute-start(bf16[128,2048]{1,0:T(8,128)(2,1)S(1)} %shard_map.97), channel_id=1, source_target_pairs={{0,224},{32,0},{64,32},{96,64},{128,96},{160,128},{192,160},{224,1... | collective-permute-start | bytes 1572872 | tf_op jit(solution)/shard_map/ppermute | solution.py:24
  244.6 12.4 %copy-start.2 = (bf16[768,2048]{1,0:T(8,128)(2,1)}, bf16[768,2048]{1,0:T(8,128)(2,1)S(1)}, u32[]{:S(2)}) copy-start(bf16[768,2048]{1,0:T(8,128)(2,1)S(1)} %add_convert_fusion.refs_9_) | copy-start | bytes 9437188
  256.5 8.6 %collective-permute-start.30 = (bf16[128,1024]{1,0:T(8,128)(2,1)S(1)}, bf16[128,1024]{1,0:T(8,128)(2,1)S(1)}, u32[]{:S(2)}, u32[]{:S(2)}) collective-permute-start(bf16[128,1024]{1,0:T(8,128)(2,1)S(1)} %shard_map.99.refs_8_), channel_id=1, source_target_pairs={{0,224},{32,0},{64,32},{96,64},{128,96},{160,128},{192,160},{224,1... | collective-permute-start | bytes 786440 | tf_op jit(solution)/shard_map/ppermute | solution.py:24
